TPU v7x, 32 devices: a whole 2x2x4 slice. The times are simulated.
32 devices in a mesh: context: 4 (over y, x), expert: 8 (over z, core).
Axes of the slice: x: 2, y: 2, z: 4, core: 2. Of those that a mesh axis runs over, the one named last changes fastest.
Arguments:
- tokens_in: bfloat16 [8, 1024, 2048], P('expert', 'context'), may hold values from -6 to 6
- positions: int32 [8, 1024], P('expert'), may hold values from 0 to 1023, as said below
- routes: int32 [8, 1024, 8], P('expert', 'context'), may hold values from 0 to 15, all different within a row; in each aligned block of 256 rows (0 to 255, 256 to 511, ..., all dimensions but the last counted through in order) at most 256 rows name the same one
- cotangent: bfloat16 [8, 1024, 2048], P('expert', 'context'), may hold values from -6 to 6
- w_query: bfloat16 [2048, 2048], P(('context', 'expert')), may hold values from -0.125 to 0.125
- w_key: bfloat16 [2048, 2048], P(('context', 'expert')), may hold values from -0.125 to 0.125
- w_value: bfloat16 [2048, 2048], P(('context', 'expert')), may hold values from -0.125 to 0.125
- w_output: bfloat16 [2048, 2048], P(('context', 'expert')), may hold values from -1 to 1
- router: bfloat16 [2048, 16], P(('context', 'expert')), may hold values from -0.0625 to 0.0625
- attn_gain: bfloat16 [2048], P(('context', 'expert')), may hold values from 0.099609375 to 1.8984375
- query_gain: bfloat16 [2048], P(('context', 'expert')), may hold values from 0.099609375 to 1.8984375
- key_gain: bfloat16 [2048], P(('context', 'expert')), may hold values from 0.099609375 to 1.8984375
- moe_gain: bfloat16 [2048], P(('context', 'expert')), may hold values from 0.099609375 to 1.8984375
- expert_gate: bfloat16 [16, 2048, 1024], P('expert', 'context'), may hold values from -0.125 to 0.125
- expert_up: bfloat16 [16, 2048, 1024], P('expert', 'context'), may hold values from -0.125 to 0.125
- expert_down: bfloat16 [16, 1024, 2048], P('expert', 'context'), may hold values from -3 to 3
Outputs:
- output: bfloat16 [8, 1024, 2048], P('expert', 'context')
- input_grad: float32 [8, 1024, 2048], P('expert', 'context')
- grad_w_query: float32 [2048, 2048], P(('context', 'expert'))
- grad_w_key: float32 [2048, 2048], P(('context', 'expert'))
- grad_w_value: float32 [2048, 2048], P(('context', 'expert'))
- grad_w_output: float32 [2048, 2048], P(('context', 'expert'))
- grad_router: float32 [2048, 16], P(('context', 'expert'))
- grad_attn_gain: float32 [2048], P(('context', 'expert'))
- grad_query_gain: float32 [2048], P(('context', 'expert'))
- grad_key_gain: float32 [2048], P(('context', 'expert'))
- grad_moe_gain: float32 [2048], P(('context', 'expert'))
- grad_expert_gate: float32 [16, 2048, 1024], P('expert', 'context')
- grad_expert_up: float32 [16, 2048, 1024], P('expert', 'context')
- grad_expert_down: float32 [16, 1024, 2048], P('expert', 'context')
Inputs may be any that keep to these rules, and one draw needn't show every extreme that they name: `routes`: each row names 8 different experts; in the rows of one device no expert is named more than 256 times. Within each sequence a permutation of its positions; each device's 256 rows are a run of 128 consecutive positions followed by the run at the mirror place from the sequence's end.
All inputs are finite; a program needn't handle non-finite values.
Results may differ from a plain program's by a relative error of at most 0.02.
Values may be sent and summed in bfloat16 or wider, within the bound.
No kernel may reach another device: no remote copies, remote signals or barrier semaphores. Data moves between devices by JAX's collectives and lax.ppermute only.
A program may use at most 512 MiB of HBM per device.

v0:
```python
import math

import jax
import jax.numpy as jnp
from jax import lax
from jax.sharding import PartitionSpec as P

HEADS = 16
HEAD_DIM = 128
TOPK = 8
EXP_DEV = 2


epsilon = 1e-05
rope_base = 10000.0
masked_value = -1e30


def rms_apply(values, gain_vector):
    return (
        values
        * lax.rsqrt(jnp.mean(values * values, axis=-1, keepdims=True) + epsilon)
        * gain_vector
    )


def rotate(values, places):
    row_count = values.shape[0]
    half_dim = HEAD_DIM // 2
    frequency = jnp.exp(
        jnp.arange(half_dim, dtype=jnp.float32) * (-2.0 * math.log(rope_base) / HEAD_DIM)
    )
    angles = places.astype(jnp.float32)[:, None] * frequency[None, :]
    cosine = jnp.cos(angles)[:, None, :]
    sine_part = jnp.sin(angles)[:, None, :]
    head_view = values.reshape(row_count, HEADS, HEAD_DIM)
    first_half = head_view[:, :, :half_dim]
    second_half = head_view[:, :, half_dim:]
    turned = jnp.concatenate(
        [
            first_half * cosine - second_half * sine_part,
            second_half * cosine + first_half * sine_part,
        ],
        axis=-1,
    )
    return turned.reshape(row_count, HEADS * HEAD_DIM)


def shards(
    tokens_in,
    positions,
    routes,
    cotangent,
    w_query,
    w_key,
    w_value,
    w_output,
    router,
    attn_gain,
    query_gain,
    key_gain,
    moe_gain,
    expert_gate,
    expert_up,
    expert_down,
):
    inputs = tokens_in[0].astype(jnp.float32)
    token_count = inputs.shape[0]
    model_width = inputs.shape[1]
    sequence_len = positions.shape[1]
    expert_devices = lax.axis_size("expert")
    expert_total = EXP_DEV * expert_devices
    capacity = token_count * TOPK * 2 // expert_total
    slot_total = EXP_DEV * expert_devices * capacity
    row_start = lax.axis_index("context") * token_count
    key_places = positions[0]
    own_places = lax.dynamic_slice_in_dim(key_places, row_start, token_count)
    gathered = (
        lax.all_gather(w_query, ("context", "expert"), axis=0, tiled=True),
        lax.all_gather(w_key, ("context", "expert"), axis=0, tiled=True),
        lax.all_gather(w_value, ("context", "expert"), axis=0, tiled=True),
        lax.all_gather(w_output, ("context", "expert"), axis=0, tiled=True),
        lax.all_gather(router, ("context", "expert"), axis=0, tiled=True),
        lax.all_gather(attn_gain, ("context", "expert"), axis=0, tiled=True),
        lax.all_gather(query_gain, ("context", "expert"), axis=0, tiled=True),
        lax.all_gather(key_gain, ("context", "expert"), axis=0, tiled=True),
        lax.all_gather(moe_gain, ("context", "expert"), axis=0, tiled=True),
    )
    query_full, key_full, value_full, output_full, router_full = (
        gathered[0],
        gathered[1],
        gathered[2],
        gathered[3],
        gathered[4],
    )
    attn_scale = gathered[5].astype(jnp.float32)
    query_scale = gathered[6].astype(jnp.float32)
    key_scale = gathered[7].astype(jnp.float32)
    moe_scale = gathered[8].astype(jnp.float32)
    gate_full, up_full, down_full = (
        lax.all_gather(expert_gate, "context", axis=1, tiled=True),
        lax.all_gather(expert_up, "context", axis=1, tiled=True),
        lax.all_gather(expert_down, "context", axis=1, tiled=True),
    )
    normed = rms_apply(inputs, attn_scale).astype(jnp.bfloat16)
    query_proj = jnp.dot(normed, query_full, preferred_element_type=jnp.float32)
    key_proj = jnp.dot(normed, key_full, preferred_element_type=jnp.float32)
    value_proj = jnp.dot(normed, value_full, preferred_element_type=jnp.float32)
    query_rot = rotate(rms_apply(query_proj, query_scale), own_places).astype(jnp.bfloat16)
    key_rot = rotate(rms_apply(key_proj, key_scale), own_places).astype(jnp.bfloat16)
    value_low = value_proj.astype(jnp.bfloat16)
    key_all, value_all = (
        lax.all_gather(key_rot, "context", axis=0, tiled=True),
        lax.all_gather(value_low, "context", axis=0, tiled=True),
    )
    score_scale = HEAD_DIM ** (-0.5)
    query_heads = query_rot.reshape(token_count, HEADS, HEAD_DIM)
    key_heads = key_all.reshape(sequence_len, HEADS, HEAD_DIM)
    value_heads = value_all.reshape(sequence_len, HEADS, HEAD_DIM)
    allowed = (key_places[None, :] <= own_places[:, None])[None]
    scores = jnp.where(
        allowed,
        jnp.einsum("qhd,khd->hqk", query_heads, key_heads, preferred_element_type=jnp.float32)
        * score_scale,
        masked_value,
    )
    row_peak = jnp.max(scores, axis=-1, keepdims=True)
    exponent = jnp.exp(scores - row_peak)
    row_total = jnp.sum(exponent, axis=-1, keepdims=True)
    log_total = row_peak + jnp.log(row_total)
    weights_low = (exponent / row_total).astype(jnp.bfloat16)
    attended = jnp.einsum(
        "hqk,khd->qhd", weights_low, value_heads, preferred_element_type=jnp.float32
    ).reshape(token_count, model_width)
    attended_low = attended.astype(jnp.bfloat16)
    middle = inputs + jnp.dot(attended_low, output_full, preferred_element_type=jnp.float32)
    mixed_rows = rms_apply(middle, moe_scale).astype(jnp.bfloat16)
    logits = jnp.dot(mixed_rows, router_full, preferred_element_type=jnp.float32)
    router_probs = jax.nn.softmax(logits, axis=-1)
    route_rows = routes[0]
    chosen = route_rows[:, :, None] == jnp.arange(expert_total, dtype=jnp.int32)[None, None, :]
    chosen_float = chosen.astype(jnp.float32)
    gate_values = jnp.sum(router_probs[:, None, :] * chosen_float, axis=-1)
    chosen_int = chosen.reshape(token_count * TOPK, expert_total).astype(jnp.int32)
    rank_index = jnp.sum((jnp.cumsum(chosen_int, axis=0) - chosen_int) * chosen_int, axis=-1)
    flat_route = route_rows.reshape(-1)
    owner_index = flat_route // EXP_DEV
    local_index = flat_route % EXP_DEV
    slot_index = (local_index * expert_devices + owner_index) * capacity + rank_index
    send_rows = (
        jnp.zeros((slot_total, model_width), jnp.bfloat16)
        .at[slot_index]
        .set(jnp.repeat(mixed_rows, TOPK, axis=0))
    )
    arrived = lax.all_to_all(
        send_rows.reshape(EXP_DEV, expert_devices, capacity, model_width),
        "expert",
        split_axis=1,
        concat_axis=1,
        tiled=True,
    )
    expert_rows = arrived.reshape(EXP_DEV, expert_devices * capacity, model_width)
    gate_act = jnp.einsum(
        "erd,edf->erf", expert_rows, gate_full, preferred_element_type=jnp.float32
    )
    up_act = jnp.einsum("erd,edf->erf", expert_rows, up_full, preferred_element_type=jnp.float32)
    sigmoid_part = jax.nn.sigmoid(gate_act)
    silu_part = gate_act * sigmoid_part
    hidden = (silu_part * up_act).astype(jnp.bfloat16)
    expert_out = jnp.einsum(
        "erf,efd->erd", hidden, down_full, preferred_element_type=jnp.float32
    ).astype(jnp.bfloat16)
    returned = lax.all_to_all(
        expert_out.reshape(EXP_DEV, expert_devices, capacity, model_width),
        "expert",
        split_axis=1,
        concat_axis=1,
        tiled=True,
    )
    picked = (
        returned.reshape(slot_total, model_width)[slot_index]
        .reshape(token_count, TOPK, model_width)
        .astype(jnp.float32)
    )
    result = middle + jnp.sum(gate_values[:, :, None] * picked, axis=1)
    grad_out = cotangent[0].astype(jnp.float32)
    grad_picked = (gate_values[:, :, None] * grad_out[:, None, :]).astype(jnp.bfloat16)
    grad_gates = jnp.sum(picked * grad_out[:, None, :], axis=-1)
    grad_send = (
        jnp.zeros((slot_total, model_width), jnp.bfloat16)
        .at[slot_index]
        .set(grad_picked.reshape(token_count * TOPK, model_width))
    )
    grad_arrived = lax.all_to_all(
        grad_send.reshape(EXP_DEV, expert_devices, capacity, model_width),
        "expert",
        split_axis=1,
        concat_axis=1,
        tiled=True,
    )
    grad_arrived = grad_arrived.reshape(EXP_DEV, expert_devices * capacity, model_width)
    grad_hidden = jnp.einsum(
        "erd,efd->erf", grad_arrived, down_full, preferred_element_type=jnp.float32
    )
    grad_down = jnp.einsum("erf,erd->efd", hidden, grad_arrived, preferred_element_type=jnp.float32)
    grad_gate_act = (
        grad_hidden * up_act * sigmoid_part * (1.0 + gate_act * (1.0 - sigmoid_part))
    ).astype(jnp.bfloat16)
    grad_up_act = (grad_hidden * silu_part).astype(jnp.bfloat16)
    grad_gate_w = jnp.einsum(
        "erd,erf->edf", expert_rows, grad_gate_act, preferred_element_type=jnp.float32
    )
    grad_up_w = jnp.einsum(
        "erd,erf->edf", expert_rows, grad_up_act, preferred_element_type=jnp.float32
    )
    grad_rows = jnp.einsum(
        "erf,edf->erd", grad_gate_act, gate_full, preferred_element_type=jnp.float32
    )
    grad_rows = (
        grad_rows
        + jnp.einsum("erf,edf->erd", grad_up_act, up_full, preferred_element_type=jnp.float32)
    ).astype(jnp.bfloat16)
    expert_grads = (
        lax.psum_scatter(
            grad_gate_w.astype(jnp.bfloat16), "context", scatter_dimension=1, tiled=True
        ).astype(jnp.float32),
        lax.psum_scatter(
            grad_up_w.astype(jnp.bfloat16), "context", scatter_dimension=1, tiled=True
        ).astype(jnp.float32),
        lax.psum_scatter(
            grad_down.astype(jnp.bfloat16), "context", scatter_dimension=1, tiled=True
        ).astype(jnp.float32),
    )
    grad_back = lax.all_to_all(
        grad_rows.reshape(EXP_DEV, expert_devices, capacity, model_width),
        "expert",
        split_axis=1,
        concat_axis=1,
        tiled=True,
    )
    grad_mixed = jnp.sum(
        grad_back.reshape(slot_total, model_width)[slot_index]
        .reshape(token_count, TOPK, model_width)
        .astype(jnp.float32),
        axis=1,
    )
    grad_rprobs = jnp.sum(grad_gates[:, :, None] * chosen_float, axis=1)
    grad_logits = (
        router_probs * (grad_rprobs - jnp.sum(router_probs * grad_rprobs, axis=-1, keepdims=True))
    ).astype(jnp.bfloat16)
    grad_router = jnp.dot(mixed_rows.T, grad_logits, preferred_element_type=jnp.float32)
    grad_mixed = grad_mixed + jnp.dot(
        grad_logits, router_full.T, preferred_element_type=jnp.float32
    )
    moe_unused, moe_pull = jax.vjp(rms_apply, middle, moe_scale)
    grad_middle_norm, grad_moe_scale = moe_pull(grad_mixed)
    grad_middle = grad_out + grad_middle_norm
    grad_branch = grad_middle.astype(jnp.bfloat16)
    grad_output_w = jnp.dot(attended_low.T, grad_branch, preferred_element_type=jnp.float32)
    grad_attended = (
        jnp.dot(grad_branch, output_full.T, preferred_element_type=jnp.float32)
        .astype(jnp.bfloat16)
        .reshape(token_count, HEADS, HEAD_DIM)
    )
    scores_again = jnp.where(
        allowed,
        jnp.einsum("qhd,khd->hqk", query_heads, key_heads, preferred_element_type=jnp.float32)
        * score_scale,
        masked_value,
    )
    probs_again = jnp.exp(scores_again - log_total)
    grad_probs = jnp.einsum(
        "qhd,khd->hqk", grad_attended, value_heads, preferred_element_type=jnp.float32
    )
    grad_value_all = jnp.einsum(
        "hqk,qhd->khd",
        probs_again.astype(jnp.bfloat16),
        grad_attended,
        preferred_element_type=jnp.float32,
    )
    inner_sum = jnp.sum(probs_again * grad_probs, axis=-1, keepdims=True)
    grad_scores = (probs_again * (grad_probs - inner_sum)).astype(jnp.bfloat16)
    grad_query = (
        jnp.einsum(
            "hqk,khd->qhd", grad_scores, key_heads, preferred_element_type=jnp.float32
        ).reshape(token_count, model_width)
        * score_scale
    )
    grad_key_all = (
        jnp.einsum(
            "hqk,qhd->khd", grad_scores, query_heads, preferred_element_type=jnp.float32
        ).reshape(sequence_len, model_width)
        * score_scale
    )
    grad_key, grad_value = (
        lax.psum_scatter(
            grad_key_all.astype(jnp.bfloat16), "context", scatter_dimension=0, tiled=True
        ).astype(jnp.float32),
        lax.psum_scatter(
            grad_value_all.reshape(sequence_len, model_width).astype(jnp.bfloat16),
            "context",
            scatter_dimension=0,
            tiled=True,
        ).astype(jnp.float32),
    )
    query_unused, query_pull = jax.vjp(
        lambda projected, gain_vector: rotate(rms_apply(projected, gain_vector), own_places),
        query_proj,
        query_scale,
    )
    grad_query_proj, grad_query_scale = query_pull(grad_query)
    key_unused, key_pull = jax.vjp(
        lambda projected, gain_vector: rotate(rms_apply(projected, gain_vector), own_places),
        key_proj,
        key_scale,
    )
    grad_key_proj, grad_key_scale = key_pull(grad_key)
    grad_query_low = grad_query_proj.astype(jnp.bfloat16)
    grad_key_low = grad_key_proj.astype(jnp.bfloat16)
    grad_value_low = grad_value.astype(jnp.bfloat16)
    grad_query_w = jnp.dot(normed.T, grad_query_low, preferred_element_type=jnp.float32)
    grad_key_w = jnp.dot(normed.T, grad_key_low, preferred_element_type=jnp.float32)
    grad_value_w = jnp.dot(normed.T, grad_value_low, preferred_element_type=jnp.float32)
    grad_normed = jnp.dot(grad_query_low, query_full.T, preferred_element_type=jnp.float32)
    grad_normed = grad_normed + jnp.dot(
        grad_key_low, key_full.T, preferred_element_type=jnp.float32
    )
    grad_normed = grad_normed + jnp.dot(
        grad_value_low, value_full.T, preferred_element_type=jnp.float32
    )
    attn_unused, attn_pull = jax.vjp(rms_apply, inputs, attn_scale)
    grad_inputs_norm, grad_attn_scale = attn_pull(grad_normed)
    grad_inputs = grad_middle + grad_inputs_norm
    reduced = (
        lax.psum_scatter(grad_query_w, ("context", "expert"), scatter_dimension=0, tiled=True),
        lax.psum_scatter(grad_key_w, ("context", "expert"), scatter_dimension=0, tiled=True),
        lax.psum_scatter(grad_value_w, ("context", "expert"), scatter_dimension=0, tiled=True),
        lax.psum_scatter(grad_output_w, ("context", "expert"), scatter_dimension=0, tiled=True),
        lax.psum_scatter(grad_router, ("context", "expert"), scatter_dimension=0, tiled=True),
        lax.psum_scatter(grad_attn_scale, ("context", "expert"), scatter_dimension=0, tiled=True),
        lax.psum_scatter(grad_query_scale, ("context", "expert"), scatter_dimension=0, tiled=True),
        lax.psum_scatter(grad_key_scale, ("context", "expert"), scatter_dimension=0, tiled=True),
        lax.psum_scatter(grad_moe_scale, ("context", "expert"), scatter_dimension=0, tiled=True),
    )
    return (
        result.astype(jnp.bfloat16)[None],
        grad_inputs[None],
        reduced[0],
        reduced[1],
        reduced[2],
        reduced[3],
        reduced[4],
        reduced[5],
        reduced[6],
        reduced[7],
        reduced[8],
        expert_grads[0],
        expert_grads[1],
        expert_grads[2],
    )


def solution(mesh):
    placed = (
        P("expert", "context", None),
        P("expert", None),
        P("expert", "context", None),
        P("expert", "context", None),
        P(("context", "expert"), None),
        P(("context", "expert"), None),
        P(("context", "expert"), None),
        P(("context", "expert"), None),
        P(("context", "expert"), None),
        P(("context", "expert")),
        P(("context", "expert")),
        P(("context", "expert")),
        P(("context", "expert")),
        P("expert", "context", None),
        P("expert", "context", None),
        P("expert", "context", None),
    )
    return jax.shard_map(
        shards,
        mesh=mesh,
        in_specs=placed,
        out_specs=(
            P("expert", "context", None),
            P("expert", "context", None),
            P(("context", "expert"), None),
            P(("context", "expert"), None),
            P(("context", "expert"), None),
            P(("context", "expert"), None),
            P(("context", "expert"), None),
            P(("context", "expert")),
            P(("context", "expert")),
            P(("context", "expert")),
            P(("context", "expert")),
            P("expert", "context", None),
            P("expert", "context", None),
            P("expert", "context", None),
        ),
        check_vma=False,
    )
```

profile of v0, /device:TPU:0, one launch (start us, length us, event | category | flops | bytes accessed | tf_op | source)
XLA Modules:
  0.0 3427.0 jit_solution(9115338842763179651)
XLA Ops:
  13.5 42.5 %all-reduce.13 = (bf16[2048]{0:T(1024)(128)(2,1)S(1)}, bf16[2048]{0:T(1024)(128)(2,1)S(1)}, bf16[2048]{0:T(1024)(128)(2,1)S(1)}, bf16[2048]{0:T(1024)(128)(2,1)S(1)}) all-reduce(bf16[2048]{0:T(1024)(128)(2,1)S(1)} %dynamic-update-slice, ...), channel_id=1, replica_groups=mesh['context'=4,'expert'=8] {'context','expert'}, use_global_device_ids=true, to_apply=%add.4 | all-reduce | flops 8192 | bytes 32768
  58.1 33.0 all-gather.15.cloned.1.call-done
  98.9 71.1 %all-gather.17.cloned.1.call-done = bf16[2048,2048]{1,0:T(8,128)(2,1)} async-done(((bf16[64,2048]{1,0:T(8,128)(2,1)}), bf16[2048,2048]{1,0:T(8,128)(2,1)}) %all-gather.17.cloned.1.call-update) | async-done | bytes 8388624 | tf_op jit(solution)/shard_map/all_gather | solution.py:80
  185.3 63.7 %all-gather.11.cloned.1.call-done = bf16[2048,2048]{1,0:T(8,128)(2,1)} async-done(((bf16[64,2048]{1,0:T(8,128)(2,1)}), bf16[2048,2048]{1,0:T(8,128)(2,1)}) %all-gather.11.cloned.1.call-update) | async-done | bytes 8388624 | tf_op jit(solution)/shard_map/all_gather | solution.py:81
  262.0 40.2 %all-gather = bf16[32,64,16]{1,2,0:T(8,128)(2,1)S(1)} all-gather(bf16[1,64,16]{1,2,0:T(8,128)(2,1)S(1)} %bitcast.226), channel_id=1, replica_groups=mesh['context'=4,'expert'=8] {'context','expert'}, dimensions={0}, use_global_device_ids=true | all-gather | bytes 67584 | tf_op jit(solution)/shard_map/all_gather | solution.py:83
  321.5 36.4 %all-gather.13.cloned.1.call-done = bf16[1024,2048]{1,0:T(8,128)(2,1)} async-done(((bf16[256,2048]{1,0:T(8,128)(2,1)}), bf16[1024,2048]{1,0:T(8,128)(2,1)}) %all-gather.13.cloned.1.call-update) | async-done | bytes 4194320 | tf_op jit(solution)/shard_map/all_gather | solution.py:114
  368.6 69.6 %all-gather.21.cloned.1.call-done = bf16[2048,2048]{1,0:T(8,128)(2,1)} async-done(((bf16[64,2048]{1,0:T(8,128)(2,1)}), bf16[2048,2048]{1,0:T(8,128)(2,1)}) %all-gather.21.cloned.1.call-update) | async-done | bytes 8388624 | tf_op jit(solution)/shard_map/all_gather | solution.py:82
  447.2 22.2 scatter_custom_fusion.1
  490.1 21.3 scatter_custom_fusion
  525.5 327.5 %all-to-all-done.2 = bf16[2,8,256,2048]{3,2,0,1:T(8,128)(2,1)} async-done(((bf16[2,8,256,2048]{3,2,0,1:T(8,128)(2,1)}), bf16[2,8,256,2048]{3,2,0,1:T(8,128)(2,1)}, u32[]{:S(2)}, u32[]{:S(2)}) %all-to-all-start.2) | async-done | bytes 16777248 | tf_op jit(solution)/shard_map/all_to_all | solution.py:194
  874.7 347.6 %all-to-all-done = bf16[2,8,256,2048]{3,2,0,1:T(8,128)(2,1)} async-done(((bf16[2,8,256,2048]{3,2,0,1:T(8,128)(2,1)}), bf16[2,8,256,2048]{3,2,0,1:T(8,128)(2,1)}, u32[]{:S(2)}, u32[]{:S(2)}) %all-to-all-start) | async-done | bytes 16777248 | tf_op jit(solution)/shard_map/all_to_all | solution.py:155
  1236.5 24.7 fusion.78
  1261.2 24.7 fusion.77
  1285.9 37.1 %multiply_convert_fusion.1 = (bf16[2,2048,1024]{2,1,0:T(8,128)(2,1)}, bf16[2,2048,1024]{2,1,0:T(8,128)(2,1)}, bf16[2,2048,1024]{2,1,0:T(8,128)(2,1)}) fusion(f32[2,2048,1024]{2,1,0:T(8,128)} %fusion.77, f32[2,2048,1024]{2,1,0:T(8,128)} %fusion.78, bf16[2,2048,2048]{2,1,0:T(8,128)(2,1)} %bitcast.202, bf16[2,1024,2048]{2,1,0:T(8,128)(2,1)} %all-gather.27.cloned.1.call-done), kind=kOutput, calls=%fused_computation.15 | convolution fusion | flops 17242783744 | bytes 83886080 | tf_op jit(solution)/shard_map/erd,efd->erf/dot_general | solution.py:202
  1323.0 22.3 convolution_convert_fusion
  1357.9 26.5 fusion.79
  1384.4 27.8 add_convert_fusion
  1426.4 295.2 %all-to-all-done.1 = bf16[2,8,256,2048]{3,2,0,1:T(8,128)(2,1)} async-done(((bf16[2,8,256,2048]{3,2,0,1:T(8,128)(2,1)}), bf16[2,8,256,2048]{3,2,0,1:T(8,128)(2,1)}, u32[]{:S(2)}, u32[]{:S(2)}) %all-to-all-start.1) | async-done | bytes 16777248 | tf_op jit(solution)/shard_map/all_to_all | solution.py:173
  1742.0 24.4 gather_fusion
  1776.1 314.9 %all-to-all-done.3 = bf16[2,8,256,2048]{3,2,0,1:T(8,128)(2,1)} async-done(((bf16[2,8,256,2048]{3,2,0,1:T(8,128)(2,1)}), bf16[2,8,256,2048]{3,2,0,1:T(8,128)(2,1)}, u32[]{:S(2)}, u32[]{:S(2)}) %all-to-all-start.3) | async-done | bytes 16777248 | tf_op jit(solution)/shard_map/all_to_all | solution.py:234
  2105.0 24.4 gather_fusion.1
  2190.2 24.2 convolution_convert_fusion.1
  2214.5 24.6 convolution_convert_fusion.2
  2239.1 24.4 convolution_convert_fusion.3
  2359.8 85.7 %reduce-scatter.27.cloned.1.call-done = bf16[2,512,1024]{2,1,0:T(8,128)(2,1)} async-done(((bf16[2,2048,1024]{2,1,0:T(8,128)(2,1)}), bf16[2,512,1024]{2,1,0:T(8,128)(2,1)}) %reduce-scatter.27.cloned.1.call-update) | async-done | bytes 2097168 | tf_op jit(solution)/shard_map/reduce_scatter | solution.py:227
  2449.6 85.3 %reduce-scatter.25.cloned.1.call-done = bf16[2,512,1024]{2,1,0:T(8,128)(2,1)} async-done(((bf16[2,2048,1024]{2,1,0:T(8,128)(2,1)}), bf16[2,512,1024]{2,1,0:T(8,128)(2,1)}) %reduce-scatter.25.cloned.1.call-update) | async-done | bytes 2097168 | tf_op jit(solution)/shard_map/reduce_scatter | solution.py:224
  2538.9 133.0 %reduce-scatter.31.cloned.1.call-done = f32[64,16]{1,0:T(8,128)} async-done(((f32[2048,16]{1,0:T(8,128)}), f32[64,16]{1,0:T(8,128)}) %reduce-scatter.31.cloned.1.call-update) | async-done | bytes 4112
  2689.8 39.3 %all-reduce.12 = (f32[2048]{0:T(1024)S(1)}, f32[2048]{0:T(1024)S(1)}, f32[2048]{0:T(1024)S(1)}, f32[2048]{0:T(1024)S(1)}) all-reduce(f32[2048]{0:T(1024)S(1)} %get-tuple-element.22, f32[2048]{0:T(1024)S(1)} %get-tuple-element.20, f32[2048]{0:T(1024)S(1)} %get-tuple-element.18, ...), channel_id=9, replica_groups=mesh['context'=4,'expert'=8] {'context','expert'}, use_global_device_ids=true, to_apply=%region_32.33.clone | all-reduce | flops 8192 | bytes 65536
  2734.9 123.8 %reduce-scatter.23.cloned.1.call-done = f32[64,2048]{1,0:T(8,128)} async-done(((f32[2048,2048]{1,0:T(8,128)}), f32[64,2048]{1,0:T(8,128)}) %reduce-scatter.23.cloned.1.call-update) | async-done | bytes 524304 | tf_op jit(solution)/shard_map/reduce_scatter | solution.py:338
  2858.7 187.1 %reduce-scatter.21.cloned.1.call-done = f32[64,2048]{1,0:T(8,128)} async-done(((f32[2048,2048]{1,0:T(8,128)}), f32[64,2048]{1,0:T(8,128)}) %reduce-scatter.21.cloned.1.call-update) | async-done | bytes 524304 | tf_op jit(solution)/shard_map/reduce_scatter | solution.py:337
  3045.8 187.1 %reduce-scatter.19.cloned.1.call-done = f32[64,2048]{1,0:T(8,128)} async-done(((f32[2048,2048]{1,0:T(8,128)}), f32[64,2048]{1,0:T(8,128)}) %reduce-scatter.19.cloned.1.call-update) | async-done | bytes 524304 | tf_op jit(solution)/shard_map/reduce_scatter | solution.py:336
  3232.9 187.2 %reduce-scatter.17.cloned.1.call-done = f32[64,2048]{1,0:T(8,128)} async-done(((f32[2048,2048]{1,0:T(8,128)}), f32[64,2048]{1,0:T(8,128)}) %reduce-scatter.17.cloned.1.call-update) | async-done | bytes 524304 | tf_op jit(solution)/shard_map/reduce_scatter | solution.py:335
  (321 shorter events, 412.8 us)
Async XLA Ops:
  7.2 83.9 %all-gather.15.cloned.1.call-start = ((), (), s32[]{:S(2)}) async-start(), calls=%async_computation.16 | async-start | bytes 8650752 | tf_op jit(solution)/shard_map/all_gather | solution.py:79
  7.9 162.1 %all-gather.17.cloned.1.call-start = ((), (), s32[]{:S(2)}) async-start(), calls=%async_computation.17 | async-start | bytes 8650752 | tf_op jit(solution)/shard_map/all_gather | solution.py:80
  8.7 240.3 %all-gather.11.cloned.1.call-start = ((), (), s32[]{:S(2)}) async-start(), calls=%async_computation.14 | async-start | bytes 8650752 | tf_op jit(solution)/shard_map/all_gather | solution.py:81
  9.4 295.1 %all-gather.19.cloned.1.call-start = ((), (), s32[]{:S(2)}) async-start(), calls=%async_computation.18 | async-start | bytes 5242880 | tf_op jit(solution)/shard_map/all_gather | solution.py:113
  56.0 193.0 %copy-start.36 = (f32[2048]{0:T(1024)}, f32[2048]{0:T(1024)S(1)}, u32[]{:S(2)}) copy-start(f32[2048]{0:T(1024)S(1)} %convert_element_type.173) | copy-start | bytes 24580
  57.6 191.4 %copy-start.48 = (f32[256]{0:T(256)}, f32[256]{0:T(256)S(1)}, u32[]{:S(2)}) copy-start(f32[256]{0:T(256)S(1)} %fusion.55) | copy-start | bytes 3076
  184.9 173.0 %all-gather.13.cloned.1.call-start = ((), (), s32[]{:S(2)}) async-start(), calls=%async_computation.15 | async-start | bytes 5242880 | tf_op jit(solution)/shard_map/all_gather | solution.py:114
  255.8 182.4 %all-gather.21.cloned.1.call-start = ((), (), s32[]{:S(2)}) async-start(), calls=%async_computation.19 | async-start | bytes 8650752 | tf_op jit(solution)/shard_map/all_gather | solution.py:82
  256.9 187.5 %copy-start.44 = (f32[2048]{0:T(1024)}, f32[2048]{0:T(1024)S(1)}, u32[]{:S(2)}) copy-start(f32[2048]{0:T(1024)S(1)} %convert_element_type.184) | copy-start | bytes 24580
  302.5 143.3 %copy-start.32 = (bf16[2048,16]{0,1:T(8,128)(2,1)}, bf16[2048,16]{0,1:T(8,128)(2,1)S(1)}, u32[]{:S(2)}) copy-start(bf16[2048,16]{0,1:T(8,128)(2,1)S(1)} %reshape.515) | copy-start | bytes 196612
  303.0 187.0 %copy-start.53 = (s32[2048,1]{0,1:T(1,128)}, s32[2048,1]{0,1:T(1,128)S(1)}, u32[]{:S(2)}) copy-start(s32[2048,1]{0,1:T(1,128)S(1)} %compare_select_fusion) | copy-start | bytes 24580
  304.5 142.7 %copy-start.8 = (f32[256,2048]{1,0:T(8,128)}, f32[256,2048]{1,0:T(8,128)S(1)}, u32[]{:S(2)}) copy-start(f32[256,2048]{1,0:T(8,128)S(1)} %bitcast_convert_fusion) | copy-start | bytes 6291460
  483.5 369.4 %all-to-all-start.2 = ((bf16[2,8,256,2048]{3,2,0,1:T(8,128)(2,1)}), bf16[2,8,256,2048]{3,2,0,1:T(8,128)(2,1)}, u32[]{:S(2)}, u32[]{:S(2)}) async-start(bf16[2,8,256,2048]{3,2,0,1:T(8,128)(2,1)} %copy.187), calls=%async_computation.2 | async-start | bytes 33554432 | tf_op jit(solution)/shard_map/all_to_all | solution.py:194
  489.3 747.2 %all-gather.25.cloned.1.call-start = ((), (), s32[]{:S(2)}) async-start(), calls=%async_computation.21 | async-start | bytes 10485760 | tf_op jit(solution)/shard_map/all_gather | solution.py:102
  852.9 369.4 %all-to-all-start = ((bf16[2,8,256,2048]{3,2,0,1:T(8,128)(2,1)}), bf16[2,8,256,2048]{3,2,0,1:T(8,128)(2,1)}, u32[]{:S(2)}, u32[]{:S(2)}) async-start(bf16[2,8,256,2048]{3,2,0,1:T(8,128)(2,1)} %copy.182), calls=%async_computation | async-start | bytes 33554432 | tf_op jit(solution)/shard_map/all_to_all | solution.py:155
  858.7 402.5 %all-gather.23.cloned.1.call-start = ((), (), s32[]{:S(2)}) async-start(), calls=%async_computation.20 | async-start | bytes 10485760 | tf_op jit(solution)/shard_map/all_gather | solution.py:101
  859.4 426.4 %all-gather.27.cloned.1.call-start = ((), (), s32[]{:S(2)}) async-start(), calls=%async_computation.22 | async-start | bytes 10485760 | tf_op jit(solution)/shard_map/all_gather | solution.py:103
  1351.9 369.6 %all-to-all-start.1 = ((bf16[2,8,256,2048]{3,2,0,1:T(8,128)(2,1)}), bf16[2,8,256,2048]{3,2,0,1:T(8,128)(2,1)}, u32[]{:S(2)}, u32[]{:S(2)}) async-start(bf16[2,8,256,2048]{3,2,0,1:T(8,128)(2,1)} %copy.184), calls=%async_computation.1 | async-start | bytes 33554432 | tf_op jit(solution)/shard_map/all_to_all | solution.py:173
  1426.4 301.0 %copy-start.54 = (s32[2048,1]{0,1:T(1,128)S(1)}, s32[2048,1]{0,1:T(1,128)}, u32[]{:S(2)}) copy-start(s32[2048,1]{0,1:T(1,128)} %copy-done.53) | copy-start | bytes 24580
  1426.4 301.0 %copy-start.39 = (f32[16,256]{1,0:T(8,128)S(1)}, f32[16,256]{1,0:T(8,128)}, u32[]{:S(2)}) copy-start(f32[16,256]{1,0:T(8,128)} %copy-done.38) | copy-start | bytes 49156
  1426.4 301.0 %copy-start.51 = (f32[16,256]{1,0:T(8,128)S(1)}, f32[16,256]{1,0:T(8,128)}, u32[]{:S(2)}) copy-start(f32[16,256]{1,0:T(8,128)} %copy-done.50) | copy-start | bytes 49156
  1721.5 369.4 %all-to-all-start.3 = ((bf16[2,8,256,2048]{3,2,0,1:T(8,128)(2,1)}), bf16[2,8,256,2048]{3,2,0,1:T(8,128)(2,1)}, u32[]{:S(2)}, u32[]{:S(2)}) async-start(bf16[2,8,256,2048]{3,2,0,1:T(8,128)(2,1)} %copy.189), calls=%async_computation.3 | async-start | bytes 33554432 | tf_op jit(solution)/shard_map/all_to_all | solution.py:234
  1727.3 549.1 %reduce-scatter.15.cloned.1.call-start = ((), (), s32[]{:S(2)}) async-start(), calls=%async_computation.24 | async-start | bytes 5242880 | tf_op jit(solution)/shard_map/reduce_scatter | solution.py:299
  2159.1 137.0 %reduce-scatter.13.cloned.1.call-start = ((), (), s32[]{:S(2)}) async-start(), calls=%async_computation.23 | async-start | bytes 5242880 | tf_op jit(solution)/shard_map/reduce_scatter | solution.py:296
  2190.2 165.5 %reduce-scatter.29.cloned.1.call-start = ((), (), s32[]{:S(2)}) async-start(), calls=%async_computation.31 | async-start | bytes 10485760 | tf_op jit(solution)/shard_map/reduce_scatter | solution.py:230
  2214.4 231.1 %reduce-scatter.27.cloned.1.call-start = ((), (), s32[]{:S(2)}) async-start(), calls=%async_computation.30 | async-start | bytes 10485760 | tf_op jit(solution)/shard_map/reduce_scatter | solution.py:227
  2239.1 295.7 %reduce-scatter.25.cloned.1.call-start = ((), (), s32[]{:S(2)}) async-start(), calls=%async_computation.29 | async-start | bytes 10485760 | tf_op jit(solution)/shard_map/reduce_scatter | solution.py:224
  2263.6 408.3 %reduce-scatter.31.cloned.1.call-start = ((), (), s32[]{:S(2)}) async-start(), calls=%async_computation.32 | async-start | bytes 1081344
  2266.3 592.4 %reduce-scatter.23.cloned.1.call-start = ((), (), s32[]{:S(2)}) async-start(), calls=%async_computation.28 | async-start | bytes 17301504 | tf_op jit(solution)/shard_map/reduce_scatter | solution.py:338
  2276.1 769.6 %reduce-scatter.21.cloned.1.call-start = ((), (), s32[]{:S(2)}) async-start(), calls=%async_computation.27 | async-start | bytes 17301504 | tf_op jit(solution)/shard_map/reduce_scatter | solution.py:337
  2287.3 945.6 %reduce-scatter.19.cloned.1.call-start = ((), (), s32[]{:S(2)}) async-start(), calls=%async_computation.26 | async-start | bytes 17301504 | tf_op jit(solution)/shard_map/reduce_scatter | solution.py:336
  2323.5 1096.6 %reduce-scatter.17.cloned.1.call-start = ((), (), s32[]{:S(2)}) async-start(), calls=%async_computation.25 | async-start | bytes 17301504 | tf_op jit(solution)/shard_map/reduce_scatter | solution.py:335
  (70 other events, 1285.6 us)
Sparse Core Ops, SparseCore 0:
  11.0 80.0 all-gather.14
  94.1 75.8 all-gather.16
  173.0 75.9 all-gather.10
  251.3 51.7 all-gather.18
  305.3 52.5 all-gather.12
  360.7 77.3 all-gather.20
  492.0 87.9 all-gather.24
  861.4 87.9 all-gather.22
  951.3 87.5 all-gather.26
  2159.3 50.5 reduce-scatter.14
  2213.7 52.6 reduce-scatter.12
  2269.3 86.3 reduce-scatter.28
  2359.1 86.4 reduce-scatter.26
  2448.4 86.3 reduce-scatter.24
  2537.0 134.8 reduce-scatter.30
  2674.6 184.0 reduce-scatter.22
  2861.4 184.3 reduce-scatter.20
  3048.5 184.3 reduce-scatter.18
  3235.7 184.3 reduce-scatter.16
where the time goes:
time: 3440 us; the launch traced here: 3430 us
  waiting for transfers between devices  2570 us (75%)
  matrix products  375 us (11%)
  local copies, waits for them, and re-layouts  216 us (6%)
  blocking collectives  122 us (4%)
  other arithmetic  105 us (3%)
    all_to_all x1, waiting for transfers between devices, shards(): lax.all_to_all(send_rows.reshape(EXP_DEV, expert_devices, capacity, model...  348 us
    all_to_all x1, waiting for transfers between devices, shards(): lax.all_to_all(grad_send.reshape(EXP_DEV, expert_devices, capacity, model...  327 us
    all_to_all x1, waiting for transfers between devices, shards(): lax.all_to_all(grad_rows.reshape(EXP_DEV, expert_devices, capacity, model...  315 us
    all_to_all x1, waiting for transfers between devices, shards(): lax.all_to_all(expert_out.reshape(EXP_DEV, expert_devices, capacity, mode...  295 us
    reduce_scatter x1, waiting for transfers between devices, shards(): lax.psum_scatter(grad_query_w, ('context', 'expert'), scatter_dimension=0...  187 us
    reduce_scatter x1, waiting for transfers between devices, shards(): lax.psum_scatter(grad_key_w, ('context', 'expert'), scatter_dimension=0,...  187 us
    reduce_scatter x1, waiting for transfers between devices, shards(): lax.psum_scatter(grad_value_w, ('context', 'expert'), scatter_dimension=0...  187 us
    unnamed x20, waiting for transfers between devices  137 us
  transfers between devices with their start and end apart: 23, of which 17 were waited for; matrix products, arithmetic and copies ran while one was open for 15% of the time, Pallas kernels for 0%

commit v1 on v0

v1 whole, which is shorter than its diff:
```python
import math

import jax
import jax.numpy as jnp
from jax import lax
from jax.sharding import PartitionSpec as P

HEADS = 16
HEAD_DIM = 128
EXP_DEV = 2
EXTRA = 128

epsilon = 1e-05
rope_base = 10000.0
masked_value = -1e30
bf16 = jnp.bfloat16
f32 = jnp.float32


def dot(left, right, dims):
    return lax.dot_general(left, right, (dims, ((), ())), preferred_element_type=f32)


def cuts(extent, parts):
    unit = 16 if extent % 16 == 0 and extent // 16 >= parts else 1
    units = extent // unit
    sizes = [(units // parts + (1 if i < units % parts else 0)) * unit for i in range(parts)]
    points = [0]
    for size in sizes:
        points.append(points[-1] + size)
    return points


def swap(value, axis, count, bit):
    return lax.ppermute(value, axis, [(i, i ^ bit) for i in range(count)])


def gather_xor(shard, axis, count, dim):
    steps = count.bit_length() - 1
    points = cuts(shard.shape[dim], steps)
    found = [[] for _ in range(count)]
    for part in range(steps):
        held = {0: lax.slice_in_dim(shard, points[part], points[part + 1], axis=dim)}
        for step in range(steps):
            bit = 1 << ((part + step) % steps)
            for place in list(held):
                held[place ^ bit] = swap(held[place], axis, count, bit)
        for place in range(count):
            found[place].append(held[place])
    return [jnp.concatenate(parts, axis=dim) for parts in found]


def scatter_xor(pieces, axis, count, dim):
    steps = count.bit_length() - 1
    points = cuts(pieces[0].shape[dim], steps)
    sums = []
    for part in range(steps):
        held = {
            place: lax.slice_in_dim(piece, points[part], points[part + 1], axis=dim)
            for place, piece in enumerate(pieces)
        }
        for step in range(steps):
            bit = 1 << ((part + steps - 1 - step) % steps)
            for place in [p for p in held if p & bit]:
                came = swap(held.pop(place).astype(bf16), axis, count, bit)
                held[place ^ bit] = held[place ^ bit].astype(f32) + came.astype(f32)
        sums.append(held[0])
    return jnp.concatenate(sums, axis=dim)


def xor_blocks(value, own, count, dim):
    width = value.shape[dim] // count
    return jnp.concatenate(
        [lax.dynamic_slice_in_dim(value, (own ^ k) * width, width, dim) for k in range(count)], axis=dim
    )


def rotate(values, cosine, sine, heads):
    rows = values.shape[0]
    view = values.reshape(rows, heads, HEAD_DIM)
    first, second = view[:, :, : HEAD_DIM // 2], view[:, :, HEAD_DIM // 2 :]
    turned = jnp.concatenate(
        [first * cosine - second * sine, second * cosine + first * sine], axis=-1
    )
    return turned.reshape(rows, heads * HEAD_DIM)


def inverse_rms(values):
    return lax.rsqrt(jnp.mean(values * values, axis=-1, keepdims=True) + epsilon)


def shards(
    tokens_in,
    positions,
    routes,
    cotangent,
    w_query,
    w_key,
    w_value,
    w_output,
    router,
    attn_gain,
    query_gain,
    key_gain,
    moe_gain,
    expert_gate,
    expert_up,
    expert_down,
):
    n_ctx, n_exp = lax.axis_size("context"), lax.axis_size("expert")
    own_ctx, own_exp = lax.axis_index("context"), lax.axis_index("expert")
    own_rows = tokens_in[0]
    tokens, width = own_rows.shape
    sequence = positions.shape[1]
    experts = EXP_DEV * n_exp
    heads = HEADS // n_ctx
    columns = heads * HEAD_DIM
    part = w_query.shape[0]

    def psum_rows(stats):
        stats = lax.psum(xor_blocks(stats, own_ctx, n_ctx, 1), "context")
        return xor_blocks(stats, own_ctx, n_ctx, 1)

    small = jnp.concatenate(
        [attn_gain[:, None], moe_gain[:, None], query_gain[:, None], key_gain[:, None], router], axis=1
    )
    small = jnp.pad(small, ((0, 0), (0, EXTRA - small.shape[1])))
    packed = jnp.concatenate(
        [w.reshape(part, n_ctx, columns).transpose(1, 0, 2) for w in (w_query, w_key, w_value)]
        + [jnp.broadcast_to(small[None], (n_ctx, part, EXTRA))],
        axis=2,
    )
    packed = lax.all_to_all(packed, "context", 0, 0, tiled=True)
    packed = lax.all_gather(packed, "expert", axis=0, tiled=False)
    packed = packed.transpose(1, 0, 2, 3).reshape(width, 3 * columns + EXTRA)
    w_qkv = packed[:, : 3 * columns]
    small_full = packed[:, 3 * columns :]
    small_rows = small_full[:, :4].T.astype(f32)
    attn_scale, moe_scale = small_rows[0], small_rows[1]
    query_scale = lax.dynamic_slice_in_dim(small_rows[2], own_ctx * columns, columns)
    key_scale = lax.dynamic_slice_in_dim(small_rows[3], own_ctx * columns, columns)
    router_full = small_full[:, 4 : 4 + experts]
    w_out = lax.all_gather(w_output, "expert", axis=0, tiled=True)

    inputs = jnp.concatenate(gather_xor(own_rows, "context", n_ctx, 0), axis=0).astype(f32)
    places = xor_blocks(positions[0], own_ctx, n_ctx, 0)

    named = jnp.sum(
        (routes[0][:, :, None] == jnp.arange(experts, dtype=jnp.int32)[None, None, :]).astype(f32), axis=1
    )
    named_all = lax.all_gather(named.astype(bf16), "expert", axis=0, tiled=True).astype(f32)
    pull = lax.all_gather(cotangent[0], "expert", axis=0, tiled=True)

    gate_w = jnp.concatenate(gather_xor(expert_gate, "context", n_ctx, 1), axis=1)
    up_w = jnp.concatenate(gather_xor(expert_up, "context", n_ctx, 1), axis=1)
    down_w = xor_blocks(
        jnp.concatenate(gather_xor(expert_down, "context", n_ctx, 1), axis=1), own_ctx, n_ctx, 1
    )

    input_r = inverse_rms(inputs)
    normed = (inputs * input_r * attn_scale).astype(bf16)
    projected = dot(normed, w_qkv, ((1,), (0,)))
    query_p, key_p = projected[:, :columns], projected[:, columns : 2 * columns]
    value = projected[:, 2 * columns :].astype(bf16)
    squares = jnp.stack([jnp.sum(query_p * query_p, axis=1), jnp.sum(key_p * key_p, axis=1)])
    squares = psum_rows(squares)
    r_both = lax.rsqrt(squares / width + epsilon)
    query_r, key_r = r_both[0][:, None], r_both[1][:, None]
    frequency = jnp.exp(
        jnp.arange(HEAD_DIM // 2, dtype=f32) * (-2.0 * math.log(rope_base) / HEAD_DIM)
    )
    angles = places.astype(f32)[:, None] * frequency[None, :]
    cosine, sine = jnp.cos(angles)[:, None, :], jnp.sin(angles)[:, None, :]
    query = rotate(query_p * query_r * query_scale, cosine, sine, heads).astype(bf16)
    keyv = rotate(key_p * key_r * key_scale, cosine, sine, heads).astype(bf16)
    score_scale = HEAD_DIM ** (-0.5)
    query_h, key_h, value_h = (v.reshape(sequence, heads, HEAD_DIM) for v in (query, keyv, value))
    allowed = (places[None, :] <= places[:, None])[None]

    def scores_of():
        raw = jnp.einsum("qhd,khd->hqk", query_h, key_h, preferred_element_type=f32)
        return jnp.where(allowed, raw * score_scale, masked_value)

    scores = scores_of()
    peak = jnp.max(scores, axis=-1, keepdims=True)
    exponent = jnp.exp(scores - peak)
    total = jnp.sum(exponent, axis=-1, keepdims=True)
    log_total = peak + jnp.log(total)
    attended = (
        jnp.einsum(
            "hqk,khd->qhd", (exponent / total).astype(bf16), value_h, preferred_element_type=f32
        )
        .reshape(sequence, columns)
        .astype(bf16)
    )
    branch = dot(attended, w_out, ((1,), (0,))).astype(bf16)
    branch_own = scatter_xor(jnp.split(branch, n_ctx, axis=0), "context", n_ctx, 0)
    middle = own_rows.astype(f32) + branch_own
    middle_r = inverse_rms(middle)
    mixed_own = (middle * middle_r * moe_scale).astype(bf16)

    mixed = lax.all_gather(xor_blocks(mixed_own, own_ctx, n_ctx, 1), "expert", axis=0, tiled=True)
    router_x = xor_blocks(router_full, own_ctx, n_ctx, 0)
    router_probs = jax.nn.softmax(dot(mixed, router_x, ((1,), (0,))), axis=-1)
    local = own_exp * EXP_DEV
    gates = lax.dynamic_slice_in_dim(router_probs * named_all, local, EXP_DEV, 1)
    hidden_g, d_gate_act, d_up_act, d_gates = [], [], [], []
    for e in range(EXP_DEV):
        gate = gates[:, e : e + 1]
        gate_act = dot(mixed, gate_w[e], ((1,), (0,)))
        up_act = dot(mixed, up_w[e], ((1,), (0,)))
        back = dot(pull, down_w[e], ((1,), (1,)))
        sig = jax.nn.sigmoid(gate_act)
        silu = gate_act * sig
        hidden = (silu * up_act).astype(bf16).astype(f32)
        d_gates.append(jnp.sum(hidden * back, axis=1, keepdims=True))
        hidden_g.append((gate * hidden).astype(bf16))
        d_hidden = gate * back
        d_gate_act.append((d_hidden * up_act * sig * (1.0 + gate_act * (1.0 - sig))).astype(bf16))
        d_up_act.append((d_hidden * silu).astype(bf16))

    slots = jnp.arange(experts, dtype=jnp.int32)[None, :]
    drp = sum(
        jnp.where(slots == local + e, d_gates[e] * named_all, 0.0) for e in range(EXP_DEV)
    )
    d_logits = (
        router_probs * (drp - jnp.sum(router_probs * drp, axis=-1, keepdims=True))
    ).astype(bf16)

    d_mixed_part = (
        dot(
            jnp.concatenate(d_gate_act + d_up_act, axis=1),
            jnp.concatenate([gate_w[e] for e in range(EXP_DEV)] + [up_w[e] for e in range(EXP_DEV)], axis=1),
            ((1,), (1,)),
        )
        + dot(d_logits, router_x, ((1,), (1,)))
    ).astype(bf16)
    d_mixed = lax.psum_scatter(d_mixed_part, "expert", scatter_dimension=0, tiled=True).astype(f32)
    d_mixed = xor_blocks(d_mixed, own_ctx, n_ctx, 1)
    out_part = dot(
        jnp.concatenate(hidden_g, axis=1), down_w.reshape(-1, width), ((1,), (0,))
    ).astype(bf16)
    out_own = lax.psum_scatter(out_part, "expert", scatter_dimension=0, tiled=True).astype(f32)
    result = (middle + out_own).astype(bf16)

    g_gate = jnp.stack([dot(mixed, d_gate_act[e], ((0,), (0,))).astype(bf16) for e in range(EXP_DEV)])
    g_up = jnp.stack([dot(mixed, d_up_act[e], ((0,), (0,))).astype(bf16) for e in range(EXP_DEV)])
    g_down = jnp.stack([dot(hidden_g[e], pull, ((0,), (0,))).astype(bf16) for e in range(EXP_DEV)])
    g_gate = scatter_xor(jnp.split(g_gate, n_ctx, axis=1), "context", n_ctx, 1)
    g_up = scatter_xor(jnp.split(g_up, n_ctx, axis=1), "context", n_ctx, 1)
    g_down = scatter_xor(
        jnp.split(xor_blocks(g_down, own_ctx, n_ctx, 1), n_ctx, axis=1), "context", n_ctx, 1
    )
    g_router = xor_blocks(dot(mixed, d_logits, ((0,), (0,))), own_ctx, n_ctx, 0)

    scaled = d_mixed * moe_scale
    g_moe = jnp.sum(d_mixed * middle * middle_r, axis=0)
    d_middle = (
        cotangent[0].astype(f32)
        + middle_r * scaled
        - middle * (middle_r**3 * jnp.mean(scaled * middle, axis=-1, keepdims=True))
    )
    d_branch = jnp.concatenate(gather_xor(d_middle.astype(bf16), "context", n_ctx, 0), axis=0)
    g_output = lax.psum_scatter(
        dot(attended, d_branch, ((0,), (0,))).astype(bf16), "expert", scatter_dimension=0, tiled=True
    ).astype(f32)

    d_attended = dot(d_branch, w_out, ((1,), (1,))).astype(bf16).reshape(sequence, heads, HEAD_DIM)
    probs = jnp.exp(scores_of() - log_total)
    d_probs = jnp.einsum("qhd,khd->hqk", d_attended, value_h, preferred_element_type=f32)
    d_value = jnp.einsum("hqk,qhd->khd", probs.astype(bf16), d_attended, preferred_element_type=f32)
    inner = jnp.sum(probs * d_probs, axis=-1, keepdims=True)
    d_scores = (probs * (d_probs - inner)).astype(bf16)
    d_query = jnp.einsum("hqk,khd->qhd", d_scores, key_h, preferred_element_type=f32)
    d_key = jnp.einsum("hqk,qhd->khd", d_scores, query_h, preferred_element_type=f32)
    d_query = rotate(d_query.reshape(sequence, columns) * score_scale, cosine, -sine, heads)
    d_key = rotate(d_key.reshape(sequence, columns) * score_scale, cosine, -sine, heads)
    inner_q = jnp.sum(query_scale * d_query * query_p, axis=1)
    inner_k = jnp.sum(key_scale * d_key * key_p, axis=1)
    inner_both = psum_rows(jnp.stack([inner_q, inner_k])) / width
    g_query_gain = jnp.sum(d_query * query_p * query_r, axis=0)
    g_key_gain = jnp.sum(d_key * key_p * key_r, axis=0)
    d_query_p = query_r * (query_scale * d_query) - query_p * (query_r**3 * inner_both[0][:, None])
    d_key_p = key_r * (key_scale * d_key) - key_p * (key_r**3 * inner_both[1][:, None])
    d_projected = jnp.concatenate(
        [d_query_p.astype(bf16), d_key_p.astype(bf16), d_value.reshape(sequence, columns).astype(bf16)],
        axis=1,
    )
    d_normed_part = dot(d_projected, w_qkv, ((1,), (1,)))
    g_attn = jnp.sum(d_normed_part * inputs * input_r, axis=0)
    d_normed = scatter_xor(
        jnp.split(d_normed_part.astype(bf16), n_ctx, axis=0), "context", n_ctx, 0
    )
    own_in = own_rows.astype(f32)
    own_r = inverse_rms(own_in)
    scaled_in = d_normed * attn_scale
    input_grad = (
        d_middle
        + own_r * scaled_in
        - own_in * (own_r**3 * jnp.mean(scaled_in * own_in, axis=-1, keepdims=True))
    )

    g_qkv = dot(normed, d_projected, ((0,), (0,)))
    spread = jnp.zeros((2, width), f32)
    spread = lax.dynamic_update_slice(
        spread, jnp.stack([g_query_gain, g_key_gain]), (jnp.zeros_like(own_ctx), own_ctx * columns)
    )
    g_small = jnp.concatenate([jnp.stack([g_attn, g_moe], axis=1), spread.T, g_router], axis=1)
    g_small = jnp.pad(g_small, ((0, 0), (0, EXTRA - g_small.shape[1])))
    g_packed = jnp.concatenate([g_qkv.astype(bf16), g_small.astype(bf16)], axis=1)
    g_packed = g_packed.reshape(n_ctx, n_exp, part, -1).transpose(1, 0, 2, 3).reshape(width, -1)
    g_packed = lax.psum_scatter(g_packed, "expert", scatter_dimension=0, tiled=True)
    g_packed = lax.all_to_all(
        g_packed.reshape(n_ctx, part, -1), "context", 0, 0, tiled=True
    ).astype(f32)
    g_weights = [
        g_packed[:, :, i * columns : (i + 1) * columns].transpose(1, 0, 2).reshape(part, width)
        for i in range(3)
    ]
    g_small = jnp.sum(g_packed[:, :, 3 * columns :], axis=0)
    return (
        result[None],
        input_grad[None],
        *g_weights,
        g_output,
        g_small[:, 4 : 4 + experts],
        g_small[:, 0],
        g_small[:, 2],
        g_small[:, 3],
        g_small[:, 1],
        g_gate,
        g_up,
        g_down,
    )


def solution(mesh):
    rows = P("expert", "context", None)
    split = P(("context", "expert"), None)
    line = P(("context", "expert"))
    return jax.shard_map(
        shards,
        mesh=mesh,
        in_specs=(rows, P("expert", None), rows, rows) + (split,) * 5 + (line,) * 4 + (rows,) * 3,
        out_specs=(rows, rows) + (split,) * 5 + (line,) * 4 + (rows,) * 3,
        check_vma=False,
    )
```

time: 3440 us -> 1290 us (0.38)
  waiting for transfers between devices: 2570 us -> 510 us
  local copies, waits for them, and re-layouts: 216 us -> 125 us
  blocking collectives: 122 us -> 51.6 us
  other arithmetic: 105 us -> 151 us
    all_to_all x4 -> x1, waiting for transfers between devices: 1290 us -> 1.59 us  [shards(): lax.all_to_all(g_packed.reshape(n_ctx, part, -1), 'context', 0, 0, tiled=...]
    reduce_scatter x9 -> x4, waiting for transfers between devices: 872 us -> 121 us  [the longest x1 87.3 us: shards(): lax.psum_scatter(out_part, 'expert', scatter_dimension=0, tiled=True)]
    ppermute x0 -> x60, waiting for transfers between devices: none -> 360 us  [swap(): return lax.ppermute(value, axis, [(i, i ^ bit) for i in range(count)])]
    all_gather x9 -> x4, waiting for transfers between devices: 274 us -> 26.7 us  [the longest x1 26.7 us: shards(): packed = lax.all_gather(packed, 'expert', axis=0, tiled=False)]
    unnamed x20 -> x8, waiting for transfers between devices: 137 us -> 0.13 us
    unnamed x2 -> x0, blocking collectives: 81.7 us -> none
    all_to_all x4 -> x0, local copies, waits for them, and re-layouts: 57.3 us -> none  [the longest x1 14.6 us: shards(): lax.all_to_all(expert_out.reshape(EXP_DEV, expert_devices, capacity, mode...]
    ppermute x0 -> x60, starting transfers between devices: none -> 49.2 us  [swap(): return lax.ppermute(value, axis, [(i, i ^ bit) for i in range(count)])]
  transfers between devices with their start and end apart: 23 -> 69, of which waited for: 17 -> 41; matrix products, arithmetic and copies ran while one was open for 15% -> 27% of each run, Pallas kernels for 0% -> 0%
where the time goes in v1:
time: 1290 us
  waiting for transfers between devices  510 us (40%)
  matrix products  378 us (29%)
  other arithmetic  151 us (12%)
  local copies, waits for them, and re-layouts  125 us (10%)
  starting transfers between devices  53.8 us (4%)
  blocking collectives  51.6 us (4%)
  between operations  16.6 us (1%)
    ppermute x60, waiting for transfers between devices, swap(): return lax.ppermute(value, axis, [(i, i ^ bit) for i in range(count)])  360 us
    dot_general x23, matrix products, dot(): lax.dot_general(left, right, (dims, ((), ())), preferred_element_type=f32)  334 us
    reduce_scatter x1, waiting for transfers between devices, shards(): lax.psum_scatter(out_part, 'expert', scatter_dimension=0, tiled=True)  87.3 us
    ppermute x60, starting transfers between devices, swap(): return lax.ppermute(value, axis, [(i, i ^ bit) for i in range(count)])  49.2 us
    unnamed x285, local copies, waits for them, and re-layouts  46.3 us
    reduce_scatter x1, waiting for transfers between devices, shards(): lax.psum_scatter(d_mixed_part, 'expert', scatter_dimension=0, tiled=True)  33.5 us
    convert_element_type x2, other arithmetic, shards(): (d_hidden * up_act * sig * (1.0 + gate_act * (1.0 - sig))).astype(bf16)  30.4 us
    all_gather x1, waiting for transfers between devices, shards(): packed = lax.all_gather(packed, 'expert', axis=0, tiled=False)  26.7 us
  transfers between devices with their start and end apart: 69, of which 41 were waited for; matrix products, arithmetic and copies ran while one was open for 27% of the time, Pallas kernels for 0%

profile of v1, /device:TPU:0, one launch (start us, length us, event | category | flops | bytes accessed | tf_op | source)
XLA Modules:
  0.0 1285.2 jit_solution(1849499649532514477)
XLA Ops:
  12.9 17.3 %all_to_all.10 = bf16[4,64,1664]{2,1,0:T(8,128)(2,1)} all-to-all(bf16[4,64,1664]{2,1,0:T(8,128)(2,1)S(1)} %copy.190), channel_id=1, replica_groups=mesh['context'=4,'expert'=8] {'context'}, dimensions={0} | all-to-all | bytes 1703936 | tf_op jit(solution)/shard_map/all_to_all | solution.py:133
  72.3 26.7 %all-gather.11.cloned.1.call-done = bf16[32,64,1664]{2,1,0:T(8,128)(2,1)} async-done(((bf16[4,64,1664]{2,1,0:T(8,128)(2,1)}), bf16[32,64,1664]{2,1,0:T(8,128)(2,1)}) %all-gather.11.cloned.1.call-update) | async-done | bytes 6815760 | tf_op jit(solution)/shard_map/all_gather | solution.py:134
  177.1 12.8 collective-permute-done.7
  236.0 13.6 %collective-permute-done.15 = bf16[2,256,1024]{2,1,0:T(8,128)(2,1)S(1)} collective-permute-done((bf16[2,256,1024]{2,1,0:T(8,128)(2,1)}, bf16[2,256,1024]{2,1,0:T(8,128)(2,1)S(1)}, u32[]{:S(2)}, u32[]{:S(2)}) %collective-permute-start.15) | collective-permute-done | bytes 1048608 | tf_op jit(solution)/shard_map/ppermute | solution.py:35
  252.2 15.0 %all_gather.22 = bf16[2048,16]{0,1:T(8,128)(2,1)S(1)} all-gather(bf16[256,16]{0,1:T(8,128)(2,1)S(1)} %convert_reduce_fusion), channel_id=1, replica_groups=mesh['context'=4,'expert'=8] {'expert'}, dimensions={0}, use_global_device_ids=true | all-gather | bytes 73728 | tf_op jit(solution)/shard_map/all_gather | solution.py:151
  296.6 21.1 %collective-permute-done.24 = bf16[2,128,2048]{2,1,0:T(8,128)(2,1)} collective-permute-done((bf16[2,128,2048]{2,1,0:T(8,128)(2,1)}, bf16[2,128,2048]{2,1,0:T(8,128)(2,1)}, u32[]{:S(2)}, u32[]{:S(2)}) %collective-permute-start.24) | collective-permute-done | bytes 1048608 | tf_op jit(solution)/shard_map/ppermute | solution.py:35
  321.5 18.6 %collective-permute-done.25 = bf16[2,128,2048]{2,1,0:T(8,128)(2,1)S(1)} collective-permute-done((bf16[2,128,2048]{2,1,0:T(8,128)(2,1)}, bf16[2,128,2048]{2,1,0:T(8,128)(2,1)S(1)}, u32[]{:S(2)}, u32[]{:S(2)}) %collective-permute-start.25) | collective-permute-done | bytes 1048608 | tf_op jit(solution)/shard_map/ppermute | solution.py:35
  342.6 17.0 %collective-permute-done.19 = bf16[2,256,1024]{2,1,0:T(8,128)(2,1)S(1)} collective-permute-done((bf16[2,256,1024]{2,1,0:T(8,128)(2,1)}, bf16[2,256,1024]{2,1,0:T(8,128)(2,1)S(1)}, u32[]{:S(2)}, u32[]{:S(2)}) %collective-permute-start.19) | collective-permute-done | bytes 1048608 | tf_op jit(solution)/shard_map/ppermute | solution.py:35
  366.5 17.6 %collective-permute-done.16 = bf16[2,256,1024]{2,1,0:T(8,128)(2,1)S(1)} collective-permute-done((bf16[2,256,1024]{2,1,0:T(8,128)(2,1)}, bf16[2,256,1024]{2,1,0:T(8,128)(2,1)S(1)}, u32[]{:S(2)}, u32[]{:S(2)}) %collective-permute-start.16) | collective-permute-done | bytes 1048608 | tf_op jit(solution)/shard_map/ppermute | solution.py:35
  385.8 20.8 %collective-permute-done.22 = bf16[2,256,1024]{2,1,0:T(8,128)(2,1)S(1)} collective-permute-done((bf16[2,256,1024]{2,1,0:T(8,128)(2,1)S(1)}, bf16[2,256,1024]{2,1,0:T(8,128)(2,1)S(1)}, u32[]{:S(2)}, u32[]{:S(2)}) %collective-permute-start.22) | collective-permute-done | bytes 1048608 | tf_op jit(solution)/shard_map/ppermute | solution.py:35
  408.3 12.0 collective-permute-done.28
  450.6 13.4 %fusion.153 = f32[2048,1024]{0,1:T(8,128)} fusion(bf16[2048,2048]{1,0:T(8,128)(2,1)S(1)} %copy-done, bf16[2,2048,1024]{2,1,0:T(8,128)(2,1)} %copy-done.17), kind=kOutput, calls=%fused_computation.414 | convolution fusion | flops 8589934592 | bytes 20971520 | tf_op jit(solution)/shard_map/dot_general | solution.py:21
  475.7 13.2 %fusion.152 = f32[2048,1024]{0,1:T(8,128)} fusion(bf16[2048,2048]{1,0:T(8,128)(2,1)S(1)} %copy-done, bf16[2,2048,1024]{2,1,0:T(8,128)(2,1)} %copy-done.19), kind=kOutput, calls=%fused_computation.413 | convolution fusion | flops 8589934592 | bytes 20971520 | tf_op jit(solution)/shard_map/dot_general | solution.py:21
  488.9 13.6 %fusion.150 = f32[2048,1024]{0,1:T(8,128)} fusion(bf16[2048,2048]{1,0:T(8,128)(2,1)S(1)} %copy-done, bf16[2,2048,1024]{2,1,0:T(8,128)(2,1)} %copy-done.19), kind=kOutput, calls=%fused_computation.411 | convolution fusion | flops 8589934592 | bytes 20971520 | tf_op jit(solution)/shard_map/dot_general | solution.py:21
  502.5 20.1 %fusion.18 = (f32[2048]{0:T(1024)S(1)}, bf16[2048,1024]{0,1:T(8,128)(2,1)}, f32[1024,2048]{1,0:T(8,128)}) fusion(f32[2048,1024]{0,1:T(8,128)} %fusion.151, f32[2048,1024]{0,1:T(8,128)} %fusion.150, bf16[1,2048,2048]{2,1,0:T(8,128)(2,1)} %all-gather.13.cloned.1.call-done, bf16[2,1024,2048]{2,1,0:T(8,128)(2,1)} %pad_maximum_fusion), kind=kOutput, calls=%fused_computation.68 | convolution fusion | flops 8608806912 | bytes 41951232 | tf_op jit(solution)/shard_map/dot_general | solution.py:21
  522.5 20.3 %fusion.20 = (f32[2048]{0:T(1024)S(1)}, bf16[2048,1024]{0,1:T(8,128)(2,1)}, f32[1024,2048]{1,0:T(8,128)}) fusion(f32[2048,1024]{0,1:T(8,128)} %fusion.153, f32[2048,1024]{0,1:T(8,128)} %fusion.152, bf16[1,2048,2048]{2,1,0:T(8,128)(2,1)} %all-gather.13.cloned.1.call-done, bf16[2,1024,2048]{2,1,0:T(8,128)(2,1)} %pad_maximum_fusion), kind=kOutput, calls=%fused_computation.70 | convolution fusion | flops 8608806912 | bytes 41951232 | tf_op jit(solution)/shard_map/dot_general | solution.py:21
  552.1 16.9 %multiply_convert_fusion.4 = (bf16[2048,1024]{0,1:T(8,128)(2,1)}, bf16[2048,1024]{0,1:T(8,128)(2,1)}, bf16[2048,1024]{0,1:T(8,128)(2,1)}) fusion(f32[2048,1024]{0,1:T(8,128)} %fusion.150, f32[2048,1024]{0,1:T(8,128)} %fusion.151, f32[1024,2048]{1,0:T(8,128)} %get-tuple-element.226, f32[2048]{0:T(1024)S(1)} %bitcast.287, bf16[2048,1024]{0,1:T(8,128)(2,1)} %get-tuple-element.79), kind=kLoop, calls=%fused_computation.96 | loop fusion | flops 35651584 | bytes 41951232 | tf_op jit(solution)/shard_map/convert_element_type | solution.py:219
  569.1 13.5 %multiply_convert_fusion.3 = (bf16[2048,1024]{0,1:T(8,128)(2,1)}, bf16[2048,1024]{0,1:T(8,128)(2,1)}, bf16[2048,1024]{0,1:T(8,128)(2,1)}) fusion(f32[2048,1024]{0,1:T(8,128)} %fusion.152, f32[2048,1024]{0,1:T(8,128)S(1)} %bitcast.265, f32[1024,2048]{1,0:T(8,128)} %get-tuple-element.225, f32[2048]{0:T(1024)S(1)} %bitcast.286, ...), kind=kLoop, calls=%fused_computation.95 | loop fusion | flops 35651584 | bytes 41951232 | tf_op jit(solution)/shard_map/convert_element_type | solution.py:219
  582.6 83.5 %add_convert_fusion = bf16[2048,2048]{1,0:T(8,128)(2,1)} fusion(f32[2048,2048]{1,0:T(8,128)} %fusion.124, bf16[2048,1024]{1,0:T(8,128)(2,1)} %get-tuple-element.113, bf16[2048,1024]{1,0:T(8,128)(2,1)} %get-tuple-element.112, bf16[2048,1024]{1,0:T(8,128)(2,1)} %get-tuple-element.111, bf16[2048,1024]{1,0:T(8,128)(2,1)} %get-tuple-element.110, ...), kind=kOutput, calls=%fused_computation.18 | convolution fusion | flops 34502344704 | bytes 58720256 | tf_op jit(solution)/shard_map/dot_general | solution.py:21
  666.2 24.9 %fusion.44 = bf16[2048,2048]{1,0:T(8,128)(2,1)} fusion(bf16[2048,2048]{1,0:T(8,128)(2,1)} %bitcast.259, bf16[2048,1024]{0,1:T(8,128)(2,1)} %get-tuple-element.201, bf16[2048,1024]{0,1:T(8,128)(2,1)} %get-tuple-element.200), kind=kOutput, calls=%fused_computation.104 | convolution fusion | flops 17200840704 | bytes 25165824 | tf_op jit(solution)/shard_map/dot_general | solution.py:21
  692.4 14.0 %convert_bitcast_fusion.1 = bf16[1,1024,2048]{2,1,0:T(8,128)(2,1)} fusion(bf16[2048,1024]{0,1:T(8,128)(2,1)} %get-tuple-element.200, bf16[1,2048,2048]{2,1,0:T(8,128)(2,1)} %all-gather.13.cloned.1.call-done), kind=kOutput, calls=%fused_computation.121 | convolution fusion | flops 8592031744 | bytes 16777216 | tf_op jit(solution)/shard_map/dot_general | solution.py:21
  706.4 12.8 convert_bitcast_fusion
  719.3 33.5 %reduce-scatter.7.cloned.1.call-done = bf16[256,2048]{1,0:T(8,128)(2,1)} async-done(((bf16[2048,2048]{1,0:T(8,128)(2,1)}), bf16[256,2048]{1,0:T(8,128)(2,1)}) %reduce-scatter.7.cloned.1.call-update) | async-done | bytes 1048592 | tf_op jit(solution)/shard_map/reduce_scatter | solution.py:238
  755.6 87.3 %reduce-scatter.5.cloned.1.call-done = bf16[256,2048]{1,0:T(8,128)(2,1)} async-done(((bf16[2048,2048]{1,0:T(8,128)(2,1)}), bf16[256,2048]{1,0:T(8,128)(2,1)}) %reduce-scatter.5.cloned.1.call-update) | async-done | bytes 1048592 | tf_op jit(solution)/shard_map/reduce_scatter | solution.py:243
  955.2 12.0 fusion.25
  967.2 11.8 convolution_convert_fusion
  1014.7 12.1 convert_bitcast_fusion.2
  1050.7 12.4 convert_bitcast_fusion.5
  1114.1 11.8 collective-permute-done.56
  1141.8 16.8 %collective-permute-done.48 = bf16[2,256,1024]{2,1,0:T(8,128)(2,1)S(1)} collective-permute-done((bf16[2,256,1024]{2,1,0:T(8,128)(2,1)S(1)}, bf16[2,256,1024]{2,1,0:T(8,128)(2,1)S(1)}, u32[]{:S(2)}, u32[]{:S(2)}) %collective-permute-start.48) | collective-permute-done | bytes 1048608 | tf_op jit(solution)/shard_map/ppermute | solution.py:35
  1171.4 32.2 %collective-permute-done.53 = bf16[2,256,1024]{2,1,0:T(8,128)(2,1)} collective-permute-done((bf16[2,256,1024]{2,1,0:T(8,128)(2,1)}, bf16[2,256,1024]{2,1,0:T(8,128)(2,1)}, u32[]{:S(2)}, u32[]{:S(2)}) %collective-permute-start.53) | collective-permute-done | bytes 1048608 | tf_op jit(solution)/shard_map/ppermute | solution.py:35
  1221.3 12.6 collective-permute-done.47
  (567 shorter events, 587.8 us)
Async XLA Ops:
  7.2 91.8 %all-gather.11.cloned.1.call-start = ((), (), s32[]{:S(2)}) async-start(), calls=%async_computation.12 | async-start | bytes 7667712 | tf_op jit(solution)/shard_map/all_gather | solution.py:134
  30.2 138.7 %all-gather.7.cloned.1.call-start = ((), (), s32[]{:S(2)}) async-start(), calls=%async_computation.6 | async-start | bytes 2359296 | tf_op jit(solution)/shard_map/all_gather | solution.py:143
  35.4 409.3 %all-gather.9.cloned.1.call-start = ((), (), s32[]{:S(2)}) async-start(), calls=%async_computation.7 | async-start | bytes 9437184 | tf_op jit(solution)/shard_map/all_gather | solution.py:202
  220.2 282.3 %all-gather.13.cloned.1.call-start = ((), (), s32[]{:S(2)}) async-start(), calls=%async_computation.13 | async-start | bytes 9437184 | tf_op jit(solution)/shard_map/all_gather | solution.py:152
  224.3 53.5 %collective-permute-start.14 = (bf16[2,256,1024]{2,1,0:T(8,128)(2,1)}, bf16[2,256,1024]{2,1,0:T(8,128)(2,1)}, u32[]{:S(2)}, u32[]{:S(2)}) collective-permute-start(bf16[2,256,1024]{2,1,0:T(8,128)(2,1)} %get-tuple-element.152), channel_id=1, source_target_pairs={{0,16},{8,24},{16,0},{24,8},{1,17},{9,25},{17,1},{25,9},{2,18},{10... | collective-permute-start | bytes 3145736 | tf_op jit(solution)/shard_map/ppermute | solution.py:35
  225.3 47.5 %collective-permute-start.12 = (bf16[2,256,1024]{2,1,0:T(8,128)(2,1)}, bf16[2,256,1024]{2,1,0:T(8,128)(2,1)}, u32[]{:S(2)}, u32[]{:S(2)}) collective-permute-start(bf16[2,256,1024]{2,1,0:T(8,128)(2,1)} %get-tuple-element.152), channel_id=1, source_target_pairs={{0,8},{8,0},{16,24},{24,16},{1,9},{9,1},{17,25},{25,17},{2,10},{10... | collective-permute-start | bytes 3145736 | tf_op jit(solution)/shard_map/ppermute | solution.py:35
  230.3 60.0 %collective-permute-start.21 = (bf16[2,256,1024]{2,1,0:T(8,128)(2,1)}, bf16[2,256,1024]{2,1,0:T(8,128)(2,1)}, u32[]{:S(2)}, u32[]{:S(2)}) collective-permute-start(bf16[2,256,1024]{2,1,0:T(8,128)(2,1)} %get-tuple-element.153), channel_id=1, source_target_pairs={{0,16},{8,24},{16,0},{24,8},{1,17},{9,25},{17,1},{25,9},{2,18},{10... | collective-permute-start | bytes 3145736 | tf_op jit(solution)/shard_map/ppermute | solution.py:35
  231.3 521.4 %reduce-scatter.7.cloned.1.call-start = ((), (), s32[]{:S(2)}) async-start(), calls=%async_computation.9 | async-start | bytes 9437184 | tf_op jit(solution)/shard_map/reduce_scatter | solution.py:238
  249.6 45.5 %collective-permute-start.18 = (bf16[2,256,1024]{2,1,0:T(8,128)(2,1)}, bf16[2,256,1024]{2,1,0:T(8,128)(2,1)S(1)}, u32[]{:S(2)}, u32[]{:S(2)}) collective-permute-start(bf16[2,256,1024]{2,1,0:T(8,128)(2,1)} %get-tuple-element.154), channel_id=1, source_target_pairs={{0,8},{8,0},{16,24},{24,16},{1,9},{9,1},{17,25},{25,17},{2,10},{10... | collective-permute-start | bytes 3145736 | tf_op jit(solution)/shard_map/ppermute | solution.py:35
  250.3 67.4 %collective-permute-start.24 = (bf16[2,128,2048]{2,1,0:T(8,128)(2,1)}, bf16[2,128,2048]{2,1,0:T(8,128)(2,1)}, u32[]{:S(2)}, u32[]{:S(2)}) collective-permute-start(bf16[2,128,2048]{2,1,0:T(8,128)(2,1)} %get-tuple-element.156), channel_id=1, source_target_pairs={{0,8},{8,0},{16,24},{24,16},{1,9},{9,1},{17,25},{25,17},{2,10},{10... | collective-permute-start | bytes 3145736 | tf_op jit(solution)/shard_map/ppermute | solution.py:35
  272.7 67.3 %collective-permute-start.25 = (bf16[2,128,2048]{2,1,0:T(8,128)(2,1)}, bf16[2,128,2048]{2,1,0:T(8,128)(2,1)S(1)}, u32[]{:S(2)}, u32[]{:S(2)}) collective-permute-start(bf16[2,128,2048]{2,1,0:T(8,128)(2,1)} %get-tuple-element.155), channel_id=1, source_target_pairs={{0,8},{8,0},{16,24},{24,16},{1,9},{9,1},{17,25},{25,17},{2,10},{10... | collective-permute-start | bytes 3145736 | tf_op jit(solution)/shard_map/ppermute | solution.py:35
  277.8 81.9 %collective-permute-start.19 = (bf16[2,256,1024]{2,1,0:T(8,128)(2,1)}, bf16[2,256,1024]{2,1,0:T(8,128)(2,1)S(1)}, u32[]{:S(2)}, u32[]{:S(2)}) collective-permute-start(bf16[2,256,1024]{2,1,0:T(8,128)(2,1)} %get-tuple-element.153), channel_id=1, source_target_pairs={{0,8},{8,0},{16,24},{24,16},{1,9},{9,1},{17,25},{25,17},{2,10},{10... | collective-permute-start | bytes 3145736 | tf_op jit(solution)/shard_map/ppermute | solution.py:35
  290.4 69.8 %collective-permute-start.20 = (bf16[2,256,1024]{2,1,0:T(8,128)(2,1)}, bf16[2,256,1024]{2,1,0:T(8,128)(2,1)S(1)}, u32[]{:S(2)}, u32[]{:S(2)}) collective-permute-start(bf16[2,256,1024]{2,1,0:T(8,128)(2,1)} %get-tuple-element.154), channel_id=1, source_target_pairs={{0,16},{8,24},{16,0},{24,8},{1,17},{9,25},{17,1},{25,9},{2,18},{10... | collective-permute-start | bytes 3145736 | tf_op jit(solution)/shard_map/ppermute | solution.py:35
  295.1 66.2 %collective-permute-start.27 = (bf16[2,128,2048]{2,1,0:T(8,128)(2,1)S(1)}, bf16[2,128,2048]{2,1,0:T(8,128)(2,1)S(1)}, u32[]{:S(2)}, u32[]{:S(2)}) collective-permute-start(bf16[2,128,2048]{2,1,0:T(8,128)(2,1)S(1)} %copy-done.66), channel_id=1, source_target_pairs={{0,16},{8,24},{16,0},{24,8},{1,17},{9,25},{17,1},{25,9},{2,18},{10... | collective-permute-start | bytes 3145736 | tf_op jit(solution)/shard_map/ppermute | solution.py:35
  317.7 47.0 %collective-permute-start.26 = (bf16[2,128,2048]{2,1,0:T(8,128)(2,1)S(1)}, bf16[2,128,2048]{2,1,0:T(8,128)(2,1)S(1)}, u32[]{:S(2)}, u32[]{:S(2)}) collective-permute-start(bf16[2,128,2048]{2,1,0:T(8,128)(2,1)S(1)} %copy-done.65), channel_id=1, source_target_pairs={{0,16},{8,24},{16,0},{24,8},{1,17},{9,25},{17,1},{25,9},{2,18},{10... | collective-permute-start | bytes 3145736 | tf_op jit(solution)/shard_map/ppermute | solution.py:35
  360.2 46.4 %collective-permute-start.22 = (bf16[2,256,1024]{2,1,0:T(8,128)(2,1)S(1)}, bf16[2,256,1024]{2,1,0:T(8,128)(2,1)S(1)}, u32[]{:S(2)}, u32[]{:S(2)}) collective-permute-start(bf16[2,256,1024]{2,1,0:T(8,128)(2,1)S(1)} %collective-permute-done.18), channel_id=1, source_target_pairs={{0,16},{8,24},{16,0},{24,8},{1,17},{9,25},{17,1},{25,9},{2,18},{10... | collective-permute-start | bytes 3145736 | tf_op jit(solution)/shard_map/ppermute | solution.py:35
  361.3 46.9 %collective-permute-start.23 = (bf16[2,256,1024]{2,1,0:T(8,128)(2,1)}, bf16[2,256,1024]{2,1,0:T(8,128)(2,1)S(1)}, u32[]{:S(2)}, u32[]{:S(2)}) collective-permute-start(bf16[2,256,1024]{2,1,0:T(8,128)(2,1)} %collective-permute-done.21), channel_id=1, source_target_pairs={{0,8},{8,0},{16,24},{24,16},{1,9},{9,1},{17,25},{25,17},{2,10},{10... | collective-permute-start | bytes 3145736 | tf_op jit(solution)/shard_map/ppermute | solution.py:35
  364.7 55.5 %collective-permute-start.28 = (bf16[2,128,2048]{2,1,0:T(8,128)(2,1)}, bf16[2,128,2048]{2,1,0:T(8,128)(2,1)S(1)}, u32[]{:S(2)}, u32[]{:S(2)}) collective-permute-start(bf16[2,128,2048]{2,1,0:T(8,128)(2,1)} %collective-permute-done.24), channel_id=1, source_target_pairs={{0,16},{8,24},{16,0},{24,8},{1,17},{9,25},{17,1},{25,9},{2,18},{10... | collective-permute-start | bytes 3145736 | tf_op jit(solution)/shard_map/ppermute | solution.py:35
  666.1 176.8 %reduce-scatter.5.cloned.1.call-start = ((), (), s32[]{:S(2)}) async-start(), calls=%async_computation.8 | async-start | bytes 9437184 | tf_op jit(solution)/shard_map/reduce_scatter | solution.py:243
  691.1 568.6 %reduce-scatter.9.cloned.1.call-start = ((), (), s32[]{:S(2)}) async-start(), calls=%async_computation.10 | async-start | bytes 7667712 | tf_op jit(solution)/shard_map/reduce_scatter | solution.py:312
  1002.3 266.7 %reduce-scatter.11.cloned.1.call-start = ((), (), s32[]{:S(2)}) async-start(), calls=%async_computation.11 | async-start | bytes 2359296 | tf_op jit(solution)/shard_map/reduce_scatter | solution.py:264
  1009.7 97.2 %collective-permute-start.57 = (bf16[2,128,2048]{2,1,0:T(8,128)(2,1)}, bf16[2,128,2048]{2,1,0:T(8,128)(2,1)}, u32[]{:S(2)}, u32[]{:S(2)}) collective-permute-start(bf16[2,128,2048]{2,1,0:T(8,128)(2,1)} %slice.498), channel_id=1, source_target_pairs={{0,8},{8,0},{16,24},{24,16},{1,9},{9,1},{17,25},{25,17},{2,10},{10... | collective-permute-start | bytes 3145736 | tf_op jit(solution)/shard_map/ppermute | solution.py:35
  1011.8 53.2 %collective-permute-start.55 = (bf16[2,128,2048]{2,1,0:T(8,128)(2,1)}, bf16[2,128,2048]{2,1,0:T(8,128)(2,1)}, u32[]{:S(2)}, u32[]{:S(2)}) collective-permute-start(bf16[2,128,2048]{2,1,0:T(8,128)(2,1)} %get-tuple-element.144), channel_id=1, source_target_pairs={{0,16},{8,24},{16,0},{24,8},{1,17},{9,25},{17,1},{25,9},{2,18},{10... | collective-permute-start | bytes 3145736 | tf_op jit(solution)/shard_map/ppermute | solution.py:35
  1013.2 55.3 %collective-permute-start.58 = (bf16[2,128,2048]{2,1,0:T(8,128)(2,1)}, bf16[2,128,2048]{2,1,0:T(8,128)(2,1)}, u32[]{:S(2)}, u32[]{:S(2)}) collective-permute-start(bf16[2,128,2048]{2,1,0:T(8,128)(2,1)} %get-tuple-element.145), channel_id=1, source_target_pairs={{0,8},{8,0},{16,24},{24,16},{1,9},{9,1},{17,25},{25,17},{2,10},{10... | collective-permute-start | bytes 3145736 | tf_op jit(solution)/shard_map/ppermute | solution.py:35
  1103.4 55.2 %collective-permute-start.48 = (bf16[2,256,1024]{2,1,0:T(8,128)(2,1)S(1)}, bf16[2,256,1024]{2,1,0:T(8,128)(2,1)S(1)}, u32[]{:S(2)}, u32[]{:S(2)}) collective-permute-start(bf16[2,256,1024]{2,1,0:T(8,128)(2,1)S(1)} %copy-done.57), channel_id=1, source_target_pairs={{0,16},{8,24},{16,0},{24,8},{1,17},{9,25},{17,1},{25,9},{2,18},{10... | collective-permute-start | bytes 3145736 | tf_op jit(solution)/shard_map/ppermute | solution.py:35
  1106.8 51.8 %collective-permute-start.51 = (bf16[2,256,1024]{2,1,0:T(8,128)(2,1)S(1)}, bf16[2,256,1024]{2,1,0:T(8,128)(2,1)S(1)}, u32[]{:S(2)}, u32[]{:S(2)}) collective-permute-start(bf16[2,256,1024]{2,1,0:T(8,128)(2,1)S(1)} %copy-done.56), channel_id=1, source_target_pairs={{0,8},{8,0},{16,24},{24,16},{1,9},{9,1},{17,25},{25,17},{2,10},{10... | collective-permute-start | bytes 3145736 | tf_op jit(solution)/shard_map/ppermute | solution.py:35
  1113.6 102.9 %collective-permute-start.42 = (bf16[2,256,1024]{2,1,0:T(8,128)(2,1)}, bf16[2,256,1024]{2,1,0:T(8,128)(2,1)}, u32[]{:S(2)}, u32[]{:S(2)}) collective-permute-start(bf16[2,256,1024]{2,1,0:T(8,128)(2,1)} %get-tuple-element.102), channel_id=1, source_target_pairs={{0,16},{8,24},{16,0},{24,8},{1,17},{9,25},{17,1},{25,9},{2,18},{10... | collective-permute-start | bytes 3145736 | tf_op jit(solution)/shard_map/ppermute | solution.py:35
  1125.9 45.0 %collective-permute-start.50 = (bf16[2,256,1024]{2,1,0:T(8,128)(2,1)}, bf16[2,256,1024]{2,1,0:T(8,128)(2,1)}, u32[]{:S(2)}, u32[]{:S(2)}) collective-permute-start(bf16[2,256,1024]{2,1,0:T(8,128)(2,1)} %get-tuple-element.98), channel_id=1, source_target_pairs={{0,8},{8,0},{16,24},{24,16},{1,9},{9,1},{17,25},{25,17},{2,10},{10... | collective-permute-start | bytes 3145736 | tf_op jit(solution)/shard_map/ppermute | solution.py:35
  1136.1 67.5 %collective-permute-start.53 = (bf16[2,256,1024]{2,1,0:T(8,128)(2,1)}, bf16[2,256,1024]{2,1,0:T(8,128)(2,1)}, u32[]{:S(2)}, u32[]{:S(2)}) collective-permute-start(bf16[2,256,1024]{2,1,0:T(8,128)(2,1)} %get-tuple-element.99), channel_id=1, source_target_pairs={{0,16},{8,24},{16,0},{24,8},{1,17},{9,25},{17,1},{25,9},{2,18},{10... | collective-permute-start | bytes 3145736 | tf_op jit(solution)/shard_map/ppermute | solution.py:35
  1158.6 58.8 %collective-permute-start.45 = (bf16[2,256,1024]{2,1,0:T(8,128)(2,1)}, bf16[2,256,1024]{2,1,0:T(8,128)(2,1)}, u32[]{:S(2)}, u32[]{:S(2)}) collective-permute-start(bf16[2,256,1024]{2,1,0:T(8,128)(2,1)} %get-tuple-element.104), channel_id=1, source_target_pairs={{0,8},{8,0},{16,24},{24,16},{1,9},{9,1},{17,25},{25,17},{2,10},{10... | collective-permute-start | bytes 3145736 | tf_op jit(solution)/shard_map/ppermute | solution.py:35
  1160.6 54.3 %collective-permute-start.37 = (bf16[128,2048]{1,0:T(8,128)(2,1)}, bf16[128,2048]{1,0:T(8,128)(2,1)}, u32[]{:S(2)}, u32[]{:S(2)}) collective-permute-start(bf16[128,2048]{1,0:T(8,128)(2,1)} %get-tuple-element.131), channel_id=1, source_target_pairs={{0,16},{8,24},{16,0},{24,8},{1,17},{9,25},{17,1},{25,9},{2,18},{10... | collective-permute-start | bytes 1572872 | tf_op jit(solution)/shard_map/ppermute | solution.py:35
  1170.9 50.4 %collective-permute-start.44 = (bf16[2,256,1024]{2,1,0:T(8,128)(2,1)}, bf16[2,256,1024]{2,1,0:T(8,128)(2,1)S(1)}, u32[]{:S(2)}, u32[]{:S(2)}) collective-permute-start(bf16[2,256,1024]{2,1,0:T(8,128)(2,1)} %get-tuple-element.106), channel_id=1, source_target_pairs={{0,8},{8,0},{16,24},{24,16},{1,9},{9,1},{17,25},{25,17},{2,10},{10... | collective-permute-start | bytes 3145736 | tf_op jit(solution)/shard_map/ppermute | solution.py:35
  (163 other events, 3105.1 us)
Sparse Core Ops, SparseCore 0:
  30.3 68.6 all-gather.10
  100.6 27.6 all-gather.6
  220.3 79.2 all-gather.8
  301.0 80.5 all-gather.12
  666.2 86.4 reduce-scatter.6
  754.9 87.9 reduce-scatter.4
  1002.5 75.1 reduce-scatter.8
  1167.2 36.6 reduce-scatter.10

commit v2 on v1

v2 whole, which is shorter than its diff:
```python
import math

import jax
import jax.numpy as jnp
from jax import lax
from jax.experimental import pallas as pl
from jax.experimental.pallas import tpu as pltpu
from jax.sharding import PartitionSpec as P

HEADS = 16
HEAD_DIM = 128
EXP_DEV = 2
EXTRA = 128
VMEM_BYTES = 56 * 1024 * 1024

epsilon = 1e-05
rope_base = 10000.0
masked_value = -1e30
bf16 = jnp.bfloat16
f32 = jnp.float32


def dot(left, right, dims):
    return lax.dot_general(left, right, (dims, ((), ())), preferred_element_type=f32)


def cuts(extent, parts):
    unit = 16 if extent % 16 == 0 and extent // 16 >= parts else 1
    units = extent // unit
    sizes = [(units // parts + (1 if i < units % parts else 0)) * unit for i in range(parts)]
    points = [0]
    for size in sizes:
        points.append(points[-1] + size)
    return points


def swap(value, axis, count, bit):
    return lax.ppermute(value, axis, [(i, i ^ bit) for i in range(count)])


def after(value, *others):
    return lax.optimization_barrier((value, others))[0]


def gather_many(shards, axis, count):
    steps = count.bit_length() - 1
    held = [{0: shard} for shard in shards]
    came = [[] for _ in range(steps)]
    for step in range(steps):
        for index, found in enumerate(held):
            bit = 1 << ((index + step) % steps)
            for place in list(found):
                found[place ^ bit] = swap(found[place], axis, count, bit)
                came[step].append(found[place ^ bit])
    return [[found[place] for place in range(count)] for found in held], came


def scatter_many(pieces, axis, count):
    steps = count.bit_length() - 1
    held = [dict(enumerate(own)) for own in pieces]
    came = [[] for _ in range(steps)]
    for step in range(steps):
        for index, found in enumerate(held):
            bit = 1 << ((index + steps - 1 - step) % steps)
            for place in [p for p in found if p & bit]:
                new = swap(found.pop(place).astype(bf16), axis, count, bit)
                came[step].append(new)
                found[place ^ bit] = found[place ^ bit].astype(f32) + new.astype(f32)
    return [found[0] for found in held], came


def slices(value, count, dim):
    points = cuts(value.shape[dim], max(count, 1))
    return [
        lax.slice_in_dim(value, points[i], points[i + 1], axis=dim) for i in range(max(count, 1))
    ]


def gather_xor(shard, axis, count, dim):
    found, _ = gather_many(slices(shard, count.bit_length() - 1, dim), axis, count)
    return jnp.concatenate([part[k] for k in range(count) for part in found], axis=dim)


def scatter_xor(pieces, axis, count, dim):
    parts = count.bit_length() - 1
    cut = [slices(piece, parts, dim) for piece in pieces]
    sums, _ = scatter_many([[own[j] for own in cut] for j in range(parts)], axis, count)
    return jnp.concatenate(sums, axis=dim)


def xor_blocks(value, own, count, dim):
    width = value.shape[dim] // count
    return jnp.concatenate(
        [lax.dynamic_slice_in_dim(value, (own ^ k) * width, width, dim) for k in range(count)], axis=dim
    )


def cost(flops, moved, exps=0):
    return pl.CostEstimate(flops=flops, bytes_accessed=moved, transcendentals=exps)


def params(steps):
    return pltpu.CompilerParams(
        dimension_semantics=("arbitrary",) * steps, vmem_limit_bytes=VMEM_BYTES
    )


def turn(values, cosine, sine):
    return values * cosine + pltpu.roll(values, HEAD_DIM // 2, 1) * sine


def attend_kernel(
    chunk, query_p, key_p, value, stats, scale, cosine, sine, place_col, place_row,
    attended, query_out, key_out, log_total,
):
    cos, sin = cosine[...], sine[...]
    scales = scale[0]
    query = turn(query_p[...] * stats[:, 0:1] * scales[0:1], cos, sin).astype(bf16)
    keyv = turn(key_p[...] * stats[:, 1:2] * scales[1:2], cos, sin).astype(bf16)
    query_out[...] = query
    key_out[...] = keyv
    values = value[...].astype(bf16)
    for start in range(0, query_p.shape[0], chunk):
        rows = slice(start, start + chunk)
        scores = dot(query[rows], keyv, ((1,), (1,))) * HEAD_DIM ** (-0.5)
        scores = jnp.where(place_row[...] <= place_col[rows], scores, masked_value)
        peak = jnp.max(scores, axis=1, keepdims=True)
        exponent = jnp.exp(scores - peak)
        total = jnp.sum(exponent, axis=1, keepdims=True)
        weights = (exponent * (1.0 / total)).astype(bf16)
        attended[rows] = dot(weights, values, ((1,), (0,))).astype(bf16)
        log_total[0, rows] = peak + jnp.log(total)


def attend(projected, stats, scales, cosine, sine, places, heads):
    rows = projected.shape[0]
    head = lambda offset: pl.BlockSpec((rows, HEAD_DIM), lambda h: (0, offset + h))
    whole = lambda shape: pl.BlockSpec(shape, lambda h: (0,) * len(shape))
    low = jax.ShapeDtypeStruct((rows, heads * HEAD_DIM), bf16)
    return pl.pallas_call(
        lambda *refs: attend_kernel(min(256, rows), *refs),
        grid=(heads,),
        in_specs=[
            head(0), head(heads), head(2 * heads),
            whole((rows, 2)),
            pl.BlockSpec((1, 2, HEAD_DIM), lambda h: (h, 0, 0)),
            whole((rows, HEAD_DIM)), whole((rows, HEAD_DIM)),
            whole((rows, 1)), whole((1, rows)),
        ],
        out_specs=[head(0), head(0), head(0), pl.BlockSpec((1, rows, 1), lambda h: (h, 0, 0))],
        out_shape=[low, low, low, jax.ShapeDtypeStruct((heads, rows, 1), f32)],
        compiler_params=params(1),
        cost_estimate=cost(4 * heads * rows * rows * HEAD_DIM, 24 * low.size // 2, heads * rows * rows),
        name="attend",
    )(projected, projected, projected, stats, scales, cosine, sine, places[:, None], places[None, :])


def attend_back_kernel(
    chunk, query_p, key_p, value, query, keyv, d_attended, log_total, stats, scale, cosine, sine,
    place_col, place_row, d_query, d_key, d_value, inner_q, inner_k, gains,
):
    values = value[...].astype(bf16)
    keys = keyv[...]
    for start in range(0, query_p.shape[0], chunk):
        rows = slice(start, start + chunk)
        queries, pull = query[rows], d_attended[rows]
        scores = dot(queries, keys, ((1,), (1,))) * HEAD_DIM ** (-0.5)
        scores = jnp.where(place_row[...] <= place_col[rows], scores, masked_value)
        probs = jnp.exp(scores - log_total[0, rows])
        d_probs = dot(pull, values, ((1,), (1,)))
        inner = jnp.sum(probs * d_probs, axis=1, keepdims=True)
        d_scores = (probs * (d_probs - inner)).astype(bf16)
        d_query[rows] = dot(d_scores, keys, ((1,), (0,)))
        more_key = dot(d_scores, queries, ((0,), (0,)))
        more_value = dot(probs.astype(bf16), pull, ((0,), (0,)))
        if start == 0:
            d_key[...] = more_key
            sums = more_value
        else:
            d_key[...] += more_key
            sums = sums + more_value
    d_value[...] = sums.astype(bf16)
    cos, sin = cosine[...], -sine[...]
    scales = scale[0]
    for index, (grad, before, inner_out) in enumerate(
        ((d_query, query_p, inner_q), (d_key, key_p, inner_k))
    ):
        back = turn(grad[...] * HEAD_DIM ** (-0.5), cos, sin)
        grad[...] = back
        moved = back * before[...]
        inner_out[0] = jnp.sum(moved * scales[index : index + 1], axis=1, keepdims=True)
        gains[0, index : index + 1] = jnp.sum(moved * stats[:, index : index + 1], axis=0, keepdims=True)


def attend_back(projected, query, keyv, d_attended, log_total, stats, scales, cosine, sine, places, heads):
    rows = projected.shape[0]
    head = lambda offset: pl.BlockSpec((rows, HEAD_DIM), lambda h: (0, offset + h))
    whole = lambda shape: pl.BlockSpec(shape, lambda h: (0,) * len(shape))
    column = pl.BlockSpec((1, rows, 1), lambda h: (h, 0, 0))
    pair = pl.BlockSpec((1, 2, HEAD_DIM), lambda h: (h, 0, 0))
    full = (rows, heads * HEAD_DIM)
    return pl.pallas_call(
        lambda *refs: attend_back_kernel(min(256, rows), *refs),
        grid=(heads,),
        in_specs=[
            head(0), head(heads), head(2 * heads), head(0), head(0), head(0),
            column, whole((rows, 2)), pair,
            whole((rows, HEAD_DIM)), whole((rows, HEAD_DIM)),
            whole((rows, 1)), whole((1, rows)),
        ],
        out_specs=[head(0), head(0), head(0), column, column, pair],
        out_shape=[
            jax.ShapeDtypeStruct(full, f32),
            jax.ShapeDtypeStruct(full, f32),
            jax.ShapeDtypeStruct(full, bf16),
            jax.ShapeDtypeStruct((heads, rows, 1), f32),
            jax.ShapeDtypeStruct((heads, rows, 1), f32),
            jax.ShapeDtypeStruct((heads, 2, HEAD_DIM), f32),
        ],
        compiler_params=params(1),
        cost_estimate=cost(
            10 * heads * rows * rows * HEAD_DIM, 30 * rows * heads * HEAD_DIM, heads * rows * rows
        ),
        name="attend_back",
    )(
        projected, projected, projected, query, keyv, d_attended, log_total, stats, scales,
        cosine, sine, places[:, None], places[None, :],
    )


def experts_kernel(e, mixed, pull, gates, gate_w, up_w, down_w, hidden_g, d_acts, d_gates):
    gate = gates[:, e : e + 1]
    width = gate_w.shape[1]
    gate_act = dot(mixed[...], gate_w[...], ((1,), (0,)))
    up_act = dot(mixed[...], up_w[...], ((1,), (0,)))
    back = dot(pull[...], down_w[...], ((1,), (1,)))
    sig = jax.nn.sigmoid(gate_act)
    silu = gate_act * sig
    hidden = (silu * up_act).astype(bf16).astype(f32)
    d_gates[...] = jnp.sum(hidden * back, axis=1, keepdims=True)
    hidden_g[...] = (gate * hidden).astype(bf16)
    d_hidden = gate * back
    d_acts[:, :width] = (d_hidden * up_act * sig * (1.0 + gate_act * (1.0 - sig))).astype(bf16)
    d_acts[:, width:] = (d_hidden * silu).astype(bf16)


def run_experts(mixed, pull, gates, gate_w, up_w, down_w, e):
    rows, (width, hidden) = mixed.shape[0], gate_w.shape
    block = min(256, rows)
    here = lambda n: pl.BlockSpec((block, n), lambda i: (i, 0))
    whole = lambda w: pl.BlockSpec(w.shape, lambda i: (0, 0))
    return pl.pallas_call(
        lambda *refs: experts_kernel(e, *refs),
        grid=(rows // block,),
        in_specs=[
            here(width), here(width), here(gates.shape[1]), whole(gate_w), whole(up_w), whole(down_w),
        ],
        out_specs=[here(hidden), here(2 * hidden), here(1)],
        out_shape=[
            jax.ShapeDtypeStruct((rows, hidden), bf16),
            jax.ShapeDtypeStruct((rows, 2 * hidden), bf16),
            jax.ShapeDtypeStruct((rows, 1), f32),
        ],
        compiler_params=params(1),
        cost_estimate=cost(
            6 * rows * width * hidden, 2 * (2 * rows * width + 3 * width * hidden + 3 * rows * hidden), rows * hidden
        ),
        name="expert",
    )(mixed, pull, gates, gate_w, up_w, down_w)


def rows_back_kernel(count, *refs):
    d_acts, gate_w, up_w = refs[:count], refs[count : 2 * count], refs[2 * count : 3 * count]
    d_logits, router, out = refs[3 * count :]
    hidden = gate_w[0].shape[1]
    total = dot(d_logits[...], router[...], ((1,), (1,)))
    for e in range(count):
        total += dot(d_acts[e][:, :hidden], gate_w[e][...], ((1,), (1,)))
        total += dot(d_acts[e][:, hidden:], up_w[e][...], ((1,), (1,)))
    out[...] = total.astype(bf16)


def rows_back(d_acts, d_logits, gate_w, up_w, router):
    rows = d_logits.shape[0]
    count = len(d_acts)
    width, hidden = gate_w[0].shape
    block, cut = min(512, rows), min(512, width)
    weight = pl.BlockSpec((cut, hidden), lambda j, i: (j, 0))
    return pl.pallas_call(
        lambda *refs: rows_back_kernel(count, *refs),
        grid=(width // cut, rows // block),
        in_specs=[pl.BlockSpec((block, 2 * hidden), lambda j, i: (i, 0))] * count
        + [weight] * (2 * count)
        + [
            pl.BlockSpec((block, d_logits.shape[1]), lambda j, i: (i, 0)),
            pl.BlockSpec((cut, router.shape[1]), lambda j, i: (j, 0)),
        ],
        out_specs=pl.BlockSpec((block, cut), lambda j, i: (i, j)),
        out_shape=jax.ShapeDtypeStruct((rows, width), bf16),
        compiler_params=params(2),
        cost_estimate=cost(
            4 * count * rows * width * hidden, 4 * count * hidden * (4 * rows + width) + 2 * rows * width
        ),
        name="rows_back",
    )(*d_acts, *gate_w, *up_w, d_logits, router)


def inverse_rms(values):
    return lax.rsqrt(jnp.mean(values * values, axis=-1, keepdims=True) + epsilon)


def shards(
    tokens_in,
    positions,
    routes,
    cotangent,
    w_query,
    w_key,
    w_value,
    w_output,
    router,
    attn_gain,
    query_gain,
    key_gain,
    moe_gain,
    expert_gate,
    expert_up,
    expert_down,
):
    n_ctx, n_exp = lax.axis_size("context"), lax.axis_size("expert")
    own_ctx, own_exp = lax.axis_index("context"), lax.axis_index("expert")
    own_rows = tokens_in[0]
    tokens, width = own_rows.shape
    sequence = positions.shape[1]
    experts = EXP_DEV * n_exp
    heads = HEADS // n_ctx
    columns = heads * HEAD_DIM
    part = w_query.shape[0]

    def psum_rows(stats):
        stats = lax.psum(xor_blocks(stats, own_ctx, n_ctx, 1), "context")
        return xor_blocks(stats, own_ctx, n_ctx, 1)

    small = jnp.concatenate(
        [attn_gain[:, None], moe_gain[:, None], query_gain[:, None], key_gain[:, None], router], axis=1
    )
    small = jnp.pad(small, ((0, 0), (0, EXTRA - small.shape[1])))

    def packed_for(owner):
        cut = [lax.dynamic_slice_in_dim(w, owner * columns, columns, 1) for w in (w_query, w_key, w_value)]
        return jnp.concatenate(cut + [small], axis=1)

    def trade(blocks):
        return [blocks[0]] + [swap(blocks[k], "context", n_ctx, k) for k in range(1, n_ctx)]

    packed = jnp.stack(trade([packed_for(own_ctx ^ k) for k in range(n_ctx)]))
    packed = xor_blocks(packed, own_ctx, n_ctx, 0)
    packed = lax.all_gather(packed, "expert", axis=0, tiled=False)
    packed = packed.transpose(1, 0, 2, 3).reshape(width, 3 * columns + EXTRA)
    w_qkv = packed[:, : 3 * columns]
    small_full = packed[:, 3 * columns :]
    small_rows = small_full[:, :4].T.astype(f32)
    attn_scale, moe_scale = small_rows[0], small_rows[1]
    query_scale = lax.dynamic_slice_in_dim(small_rows[2], own_ctx * columns, columns)
    key_scale = lax.dynamic_slice_in_dim(small_rows[3], own_ctx * columns, columns)
    router_full = jnp.pad(small_full[:, 4 : 4 + experts], ((0, 0), (0, EXTRA - experts)))

    inputs = gather_xor(own_rows, "context", n_ctx, 0).astype(f32)
    places = xor_blocks(positions[0], own_ctx, n_ctx, 0)
    named = jnp.sum(
        (routes[0][:, :, None] == jnp.arange(experts, dtype=jnp.int32)[None, None, :]).astype(f32), axis=1
    )
    w_out = lax.all_gather(after(w_output, packed), "expert", axis=0, tiled=True)

    def fetch_expert(e, *first):
        shards = expert_gate[e], expert_up[e], expert_down[e]
        if first:
            shards = after(shards, *first)
        halves = slices(shards[2], n_ctx.bit_length() - 1, 0)
        found, came = gather_many([shards[0], shards[1], *halves], "context", n_ctx)
        return (found[0], found[1], found[2:]), came

    def whole_expert(gate_k, up_k, down_k):
        down = jnp.concatenate([half[k] for k in range(n_ctx) for half in down_k])
        return jnp.concatenate(gate_k), jnp.concatenate(up_k), xor_blocks(down, own_ctx, n_ctx, 0)

    fetched, came = fetch_expert(0)

    inputs = after(inputs, came[0])
    input_r = inverse_rms(inputs)
    normed = (inputs * input_r * attn_scale).astype(bf16)
    projected = dot(normed, w_qkv, ((1,), (0,)))
    query_p, key_p = projected[:, :columns], projected[:, columns : 2 * columns]
    squares = jnp.stack([jnp.sum(query_p * query_p, axis=1), jnp.sum(key_p * key_p, axis=1)])
    squares = psum_rows(after(squares, came[1][0:4:2]))
    pull = lax.all_gather(after(cotangent[0], squares), "expert", axis=0, tiled=True)
    r_both = lax.rsqrt(squares / width + epsilon)
    query_r, key_r = r_both[0][:, None], r_both[1][:, None]
    frequency = jnp.exp(
        jnp.arange(HEAD_DIM // 2, dtype=f32) * (-2.0 * math.log(rope_base) / HEAD_DIM)
    )
    angles = places.astype(f32)[:, None] * frequency[None, :]
    cosine, sine = jnp.cos(angles), jnp.sin(angles)
    cosine, sine = jnp.concatenate([cosine, cosine], 1), jnp.concatenate([-sine, sine], 1)
    stats = after(r_both.T, came[1][1:4:2])
    scales = jnp.stack(
        [query_scale.reshape(heads, HEAD_DIM), key_scale.reshape(heads, HEAD_DIM)], axis=1
    )
    attended, query, keyv, log_total = attend(
        projected, stats, scales, cosine, sine, places, heads
    )
    branch = dot(attended, w_out, ((1,), (0,))).astype(bf16)
    weights = [whole_expert(*after(fetched, branch))]
    branch = after(branch, fetched)
    branch_own = scatter_xor(jnp.split(branch, n_ctx, axis=0), "context", n_ctx, 0)
    fetched, came = zip(*(fetch_expert(e, branch_own) for e in range(1, EXP_DEV)))
    middle = own_rows.astype(f32) + branch_own
    middle_r = inverse_rms(middle)
    mixed_own = (middle * middle_r * moe_scale).astype(bf16)

    own_probs = jax.nn.softmax(dot(mixed_own, router_full, ((1,), (0,)))[:, :experts], axis=-1)
    probs_high = own_probs.astype(bf16)
    probs_low = (own_probs - probs_high.astype(f32)).astype(bf16)
    beside = jnp.concatenate([probs_high, probs_low, named.astype(bf16)], axis=1)
    beside = jnp.pad(beside, ((0, 0), (0, EXTRA - beside.shape[1])))
    mixed_own = jnp.concatenate([xor_blocks(mixed_own, own_ctx, n_ctx, 1), beside], axis=1)
    mixed_wide = lax.all_gather(after(mixed_own, pull), "expert", axis=0, tiled=True)
    mixed_wide = after(mixed_wide, [(more[0], more[1][:4]) for more in came])
    mixed, beside = mixed_wide[:, :width], mixed_wide[:, width:].astype(f32)
    router_x = xor_blocks(router_full, own_ctx, n_ctx, 0)
    router_probs = beside[:, :experts] + beside[:, experts : 2 * experts]
    named_all = beside[:, 2 * experts : 3 * experts]
    local = own_exp * EXP_DEV
    gates = lax.dynamic_slice_in_dim(router_probs * named_all, local, EXP_DEV, 1)
    acts = [run_experts(mixed_wide, pull, gates, *weights[0], 0)]
    for e in range(1, EXP_DEV):
        weights.append(whole_expert(*after(fetched[e - 1], acts)))
        acts.append(run_experts(after(mixed_wide, acts), pull, gates, *weights[e], e))
    hidden_g, d_acts, d_gates = zip(*acts)
    ff = weights[0][0].shape[1]

    slots = jnp.arange(experts, dtype=jnp.int32)[None, :]
    drp = sum(
        jnp.where(slots == local + e, d_gates[e] * named_all, 0.0) for e in range(EXP_DEV)
    )
    d_logits = (
        router_probs * (drp - jnp.sum(router_probs * drp, axis=-1, keepdims=True))
    ).astype(bf16)
    d_logits = jnp.pad(d_logits, ((0, 0), (0, EXTRA - experts)))

    d_mixed_part = rows_back(d_acts, d_logits, [w[0] for w in weights], [w[1] for w in weights], router_x)
    d_mixed = lax.psum_scatter(d_mixed_part, "expert", scatter_dimension=0, tiled=True).astype(f32)
    d_mixed = xor_blocks(d_mixed, own_ctx, n_ctx, 1)

    def weight_grads(e, hidden, grads):
        gate_g = dot(mixed, grads[:, :ff], ((0,), (0,))).astype(bf16)
        up_g = dot(mixed, grads[:, ff:], ((0,), (0,))).astype(bf16)
        down_g = xor_blocks(dot(hidden, pull, ((0,), (0,))).astype(bf16), own_ctx, n_ctx, 0)
        return gate_g, up_g, down_g

    def reduce_grads(gate_g, up_g, down_g):
        parts = n_ctx.bit_length() - 1
        cut = [slices(piece, parts, 0) for piece in jnp.split(down_g, n_ctx)]
        halves = [[own[j] for own in cut] for j in range(parts)]
        sums, came = scatter_many(
            [jnp.split(gate_g, n_ctx), jnp.split(up_g, n_ctx), *halves], "context", n_ctx
        )
        return (sums[0], sums[1], jnp.concatenate(sums[2:])), came

    g_first = weight_grads(0, *after((hidden_g[0], d_acts[0]), d_mixed_part))
    g_expert, came = reduce_grads(*g_first)
    g_experts = [g_expert]
    out_part = dot(after(hidden_g[0], g_first), weights[0][2], ((1,), (0,)))
    for e in range(1, EXP_DEV):
        out_part += dot(after(hidden_g[e], out_part, came[0][0:4:2]), weights[e][2], ((1,), (0,)))
    out_part = out_part.astype(bf16)
    out_own = lax.psum_scatter(out_part, "expert", scatter_dimension=0, tiled=True).astype(f32)
    d_mixed = after(d_mixed, came[0][1:4:2], out_part)
    g_router = xor_blocks(dot(mixed, d_logits, ((0,), (0,)))[:, :experts], own_ctx, n_ctx, 0)

    scaled = d_mixed * moe_scale
    g_moe = jnp.sum(d_mixed * middle * middle_r, axis=0)
    d_middle = (
        cotangent[0].astype(f32)
        + middle_r * scaled
        - middle * (middle_r**3 * jnp.mean(scaled * middle, axis=-1, keepdims=True))
    )
    d_branch = gather_xor(d_middle.astype(bf16), "context", n_ctx, 0)
    g_raw = [weight_grads(e, *after((hidden_g[e], d_acts[e]), d_middle)) for e in range(1, EXP_DEV)]
    d_branch = after(d_branch, g_raw, g_experts)
    came = []
    for raw in g_raw:
        g_expert, more = reduce_grads(*after(raw, d_branch))
        g_experts.append(g_expert)
        came.append(more)
    g_output = lax.psum_scatter(
        dot(attended, d_branch, ((0,), (0,))).astype(bf16), "expert", scatter_dimension=0, tiled=True
    ).astype(f32)

    d_attended = dot(d_branch, w_out, ((1,), (1,))).astype(bf16)
    d_query, d_key, d_value, inner_q, inner_k, g_heads = attend_back(
        projected, query, keyv, d_attended, log_total, stats, scales, cosine, sine, places, heads
    )
    result = (middle + after(out_own, d_query)).astype(bf16)
    inner_q, inner_k = jnp.sum(inner_q[:, :, 0], axis=0), jnp.sum(inner_k[:, :, 0], axis=0)
    inner_both = jnp.stack([inner_q, inner_k])
    inner_both = psum_rows(after(inner_both, [more[0][0:4:2] for more in came])) / width
    g_heads = g_heads.transpose(1, 0, 2).reshape(2, columns)
    d_query_p = query_r * (query_scale * d_query) - query_p * (query_r**3 * inner_both[0][:, None])
    d_key_p = key_r * (key_scale * d_key) - key_p * (key_r**3 * inner_both[1][:, None])
    d_projected = jnp.concatenate(
        [d_query_p.astype(bf16), d_key_p.astype(bf16), d_value], axis=1
    )
    d_projected = after(d_projected, [more[0][1:4:2] for more in came])
    d_normed_part = dot(d_projected, w_qkv, ((1,), (1,)))
    g_attn = jnp.sum(d_normed_part * inputs * input_r, axis=0)
    d_normed = after(d_normed_part.astype(bf16), [more[0] for more in came])
    d_normed = scatter_xor(jnp.split(d_normed, n_ctx, axis=0), "context", n_ctx, 0)
    own_in = own_rows.astype(f32)
    own_r = inverse_rms(own_in)
    scaled_in = d_normed * attn_scale
    input_grad = (
        d_middle
        + own_r * scaled_in
        - own_in * (own_r**3 * jnp.mean(scaled_in * own_in, axis=-1, keepdims=True))
    )

    g_qkv = dot(normed, d_projected, ((0,), (0,)))
    spread = jnp.zeros((2, width), f32)
    spread = lax.dynamic_update_slice(
        spread, g_heads, (jnp.zeros_like(own_ctx), own_ctx * columns)
    )
    g_small = jnp.concatenate([jnp.stack([g_attn, g_moe], axis=1), spread.T, g_router], axis=1)
    g_small = jnp.pad(g_small, ((0, 0), (0, EXTRA - g_small.shape[1])))
    g_packed = jnp.concatenate([g_qkv.astype(bf16), g_small.astype(bf16)], axis=1)
    g_packed = g_packed.reshape(n_ctx, n_exp, part, -1).transpose(1, 0, 2, 3).reshape(width, -1)
    g_packed = lax.psum_scatter(g_packed, "expert", scatter_dimension=0, tiled=True)
    g_packed = xor_blocks(g_packed.reshape(n_ctx, part, -1), own_ctx, n_ctx, 0)
    g_packed = jnp.stack(trade([g_packed[k] for k in range(n_ctx)])).astype(f32)
    g_packed = xor_blocks(g_packed, own_ctx, n_ctx, 0)
    g_weights = [
        g_packed[:, :, i * columns : (i + 1) * columns].transpose(1, 0, 2).reshape(part, width)
        for i in range(3)
    ]
    g_small = jnp.sum(g_packed[:, :, 3 * columns :], axis=0)
    return (
        result[None],
        input_grad[None],
        *g_weights,
        g_output,
        g_small[:, 4 : 4 + experts],
        g_small[:, 0],
        g_small[:, 2],
        g_small[:, 3],
        g_small[:, 1],
        *(jnp.stack([grads[i] for grads in g_experts]) for i in range(3)),
    )


def solution(mesh):
    rows = P("expert", "context", None)
    split = P(("context", "expert"), None)
    line = P(("context", "expert"))
    return jax.shard_map(
        shards,
        mesh=mesh,
        in_specs=(rows, P("expert", None), rows, rows) + (split,) * 5 + (line,) * 4 + (rows,) * 3,
        out_specs=(rows, rows) + (split,) * 5 + (line,) * 4 + (rows,) * 3,
        check_vma=False,
    )
```

time: 1290 us -> 962 us (0.75)
  waiting for transfers between devices: 510 us -> 274 us
  matrix products: 378 us -> 154 us
  Pallas kernels: 0 us -> 170 us
  other arithmetic: 151 us -> 97.6 us
  starting transfers between devices: 53.8 us -> 80.8 us
  blocking collectives: 51.6 us -> 34 us
    dot_general x23 -> x16, matrix products: 334 us -> 154 us  [dot(): lax.dot_general(left, right, (dims, ((), ())), preferred_element_type=f32)]
    pallas_call x0 -> x5, Pallas kernels: none -> 170 us  [the longest x2 75.6 us: run_experts(): pl.pallas_call(lambda *refs: experts_kernel(e, *refs), grid=(rows // bloc...]
    ppermute x60 -> x78, waiting for transfers between devices: 360 us -> 271 us  [swap(): return lax.ppermute(value, axis, [(i, i ^ bit) for i in range(count)])]
    reduce_scatter x1, waiting for transfers between devices: 87.3 us -> 0.01 us  [shards(): lax.psum_scatter(out_part, 'expert', scatter_dimension=0, tiled=True)]
    dot_general x6 -> x0, matrix products: 43.9 us -> none  [the longest x1 9.46 us: shards(): jnp.einsum('hqk,khd->qhd', (exponent / total).astype(bf16), value_h, pref...]
    convert_element_type x12 -> x13, other arithmetic: 51.6 us -> 17 us  [the longest x8 8.37 us: scatter_many(): new = swap(found.pop(place).astype(bf16), axis, count, bit)]
    reduce_scatter x1, waiting for transfers between devices: 33.5 us -> 0.01 us  [shards(): lax.psum_scatter(d_mixed_part, 'expert', scatter_dimension=0, tiled=True)]
    ppermute x60 -> x78, starting transfers between devices: 49.2 us -> 80 us  [swap(): return lax.ppermute(value, axis, [(i, i ^ bit) for i in range(count)])]
  transfers between devices with their start and end apart: 69 -> 86, of which waited for: 41 -> 34; matrix products, arithmetic and copies ran while one was open for 27% -> 34% of each run, Pallas kernels for 0% -> 9%
where the time goes in v2:
time: 962 us; the launch traced here: 952 us
  waiting for transfers between devices  274 us (28%)
  Pallas kernels  170 us (18%)
  matrix products  154 us (16%)
  local copies, waits for them, and re-layouts  125 us (13%)
  other arithmetic  97.6 us (10%)
  starting transfers between devices  80.8 us (8%)
  blocking collectives  34 us (4%)
  between operations  16.4 us (2%)
    ppermute x78, waiting for transfers between devices, swap(): return lax.ppermute(value, axis, [(i, i ^ bit) for i in range(count)])  271 us
    dot_general x16, matrix products, dot(): lax.dot_general(left, right, (dims, ((), ())), preferred_element_type=f32)  154 us
    ppermute x78, starting transfers between devices, swap(): return lax.ppermute(value, axis, [(i, i ^ bit) for i in range(count)])  80 us
    pallas_call x2, Pallas kernels, run_experts(): pl.pallas_call(lambda *refs: experts_kernel(e, *refs), grid=(rows // bloc...  75.6 us
    unnamed x218, local copies, waits for them, and re-layouts  53.1 us
    pallas_call x1, Pallas kernels, rows_back(): pl.pallas_call(lambda *refs: rows_back_kernel(count, *refs), grid=(width...  48.9 us
    psum x2, blocking collectives, psum_rows(): stats = lax.psum(xor_blocks(stats, own_ctx, n_ctx, 1), 'context')  34 us
    pallas_call x1, Pallas kernels, attend_back(): pl.pallas_call(lambda *refs: attend_back_kernel(min(256, rows), *refs), g...  29.3 us
  transfers between devices with their start and end apart: 86, of which 34 were waited for; matrix products, arithmetic and copies ran while one was open for 34% of the time, Pallas kernels for 9%

profile of v2, /device:TPU:0, one launch (start us, length us, event | category | flops | bytes accessed | tf_op | source)
XLA Modules:
  0.0 952.3 jit_solution(6402073972074949346)
XLA Ops:
  41.5 15.1 %collective-permute-done = bf16[128,2048]{1,0:T(8,128)(2,1)} collective-permute-done((bf16[128,2048]{1,0:T(8,128)(2,1)}, bf16[128,2048]{1,0:T(8,128)(2,1)}, u32[]{:S(2)}, u32[]{:S(2)}) %collective-permute-start) | collective-permute-done | bytes 524320 | tf_op jit(solution)/shard_map/ppermute | solution.py:38
  74.9 15.3 %collective-permute-done.5 = bf16[128,2048]{1,0:T(8,128)(2,1)S(1)} collective-permute-done((bf16[128,2048]{1,0:T(8,128)(2,1)}, bf16[128,2048]{1,0:T(8,128)(2,1)S(1)}, u32[]{:S(2)}, u32[]{:S(2)}) %collective-permute-start.5) | collective-permute-done | bytes 524320 | tf_op jit(solution)/shard_map/ppermute | solution.py:38
  94.8 10.6 %collective-permute-done.9 = bf16[128,2048]{1,0:T(8,128)(2,1)S(1)} collective-permute-done((bf16[128,2048]{1,0:T(8,128)(2,1)}, bf16[128,2048]{1,0:T(8,128)(2,1)S(1)}, u32[]{:S(2)}, u32[]{:S(2)}) %collective-permute-start.9) | collective-permute-done | bytes 524320 | tf_op jit(solution)/shard_map/ppermute | solution.py:38
  129.8 9.5 psum.14
  149.7 15.9 %collective-permute-done.15 = bf16[512,1024]{1,0:T(8,128)(2,1)} collective-permute-done((bf16[512,1024]{1,0:T(8,128)(2,1)}, bf16[512,1024]{1,0:T(8,128)(2,1)}, u32[]{:S(2)}, u32[]{:S(2)}) %collective-permute-start.15) | collective-permute-done | bytes 1048608 | tf_op jit(solution)/shard_map/ppermute | solution.py:38
  168.6 16.7 %attend.1 = (bf16[1024,512]{1,0:T(8,128)(2,1)}, bf16[1024,512]{1,0:T(8,128)(2,1)}, bf16[1024,512]{1,0:T(8,128)(2,1)}, f32[4,1024,1]{2,1,0:T(8,128)}) custom-call(f32[1024,1536]{1,0:T(8,128)} %copy-done, f32[1024,1536]{1,0:T(8,128)} %copy-done, f32[1024,1536]{1,0:T(8,128)} %copy-done, f32[1024,2]{1,0:T(8,128)} %get-tuple-element.91.refs_3_.refs_7_, ...), custom_call_target="tpu_custom_call" | custom-call | flops 2147483648 | bytes 6291456 | tf_op jit(solution)/shard_map/attend/pallas_call | solution.py:140
  192.3 11.9 %collective-permute-done.22 = bf16[128,2048]{1,0:T(8,128)(2,1)S(1)} collective-permute-done((bf16[128,2048]{1,0:T(8,128)(2,1)S(1)}, bf16[128,2048]{1,0:T(8,128)(2,1)S(1)}, u32[]{:S(2)}, u32[]{:S(2)}) %collective-permute-start.22) | collective-permute-done | bytes 524320 | tf_op jit(solution)/shard_map/ppermute | solution.py:38
  239.0 19.8 %collective-permute-done.27 = bf16[512,1024]{1,0:T(8,128)(2,1)} collective-permute-done((bf16[512,1024]{1,0:T(8,128)(2,1)S(1)}, bf16[512,1024]{1,0:T(8,128)(2,1)}, u32[]{:S(2)}, u32[]{:S(2)}) %collective-permute-start.27) | collective-permute-done | bytes 1048608 | tf_op jit(solution)/shard_map/ppermute | solution.py:38
  276.3 16.9 %collective-permute-done.30 = bf16[128,2048]{1,0:T(8,128)(2,1)} collective-permute-done((bf16[128,2048]{1,0:T(8,128)(2,1)S(1)}, bf16[128,2048]{1,0:T(8,128)(2,1)}, u32[]{:S(2)}, u32[]{:S(2)}) %collective-permute-start.30) | collective-permute-done | bytes 524320 | tf_op jit(solution)/shard_map/ppermute | solution.py:38
  300.5 10.7 %collective-permute-done.29 = bf16[128,2048]{1,0:T(8,128)(2,1)} collective-permute-done((bf16[128,2048]{1,0:T(8,128)(2,1)}, bf16[128,2048]{1,0:T(8,128)(2,1)}, u32[]{:S(2)}, u32[]{:S(2)}) %collective-permute-start.29) | collective-permute-done | bytes 524320 | tf_op jit(solution)/shard_map/ppermute | solution.py:38
  321.3 37.8 %expert.2 = (bf16[2048,1024]{1,0:T(8,128)(2,1)}, bf16[2048,2048]{1,0:T(8,128)(2,1)}, f32[2048,1]{1,0:T(8,128)}) custom-call(bf16[2048,2176]{1,0:T(8,128)(2,1)} %all-gather.10.cloned.1.call-done.refs_0_, bf16[2048,2048]{1,0:T(8,128)(2,1)} %all-gather.8.cloned.1.call-done.refs_1_, f32[2048,2]{1,0:T(8,128)} %dynamic-slice_multiply_fusion.refs_2_, ...), custom_call_target="tpu_custom_call" | custom-call | flops 25769803776 | bytes 41943040 | tf_op jit(solution)/shard_map/expert/pallas_call | solution.py:252
  384.3 37.9 %expert.3 = (bf16[2048,1024]{1,0:T(8,128)(2,1)}, bf16[2048,2048]{1,0:T(8,128)(2,1)}, f32[2048,1]{1,0:T(8,128)}) custom-call(bf16[2048,2176]{1,0:T(8,128)(2,1)} %all-gather.10.cloned.1.call-done.refs_0_, bf16[2048,2048]{1,0:T(8,128)(2,1)} %all-gather.8.cloned.1.call-done.refs_1_, f32[2048,2]{1,0:T(8,128)} %dynamic-slice_multiply_fusion.refs_2_, ...), custom_call_target="tpu_custom_call" | custom-call | flops 25769803776 | bytes 41943040 | tf_op jit(solution)/shard_map/expert/pallas_call | solution.py:252
  427.3 48.9 %rows_back.1 = bf16[2048,2048]{1,0:T(8,128)(2,1)} custom-call(bf16[2048,2048]{1,0:T(8,128)(2,1)} %get-tuple-element.139.refs_0_, bf16[2048,2048]{1,0:T(8,128)(2,1)} %get-tuple-element.146.refs_1_, bf16[2048,1024]{1,0:T(8,128)(2,1)} %copy-done.57, bf16[2048,1024]{1,0:T(8,128)(2,1)} %copy-done.56, bf16[2048,1024]{1,0:T(8,128)(2,1)} %copy-done.55, ...), custom_call_target="tpu_custom_call" | custom-call | flops 34359738368 | bytes 92274688 | tf_op jit(solution)/shard_map/rows_back/pallas_call | solution.py:289
  477.3 13.0 %fusion.23 = bf16[2048,1024]{1,0:T(8,128)(2,1)S(1)} fusion(bf16[2048,2048]{1,0:T(8,128)(2,1)} %get-tuple-element.139.refs_0_, bf16[2048,2176]{1,0:T(8,128)(2,1)} %all-gather.10.cloned.1.call-done.refs_0_), kind=kOutput, calls=%fused_computation.31 | convolution fusion | flops 8592031744 | bytes 16777216 | tf_op jit(solution)/shard_map/dot_general | solution.py:24
  490.3 12.3 %fusion.18 = bf16[2048,1024]{1,0:T(8,128)(2,1)S(1)} fusion(bf16[2048,2048]{1,0:T(8,128)(2,1)} %get-tuple-element.139.refs_0_, bf16[2048,2176]{1,0:T(8,128)(2,1)S(1)} %bitcast.156), kind=kOutput, calls=%fused_computation.30 | convolution fusion | flops 8592031744 | bytes 16777216 | tf_op jit(solution)/shard_map/dot_general | solution.py:24
  509.1 12.2 %fusion.74 = f32[2048,2048]{1,0:T(8,128)} fusion(bf16[2048,1024]{1,0:T(8,128)(2,1)S(1)} %copy-done.80, bf16[256,2048]{1,0:T(8,128)(2,1)S(1)} %copy-done.25, bf16[256,2048]{1,0:T(8,128)(2,1)S(1)} %copy-done.27, bf16[256,2048]{1,0:T(8,128)(2,1)S(1)} %copy-done.29, bf16[256,2048]{1,0:T(8,128)(2,1)S(1)} %copy-done.23), kind=kOutput, calls=%fused_computation.311 | convolution fusion | flops 8606711808 | bytes 25165824 | tf_op jit(solution)/shard_map/dot_general | solution.py:24
  536.1 16.6 %collective-permute-done.39 = bf16[512,1024]{1,0:T(8,128)(2,1)} collective-permute-done((bf16[512,1024]{1,0:T(8,128)(2,1)S(1)}, bf16[512,1024]{1,0:T(8,128)(2,1)}, u32[]{:S(2)}, u32[]{:S(2)}) %collective-permute-start.39) | collective-permute-done | bytes 1048608 | tf_op jit(solution)/shard_map/ppermute | solution.py:38
  555.9 15.8 %add_convert_fusion = bf16[2048,2048]{1,0:T(8,128)(2,1)} fusion(f32[2048,2048]{1,0:T(8,128)} %fusion.74, bf16[2048,1024]{1,0:T(8,128)(2,1)} %get-tuple-element.147, bf16[256,2048]{1,0:T(8,128)(2,1)S(1)} %copy-done.33, bf16[256,2048]{1,0:T(8,128)(2,1)S(1)} %copy-done.35, bf16[256,2048]{1,0:T(8,128)(2,1)S(1)} %copy-done.37, bf16[256,2048]{1,0:T(8,128)(2,1)S(1)} %copy-done.31), kind=kOutput, calls=%fused_computation | convolution fusion | flops 8615100416 | bytes 33554432 | tf_op jit(solution)/shard_map/dot_general | solution.py:24
  594.4 12.9 %fusion.33 = bf16[2048,1024]{1,0:T(8,128)(2,1)S(1)} fusion(bf16[2048,2048]{1,0:T(8,128)(2,1)} %get-tuple-element.146.refs_1_, bf16[2048,2176]{1,0:T(8,128)(2,1)} %all-gather.10.cloned.1.call-done.refs_0_), kind=kOutput, calls=%fused_computation.33 | convolution fusion | flops 8592031744 | bytes 16777216 | tf_op jit(solution)/shard_map/dot_general | solution.py:24
  607.4 14.3 %fusion.28 = bf16[2048,1024]{1,0:T(8,128)(2,1)S(1)} fusion(bf16[2048,2048]{1,0:T(8,128)(2,1)} %get-tuple-element.146.refs_1_, bf16[2048,2176]{1,0:T(8,128)(2,1)} %all-gather.10.cloned.1.call-done.refs_0_), kind=kOutput, calls=%fused_computation.32 | convolution fusion | flops 8592031744 | bytes 16777216 | tf_op jit(solution)/shard_map/dot_general | solution.py:24
  621.7 12.9 %convolution_convert_fusion.2 = bf16[1024,2048]{1,0:T(8,128)(2,1)S(1)} fusion(bf16[2048,1024]{1,0:T(8,128)(2,1)S(1)} %copy-done.81, bf16[2048,2048]{1,0:T(8,128)(2,1)} %all-gather.8.cloned.1.call-done.refs_1_), kind=kOutput, calls=%fused_computation.35 | convolution fusion | flops 8592031744 | bytes 16777216 | tf_op jit(solution)/shard_map/dot_general | solution.py:24
  640.6 10.2 %collective-permute-done.47 = bf16[128,2048]{1,0:T(8,128)(2,1)S(1)} collective-permute-done((bf16[128,2048]{1,0:T(8,128)(2,1)S(1)}, bf16[128,2048]{1,0:T(8,128)(2,1)S(1)}, u32[]{:S(2)}, u32[]{:S(2)}) %collective-permute-start.47) | collective-permute-done | bytes 524320 | tf_op jit(solution)/shard_map/ppermute | solution.py:38
  659.3 29.3 %attend_back.1 = (f32[1024,512]{1,0:T(8,128)}, f32[1024,512]{1,0:T(8,128)}, bf16[1024,512]{1,0:T(8,128)(2,1)}, f32[4,1024,1]{2,1,0:T(8,128)}, f32[4,1024,1]{2,1,0:T(8,128)}, /*index=5*/f32[4,2,128]{2,1,0:T(2,128)}) custom-call(f32[1024,1536]{1,0:T(8,128)} %copy-done, f32[1024,1536]{1,0:T(8,128)} %copy-done, f32[1024,1536]{1,0:T(8,128)} %copy-done, ...), custom_call_target="tpu_custom_call" | custom-call | flops 5368709120 | bytes 15728640 | tf_op jit(solution)/shard_map/attend_back/pallas_call | solution.py:202
  694.6 24.5 %psum.15 = f32[2,1024]{1,0:T(2,128)S(1)} all-reduce(f32[2,1024]{1,0:T(2,128)S(1)} %pad_maximum_fusion.22), channel_id=1, replica_groups=mesh['context'=4,'expert'=8] {'context'}, use_global_device_ids=true, to_apply=%region_15.16 | all-reduce | flops 2048 | bytes 16384 | tf_op jit(solution)/shard_map/psum | solution.py:341
  725.5 11.2 %multiply_reduce_fusion = (bf16[2048]{0:T(1024)(128)(2,1)S(1)}, bf16[1024,2048]{1,0:T(8,128)(2,1)}) fusion(f32[1024,2048]{1,0:T(8,128)S(1)} %bitcast.132, f32[1024]{0:T(1024)S(1)} %copy-done.76, bf16[1024,1536]{1,0:T(8,128)(2,1)S(1)} %pad_maximum_fusion.7, bf16[2048,1664]{1,0:T(8,128)(2,1)} %bitcast.138), kind=kOutput, calls=%fused_computation.1 | convolution fusion | flops 6450837504 | bytes 22028288 | tf_op jit(solution)/shard_map/dot_general | solution.py:24
  736.8 9.9 %convolution_convert_fusion = bf16[2048,1536]{0,1:T(8,128)(2,1)} fusion(bf16[1024,1536]{1,0:T(8,128)(2,1)S(1)} %pad_maximum_fusion.7, f32[1024,2048]{1,0:T(8,128)S(1)} %bitcast.132, f32[2048]{0:T(1024)S(1)} %copy-done.61, f32[1024]{0:T(1024)S(1)} %copy-done.76), kind=kOutput, calls=%fused_computation.4 | convolution fusion | flops 6451888128 | bytes 17838080 | tf_op jit(solution)/shard_map/dot_general | solution.py:24
  753.6 9.8 %copy.161 = bf16[2048,1664]{1,0:T(8,128)(2,1)} copy(bf16[2048,1664]{0,1:T(8,128)(2,1)} %pad_maximum_fusion) | data formatting | bytes 13631488 | tf_op jit(solution)/shard_map/concatenate | solution.py:535
  769.8 13.0 %convolution_convert_fusion.1 = bf16[1024,2048]{1,0:T(8,128)(2,1)S(1)} fusion(bf16[2048,1024]{1,0:T(8,128)(2,1)} %get-tuple-element.148, bf16[2048,2048]{1,0:T(8,128)(2,1)} %all-gather.8.cloned.1.call-done.refs_1_), kind=kOutput, calls=%fused_computation.34 | convolution fusion | flops 8592031744 | bytes 16777216 | tf_op jit(solution)/shard_map/dot_general | solution.py:24
  786.5 11.6 %collective-permute-done.52 = bf16[128,2048]{1,0:T(8,128)(2,1)S(1)} collective-permute-done((bf16[128,2048]{1,0:T(8,128)(2,1)S(1)}, bf16[128,2048]{1,0:T(8,128)(2,1)S(1)}, u32[]{:S(2)}, u32[]{:S(2)}) %collective-permute-start.52) | collective-permute-done | bytes 524320 | tf_op jit(solution)/shard_map/ppermute | solution.py:38
  851.6 11.5 %collective-permute-done.76 = bf16[128,2048]{1,0:T(8,128)(2,1)S(1)} collective-permute-done((bf16[128,2048]{1,0:T(8,128)(2,1)S(1)}, bf16[128,2048]{1,0:T(8,128)(2,1)S(1)}, u32[]{:S(2)}, u32[]{:S(2)}) %collective-permute-start.76) | collective-permute-done | bytes 524320 | tf_op jit(solution)/shard_map/ppermute | solution.py:38
  873.1 17.1 %collective-permute-done.66 = bf16[128,2048]{1,0:T(8,128)(2,1)S(1)} collective-permute-done((bf16[128,2048]{1,0:T(8,128)(2,1)S(1)}, bf16[128,2048]{1,0:T(8,128)(2,1)S(1)}, u32[]{:S(2)}, u32[]{:S(2)}) %collective-permute-start.66) | collective-permute-done | bytes 524320 | tf_op jit(solution)/shard_map/ppermute | solution.py:38
  896.1 20.6 %collective-permute-done.65 = bf16[128,2048]{1,0:T(8,128)(2,1)S(1)} collective-permute-done((bf16[128,2048]{1,0:T(8,128)(2,1)S(1)}, bf16[128,2048]{1,0:T(8,128)(2,1)S(1)}, u32[]{:S(2)}, u32[]{:S(2)}) %collective-permute-start.65) | collective-permute-done | bytes 524320 | tf_op jit(solution)/shard_map/ppermute | solution.py:38
  (541 shorter events, 390.7 us)
Async XLA Ops:
  7.2 100.2 %all-gather.12.cloned.1.call-start = ((), (), s32[]{:S(2)}) async-start(), calls=%async_computation.11 | async-start | bytes 7667712 | tf_op jit(solution)/shard_map/all_gather | solution.py:358
  27.5 157.8 %all-gather.6.cloned.1.call-start = ((), (), s32[]{:S(2)}) async-start(), calls=%async_computation.4 | async-start | bytes 2359296 | tf_op jit(solution)/shard_map/all_gather | solution.py:373
  34.4 71.5 %collective-permute-start.6 = (bf16[512,1024]{1,0:T(8,128)(2,1)S(1)}, bf16[512,1024]{1,0:T(8,128)(2,1)}, u32[]{:S(2)}, u32[]{:S(2)}) collective-permute-start(bf16[512,1024]{1,0:T(8,128)(2,1)S(1)} %get-tuple-element.101), channel_id=1, source_target_pairs={{0,8},{8,0},{16,24},{24,16},{1,9},{9,1},{17,25},{25,17},{2,10},{10... | collective-permute-start | bytes 3145736 | tf_op jit(solution)/shard_map/ppermute | solution.py:38
  59.0 47.7 %collective-permute-start.7 = (bf16[512,1024]{1,0:T(8,128)(2,1)}, bf16[512,1024]{1,0:T(8,128)(2,1)}, u32[]{:S(2)}, u32[]{:S(2)}) collective-permute-start(bf16[512,1024]{1,0:T(8,128)(2,1)} %get-tuple-element.105), channel_id=1, source_target_pairs={{0,16},{8,24},{16,0},{24,8},{1,17},{9,25},{17,1},{25,9},{2,18},{10... | collective-permute-start | bytes 3145736 | tf_op jit(solution)/shard_map/ppermute | solution.py:38
  113.8 117.2 %all-gather.8.cloned.1.call-start = ((), (), s32[]{:S(2)}) async-start(), calls=%async_computation.5 | async-start | bytes 9437184 | tf_op jit(solution)/shard_map/all_gather | solution.py:396
  139.4 178.6 %all-gather.10.cloned.1.call-start = ((), (), s32[]{:S(2)}) async-start(), calls=%async_computation.6 | async-start | bytes 10027008 | tf_op jit(solution)/shard_map/all_gather | solution.py:427
  141.5 48.2 %collective-permute-start.19 = (bf16[128,2048]{1,0:T(8,128)(2,1)}, bf16[128,2048]{1,0:T(8,128)(2,1)}, u32[]{:S(2)}, u32[]{:S(2)}) collective-permute-start(bf16[128,2048]{1,0:T(8,128)(2,1)} %get-tuple-element.110), channel_id=1, source_target_pairs={{0,8},{8,0},{16,24},{24,16},{1,9},{9,1},{17,25},{25,17},{2,10},{10... | collective-permute-start | bytes 1572872 | tf_op jit(solution)/shard_map/ppermute | solution.py:38
  143.4 46.3 %collective-permute-start.17 = (bf16[128,2048]{1,0:T(8,128)(2,1)}, bf16[128,2048]{1,0:T(8,128)(2,1)}, u32[]{:S(2)}, u32[]{:S(2)}) collective-permute-start(bf16[128,2048]{1,0:T(8,128)(2,1)} %get-tuple-element.109), channel_id=1, source_target_pairs={{0,16},{8,24},{16,0},{24,8},{1,17},{9,25},{17,1},{25,9},{2,18},{10... | collective-permute-start | bytes 1572872 | tf_op jit(solution)/shard_map/ppermute | solution.py:38
  231.0 353.6 %reduce-scatter.7.cloned.1.call-start = ((), (), s32[]{:S(2)}) async-start(), calls=%async_computation.8 | async-start | bytes 9437184 | tf_op jit(solution)/shard_map/reduce_scatter | solution.py:452
  234.3 78.3 %collective-permute-start.31 = (bf16[512,1024]{1,0:T(8,128)(2,1)S(1)}, bf16[512,1024]{1,0:T(8,128)(2,1)}, u32[]{:S(2)}, u32[]{:S(2)}) collective-permute-start(bf16[512,1024]{1,0:T(8,128)(2,1)S(1)} %get-tuple-element.121), channel_id=1, source_target_pairs={{0,16},{8,24},{16,0},{24,8},{1,17},{9,25},{17,1},{25,9},{2,18},{10... | collective-permute-start | bytes 3145736 | tf_op jit(solution)/shard_map/ppermute | solution.py:38
  235.1 78.7 %collective-permute-start.33 = (bf16[512,1024]{1,0:T(8,128)(2,1)}, bf16[512,1024]{1,0:T(8,128)(2,1)}, u32[]{:S(2)}, u32[]{:S(2)}) collective-permute-start(bf16[512,1024]{1,0:T(8,128)(2,1)} %get-tuple-element.125), channel_id=1, source_target_pairs={{0,8},{8,0},{16,24},{24,16},{1,9},{9,1},{17,25},{25,17},{2,10},{10... | collective-permute-start | bytes 3145736 | tf_op jit(solution)/shard_map/ppermute | solution.py:38
  237.5 55.7 %collective-permute-start.30 = (bf16[128,2048]{1,0:T(8,128)(2,1)S(1)}, bf16[128,2048]{1,0:T(8,128)(2,1)}, u32[]{:S(2)}, u32[]{:S(2)}) collective-permute-start(bf16[128,2048]{1,0:T(8,128)(2,1)S(1)} %get-tuple-element.130), channel_id=1, source_target_pairs={{0,16},{8,24},{16,0},{24,8},{1,17},{9,25},{17,1},{25,9},{2,18},{10... | collective-permute-start | bytes 1572872 | tf_op jit(solution)/shard_map/ppermute | solution.py:38
  258.7 55.9 %collective-permute-start.32 = (bf16[512,1024]{1,0:T(8,128)(2,1)}, bf16[512,1024]{1,0:T(8,128)(2,1)}, u32[]{:S(2)}, u32[]{:S(2)}) collective-permute-start(bf16[512,1024]{1,0:T(8,128)(2,1)} %collective-permute-done.27), channel_id=1, source_target_pairs={{0,16},{8,24},{16,0},{24,8},{1,17},{9,25},{17,1},{25,9},{2,18},{10... | collective-permute-start | bytes 3145736 | tf_op jit(solution)/shard_map/ppermute | solution.py:38
  260.2 55.1 %collective-permute-start.34 = (bf16[512,1024]{1,0:T(8,128)(2,1)}, bf16[512,1024]{1,0:T(8,128)(2,1)}, u32[]{:S(2)}, u32[]{:S(2)}) collective-permute-start(bf16[512,1024]{1,0:T(8,128)(2,1)} %collective-permute-done.28), channel_id=1, source_target_pairs={{0,8},{8,0},{16,24},{24,16},{1,9},{9,1},{17,25},{25,17},{2,10},{10... | collective-permute-start | bytes 3145736 | tf_op jit(solution)/shard_map/ppermute | solution.py:38
  311.3 47.9 %collective-permute-start.37 = (bf16[128,2048]{1,0:T(8,128)(2,1)S(1)}, bf16[128,2048]{1,0:T(8,128)(2,1)}, u32[]{:S(2)}, u32[]{:S(2)}) collective-permute-start(bf16[128,2048]{1,0:T(8,128)(2,1)S(1)} %get-tuple-element.130), channel_id=1, source_target_pairs={{0,8},{8,0},{16,24},{24,16},{1,9},{9,1},{17,25},{25,17},{2,10},{10... | collective-permute-start | bytes 1572872 | tf_op jit(solution)/shard_map/ppermute | solution.py:38
  312.5 46.6 %collective-permute-start.35 = (bf16[128,2048]{1,0:T(8,128)(2,1)}, bf16[128,2048]{1,0:T(8,128)(2,1)}, u32[]{:S(2)}, u32[]{:S(2)}) collective-permute-start(bf16[128,2048]{1,0:T(8,128)(2,1)} %get-tuple-element.129), channel_id=1, source_target_pairs={{0,16},{8,24},{16,0},{24,8},{1,17},{9,25},{17,1},{25,9},{2,18},{10... | collective-permute-start | bytes 1572872 | tf_op jit(solution)/shard_map/ppermute | solution.py:38
  313.8 45.4 %collective-permute-start.38 = (bf16[128,2048]{1,0:T(8,128)(2,1)}, bf16[128,2048]{1,0:T(8,128)(2,1)}, u32[]{:S(2)}, u32[]{:S(2)}) collective-permute-start(bf16[128,2048]{1,0:T(8,128)(2,1)} %collective-permute-done.30), channel_id=1, source_target_pairs={{0,8},{8,0},{16,24},{24,16},{1,9},{9,1},{17,25},{25,17},{2,10},{10... | collective-permute-start | bytes 1572872 | tf_op jit(solution)/shard_map/ppermute | solution.py:38
  314.6 44.5 %collective-permute-start.36 = (bf16[128,2048]{1,0:T(8,128)(2,1)}, bf16[128,2048]{1,0:T(8,128)(2,1)}, u32[]{:S(2)}, u32[]{:S(2)}) collective-permute-start(bf16[128,2048]{1,0:T(8,128)(2,1)} %collective-permute-done.29), channel_id=1, source_target_pairs={{0,16},{8,24},{16,0},{24,8},{1,17},{9,25},{17,1},{25,9},{2,18},{10... | collective-permute-start | bytes 1572872 | tf_op jit(solution)/shard_map/ppermute | solution.py:38
  476.1 351.9 %reduce-scatter.5.cloned.1.call-start = ((), (), s32[]{:S(2)}) async-start(), calls=%async_computation.7 | async-start | bytes 9437184 | tf_op jit(solution)/shard_map/reduce_scatter | solution.py:477
  505.2 47.4 %collective-permute-start.39 = (bf16[512,1024]{1,0:T(8,128)(2,1)S(1)}, bf16[512,1024]{1,0:T(8,128)(2,1)}, u32[]{:S(2)}, u32[]{:S(2)}) collective-permute-start(bf16[512,1024]{1,0:T(8,128)(2,1)S(1)} %get-tuple-element.288), channel_id=1, source_target_pairs={{0,16},{8,24},{16,0},{24,8},{1,17},{9,25},{17,1},{25,9},{2,18},{10... | collective-permute-start | bytes 3145736 | tf_op jit(solution)/shard_map/ppermute | solution.py:38
  508.4 47.5 %collective-permute-start.40 = (bf16[512,1024]{1,0:T(8,128)(2,1)S(1)}, bf16[512,1024]{1,0:T(8,128)(2,1)}, u32[]{:S(2)}, u32[]{:S(2)}) collective-permute-start(bf16[512,1024]{1,0:T(8,128)(2,1)S(1)} %get-tuple-element.286), channel_id=1, source_target_pairs={{0,8},{8,0},{16,24},{24,16},{1,9},{9,1},{17,25},{25,17},{2,10},{10... | collective-permute-start | bytes 3145736 | tf_op jit(solution)/shard_map/ppermute | solution.py:38
  531.4 45.5 %collective-permute-start.49 = (bf16[512,1024]{1,0:T(8,128)(2,1)}, bf16[512,1024]{1,0:T(8,128)(2,1)}, u32[]{:S(2)}, u32[]{:S(2)}) collective-permute-start(bf16[512,1024]{1,0:T(8,128)(2,1)} %add_convert_fusion.5), channel_id=1, source_target_pairs={{0,8},{8,0},{16,24},{24,16},{1,9},{9,1},{17,25},{25,17},{2,10},{10... | collective-permute-start | bytes 3145736 | tf_op jit(solution)/shard_map/ppermute | solution.py:38
  534.7 46.0 %collective-permute-start.50 = (bf16[512,1024]{1,0:T(8,128)(2,1)}, bf16[512,1024]{1,0:T(8,128)(2,1)}, u32[]{:S(2)}, u32[]{:S(2)}) collective-permute-start(bf16[512,1024]{1,0:T(8,128)(2,1)} %add_convert_fusion.4), channel_id=1, source_target_pairs={{0,16},{8,24},{16,0},{24,8},{1,17},{9,25},{17,1},{25,9},{2,18},{10... | collective-permute-start | bytes 3145736 | tf_op jit(solution)/shard_map/ppermute | solution.py:38
  571.8 356.0 %reduce-scatter.9.cloned.1.call-start = ((), (), s32[]{:S(2)}) async-start(), calls=%async_computation.9 | async-start | bytes 7667712 | tf_op jit(solution)/shard_map/reduce_scatter | solution.py:537
  590.3 47.0 %collective-permute-start.46 = (bf16[128,2048]{1,0:T(8,128)(2,1)S(1)}, bf16[128,2048]{1,0:T(8,128)(2,1)S(1)}, u32[]{:S(2)}, u32[]{:S(2)}) collective-permute-start(bf16[128,2048]{1,0:T(8,128)(2,1)S(1)} %get-tuple-element.320), channel_id=1, source_target_pairs={{0,16},{8,24},{16,0},{24,8},{1,17},{9,25},{17,1},{25,9},{2,18},{10... | collective-permute-start | bytes 1572872 | tf_op jit(solution)/shard_map/ppermute | solution.py:38
  591.9 48.5 %collective-permute-start.44 = (bf16[128,2048]{1,0:T(8,128)(2,1)S(1)}, bf16[128,2048]{1,0:T(8,128)(2,1)S(1)}, u32[]{:S(2)}, u32[]{:S(2)}) collective-permute-start(bf16[128,2048]{1,0:T(8,128)(2,1)S(1)} %get-tuple-element.320), channel_id=1, source_target_pairs={{0,8},{8,0},{16,24},{24,16},{1,9},{9,1},{17,25},{25,17},{2,10},{10... | collective-permute-start | bytes 1572872 | tf_op jit(solution)/shard_map/ppermute | solution.py:38
  593.4 47.1 %collective-permute-start.45 = (bf16[128,2048]{1,0:T(8,128)(2,1)S(1)}, bf16[128,2048]{1,0:T(8,128)(2,1)S(1)}, u32[]{:S(2)}, u32[]{:S(2)}) collective-permute-start(bf16[128,2048]{1,0:T(8,128)(2,1)S(1)} %get-tuple-element.321), channel_id=1, source_target_pairs={{0,16},{8,24},{16,0},{24,8},{1,17},{9,25},{17,1},{25,9},{2,18},{10... | collective-permute-start | bytes 1572872 | tf_op jit(solution)/shard_map/ppermute | solution.py:38
  593.9 45.0 %collective-permute-start.43 = (bf16[128,2048]{1,0:T(8,128)(2,1)S(1)}, bf16[128,2048]{1,0:T(8,128)(2,1)S(1)}, u32[]{:S(2)}, u32[]{:S(2)}) collective-permute-start(bf16[128,2048]{1,0:T(8,128)(2,1)S(1)} %get-tuple-element.321), channel_id=1, source_target_pairs={{0,8},{8,0},{16,24},{24,16},{1,9},{9,1},{17,25},{25,17},{2,10},{10... | collective-permute-start | bytes 1572872 | tf_op jit(solution)/shard_map/ppermute | solution.py:38
  769.8 166.9 %reduce-scatter.11.cloned.1.call-start = ((), (), s32[]{:S(2)}) async-start(), calls=%async_computation.10 | async-start | bytes 2359296 | tf_op jit(solution)/shard_map/reduce_scatter | solution.py:496
  869.0 49.9 %collective-permute-start.74 = (bf16[512,1024]{1,0:T(8,128)(2,1)S(1)}, bf16[512,1024]{1,0:T(8,128)(2,1)S(1)}, u32[]{:S(2)}, u32[]{:S(2)}) collective-permute-start(bf16[512,1024]{1,0:T(8,128)(2,1)S(1)} %add_convert_fusion.2), channel_id=1, source_target_pairs={{0,8},{8,0},{16,24},{24,16},{1,9},{9,1},{17,25},{25,17},{2,10},{10... | collective-permute-start | bytes 3145736 | tf_op jit(solution)/shard_map/ppermute | solution.py:38
  871.1 52.0 %collective-permute-start.75 = (bf16[512,1024]{1,0:T(8,128)(2,1)S(1)}, bf16[512,1024]{1,0:T(8,128)(2,1)S(1)}, u32[]{:S(2)}, u32[]{:S(2)}) collective-permute-start(bf16[512,1024]{1,0:T(8,128)(2,1)S(1)} %add_convert_fusion.1), channel_id=1, source_target_pairs={{0,16},{8,24},{16,0},{24,8},{1,17},{9,25},{17,1},{25,9},{2,18},{10... | collective-permute-start | bytes 3145736 | tf_op jit(solution)/shard_map/ppermute | solution.py:38
  872.2 44.5 %collective-permute-start.65 = (bf16[128,2048]{1,0:T(8,128)(2,1)S(1)}, bf16[128,2048]{1,0:T(8,128)(2,1)S(1)}, u32[]{:S(2)}, u32[]{:S(2)}) collective-permute-start(bf16[128,2048]{1,0:T(8,128)(2,1)S(1)} %get-tuple-element.269), channel_id=1, source_target_pairs={{0,16},{8,24},{16,0},{24,8},{1,17},{9,25},{17,1},{25,9},{2,18},{10... | collective-permute-start | bytes 1572872 | tf_op jit(solution)/shard_map/ppermute | solution.py:38
  (141 other events, 2527.3 us)
Sparse Core Ops, SparseCore 0:
  27.6 69.4 all-gather.11
  113.9 29.3 all-gather.5
  145.0 81.5 all-gather.7
  231.2 86.7 all-gather.9
  476.3 88.0 reduce-scatter.6
  571.9 87.8 reduce-scatter.4
  769.9 72.0 reduce-scatter.8
  844.3 33.9 reduce-scatter.10

commit v3 on v2

v3 whole, which is shorter than its diff:
```python
import math

import jax
import jax.numpy as jnp
from jax import lax
from jax.experimental import pallas as pl
from jax.experimental.pallas import tpu as pltpu
from jax.sharding import PartitionSpec as P

HEADS = 16
HEAD_DIM = 128
EXP_DEV = 2
EXTRA = 128
VMEM_BYTES = 56 * 1024 * 1024

epsilon = 1e-05
rope_base = 10000.0
masked_value = -1e30
bf16 = jnp.bfloat16
f32 = jnp.float32


def dot(left, right, dims):
    return lax.dot_general(left, right, (dims, ((), ())), preferred_element_type=f32)


def cuts(extent, parts):
    unit = 16 if extent % 16 == 0 and extent // 16 >= parts else 1
    units = extent // unit
    sizes = [(units // parts + (1 if i < units % parts else 0)) * unit for i in range(parts)]
    points = [0]
    for size in sizes:
        points.append(points[-1] + size)
    return points


def swap(value, axis, count, bit):
    return lax.ppermute(value, axis, [(i, i ^ bit) for i in range(count)])


def after(value, *others):
    return lax.optimization_barrier((value, others))[0]


def gather_direct(shard, axis, count):
    return [shard] + [swap(shard, axis, count, k) for k in range(1, count)]


def gather_step(state, axis, count, *first):
    steps = count.bit_length() - 1
    came = []
    for index, (arrays, found) in enumerate(state):
        bit = 1 << ((index + len(arrays) - 1) % steps)
        send = arrays[0] if len(arrays) == 1 else jnp.concatenate(arrays)
        new = swap(after(send, *first) if first else send, axis, count, bit)
        for block, place in enumerate(list(found)):
            found[place ^ bit] = (new, block)
        arrays.append(new)
        came.append(new)
    return came


def gather_start(shards):
    return [([shard], {0: (shard, 0)}) for shard in shards]


def gathered(state):
    return [
        [(*found[place], arrays[0].shape[0]) for place in range(len(found))] for arrays, found in state
    ]


def scatter_step(state, axis, count, step, *first):
    steps = count.bit_length() - 1
    sends = []
    for index, found in enumerate(state):
        bit = 1 << ((index + steps - 1 - step) % steps)
        away = [p for p in sorted(found) if p & bit]
        send = [found.pop(p).astype(bf16) for p in away]
        sends.append((bit, away, jnp.concatenate(send) if len(send) > 1 else send[0]))
    if first:
        held = after([send for _, _, send in sends], *first)
        sends = [(bit, away, send) for (bit, away, _), send in zip(sends, held)]
    came = [swap(send, axis, count, bit) for bit, _, send in sends]
    for found, (bit, away, _), new in zip(state, sends, came):
        rows = found[0].shape[0]
        for block, p in enumerate(away):
            part = lax.slice_in_dim(new, block * rows, (block + 1) * rows, axis=0)
            found[p ^ bit] = found[p ^ bit].astype(f32) + part.astype(f32)
    return came


def scatter_state(pieces):
    return [dict(enumerate(own)) for own in pieces]


def row_parts(pieces, parts):
    points = cuts(pieces[0].shape[0], parts)
    return [[piece[points[j] : points[j + 1]] for piece in pieces] for j in range(parts)]


def scatter_xor(pieces, axis, count):
    parts = count.bit_length() - 1
    state = scatter_state(row_parts(pieces, parts))
    came = ()
    for step in range(parts):
        came = scatter_step(state, axis, count, step, *came)
    return jnp.concatenate([found[0] for found in state])


def xor_blocks(value, own, count, dim):
    width = value.shape[dim] // count
    return jnp.concatenate(
        [lax.dynamic_slice_in_dim(value, (own ^ k) * width, width, dim) for k in range(count)], axis=dim
    )


def cost(flops, moved, exps=0):
    return pl.CostEstimate(flops=flops, bytes_accessed=moved, transcendentals=exps)


def params(steps):
    return pltpu.CompilerParams(
        dimension_semantics=("arbitrary",) * steps, vmem_limit_bytes=VMEM_BYTES
    )


def turn(values, cosine, sine):
    return values * cosine + pltpu.roll(values, HEAD_DIM // 2, 1) * sine


def project_kernel(columns, tokens, scale, gain, weights, projected, normed, squares):
    low = (tokens[...].astype(f32) * scale[...] * gain[...]).astype(bf16)
    normed[...] = low
    part = weights[...].reshape(low.shape[1], weights.shape[3])[:, : 3 * columns]
    new = dot(low, part, ((1,), (0,)))
    step = pl.program_id(0)

    @pl.when(step == 0)
    def _():
        projected[...] = new

    @pl.when(step > 0)
    def _():
        projected[...] += new

    @pl.when(step == pl.num_programs(0) - 1)
    def _():
        ones = jnp.ones((8, columns), bf16)
        for i in range(2):
            own = projected[:, i * columns : (i + 1) * columns]
            full = own * own
            high = full.astype(bf16)
            low = (full - high.astype(f32)).astype(bf16)
            total = dot(ones, high, ((1,), (1,))) + dot(ones, low, ((1,), (1,)))
            squares[i : i + 1] = total[0:1]


def project(tokens, scale, gain, packed, columns):
    rows, width = tokens.shape
    n_exp, n_ctx, part, wide = packed.shape
    cut = n_exp * part
    return pl.pallas_call(
        lambda *refs: project_kernel(columns, *refs),
        grid=(n_ctx,),
        in_specs=[
            pl.BlockSpec((rows, cut), lambda c: (0, c)),
            pl.BlockSpec((rows, 1), lambda c: (0, 0)),
            pl.BlockSpec((1, cut), lambda c: (0, c)),
            pl.BlockSpec((n_exp, 1, part, wide), lambda c: (0, c, 0, 0)),
        ],
        out_specs=[
            pl.BlockSpec((rows, 3 * columns), lambda c: (0, 0)),
            pl.BlockSpec((rows, cut), lambda c: (0, c)),
            pl.BlockSpec((2, rows), lambda c: (0, 0)),
        ],
        out_shape=[
            jax.ShapeDtypeStruct((rows, 3 * columns), f32),
            jax.ShapeDtypeStruct((rows, width), bf16),
            jax.ShapeDtypeStruct((2, rows), f32),
        ],
        compiler_params=params(1),
        cost_estimate=cost(6 * rows * width * columns, 4 * rows * width + 2 * packed.size + 12 * rows * columns),
        name="project",
    )(tokens, scale, gain, packed)


def side_grads_kernel(columns, normed, d_value, attended, d_branch, out):
    shape = (*out.shape[:3], columns)
    grad = dot(normed[...], d_value[...], ((0,), (0,))).astype(bf16)
    out[:, :, :, :columns] = grad.reshape(shape)
    grad = dot(attended[...], d_branch[...], ((0,), (0,))).astype(bf16)
    out[:, :, :, columns:] = grad.reshape(shape)


def side_grads(normed, d_value, attended, d_branch, n_exp, n_ctx):
    rows, width = normed.shape
    columns, cut = d_value.shape[1], width // n_ctx
    part = cut // n_exp
    here = pl.BlockSpec((rows, cut), lambda c: (0, c))
    whole = pl.BlockSpec((rows, columns), lambda c: (0, 0))
    return pl.pallas_call(
        lambda *refs: side_grads_kernel(columns, *refs),
        grid=(n_ctx,),
        in_specs=[here, whole, whole, here],
        out_specs=pl.BlockSpec((n_exp, 1, part, 2 * columns), lambda c: (0, c, 0, 0)),
        out_shape=jax.ShapeDtypeStruct((n_exp, n_ctx, part, 2 * columns), bf16),
        compiler_params=params(1),
        cost_estimate=cost(4 * rows * width * columns, 6 * rows * width),
        name="side_grads",
    )(normed, d_value, attended, d_branch)


def project_back_kernel(columns, d_projected, weights, tokens, scale, normed, beside, d_normed, out):
    part = weights[...].reshape(normed.shape[1], weights.shape[3])[:, : 3 * columns]
    grad = dot(d_projected[...], part, ((1,), (1,)))
    d_normed[...] = grad.astype(bf16)
    moved = (grad * tokens[...].astype(f32) * scale[...]).astype(bf16)
    gain = dot(moved, jnp.ones((moved.shape[0], EXTRA), bf16), ((0,), (0,)))
    small = jnp.where(lax.broadcasted_iota(jnp.int32, gain.shape, 1) == 0, gain, beside[...])
    grads = dot(normed[...], d_projected[:, : 2 * columns], ((0,), (0,)))
    shape = out.shape[:3]
    out[:, :, :, : 2 * columns] = grads.astype(bf16).reshape(*shape, 2 * columns)
    out[:, :, :, 2 * columns :] = small.astype(bf16).reshape(*shape, EXTRA)


def project_back(d_projected, packed, tokens, scale, normed, beside):
    rows, width = normed.shape
    n_exp, n_ctx, part, wide = packed.shape
    columns, cut = d_projected.shape[1] // 3, n_exp * part
    here = pl.BlockSpec((rows, cut), lambda c: (0, c))
    return pl.pallas_call(
        lambda *refs: project_back_kernel(columns, *refs),
        grid=(n_ctx,),
        in_specs=[
            pl.BlockSpec((rows, 3 * columns), lambda c: (0, 0)),
            pl.BlockSpec((n_exp, 1, part, wide), lambda c: (0, c, 0, 0)),
            here,
            pl.BlockSpec((rows, 1), lambda c: (0, 0)),
            here,
            pl.BlockSpec((cut, EXTRA), lambda c: (c, 0)),
        ],
        out_specs=[
            here,
            pl.BlockSpec((n_exp, 1, part, 2 * columns + EXTRA), lambda c: (0, c, 0, 0)),
        ],
        out_shape=[
            jax.ShapeDtypeStruct((rows, width), bf16),
            jax.ShapeDtypeStruct((n_exp, n_ctx, part, 2 * columns + EXTRA), bf16),
        ],
        compiler_params=params(1),
        cost_estimate=cost(10 * rows * width * columns, 8 * rows * width + 4 * packed.size),
        name="project_back",
    )(d_projected, packed, tokens, scale, normed, beside)


def attend_kernel(
    chunk, query_p, key_p, value, stats, scale, cosine, sine, place_col, place_row,
    attended, query_out, key_out, log_total,
):
    cos, sin = cosine[...], sine[...]
    scales = scale[0]
    query = turn(query_p[...] * stats[:, 0:1] * scales[0:1], cos, sin).astype(bf16)
    keyv = turn(key_p[...] * stats[:, 1:2] * scales[1:2], cos, sin).astype(bf16)
    query_out[...] = query
    key_out[...] = keyv
    values = value[...].astype(bf16)
    for start in range(0, query_p.shape[0], chunk):
        rows = slice(start, start + chunk)
        scores = dot(query[rows], keyv, ((1,), (1,))) * HEAD_DIM ** (-0.5)
        scores = jnp.where(place_row[...] <= place_col[rows], scores, masked_value)
        peak = jnp.max(scores, axis=1, keepdims=True)
        exponent = jnp.exp(scores - peak)
        total = jnp.sum(exponent, axis=1, keepdims=True)
        weights = (exponent * (1.0 / total)).astype(bf16)
        attended[rows] = dot(weights, values, ((1,), (0,))).astype(bf16)
        log_total[0, rows] = peak + jnp.log(total)


def attend(projected, stats, scales, cosine, sine, places, heads):
    rows = projected.shape[0]
    head = lambda offset: pl.BlockSpec((rows, HEAD_DIM), lambda h: (0, offset + h))
    whole = lambda shape: pl.BlockSpec(shape, lambda h: (0,) * len(shape))
    low = jax.ShapeDtypeStruct((rows, heads * HEAD_DIM), bf16)
    return pl.pallas_call(
        lambda *refs: attend_kernel(min(256, rows), *refs),
        grid=(heads,),
        in_specs=[
            head(0), head(heads), head(2 * heads),
            whole((rows, 2)),
            pl.BlockSpec((1, 2, HEAD_DIM), lambda h: (h, 0, 0)),
            whole((rows, HEAD_DIM)), whole((rows, HEAD_DIM)),
            whole((rows, 1)), whole((1, rows)),
        ],
        out_specs=[head(0), head(0), head(0), pl.BlockSpec((1, rows, 1), lambda h: (h, 0, 0))],
        out_shape=[low, low, low, jax.ShapeDtypeStruct((heads, rows, 1), f32)],
        compiler_params=params(1),
        cost_estimate=cost(4 * heads * rows * rows * HEAD_DIM, 24 * low.size // 2, heads * rows * rows),
        name="attend",
    )(projected, projected, projected, stats, scales, cosine, sine, places[:, None], places[None, :])


def attend_back_kernel(
    chunk, query_p, key_p, value, query, keyv, d_attended, log_total, stats, scale, cosine, sine,
    place_col, place_row, d_query, d_key, d_value, inner_q, inner_k, gains,
):
    values = value[...].astype(bf16)
    keys = keyv[...]
    for start in range(0, query_p.shape[0], chunk):
        rows = slice(start, start + chunk)
        queries, pull = query[rows], d_attended[rows]
        scores = dot(queries, keys, ((1,), (1,))) * HEAD_DIM ** (-0.5)
        scores = jnp.where(place_row[...] <= place_col[rows], scores, masked_value)
        probs = jnp.exp(scores - log_total[0, rows])
        d_probs = dot(pull, values, ((1,), (1,)))
        inner = jnp.sum(probs * d_probs, axis=1, keepdims=True)
        d_scores = (probs * (d_probs - inner)).astype(bf16)
        d_query[rows] = dot(d_scores, keys, ((1,), (0,)))
        more_key = dot(d_scores, queries, ((0,), (0,)))
        more_value = dot(probs.astype(bf16), pull, ((0,), (0,)))
        if start == 0:
            d_key[...] = more_key
            sums = more_value
        else:
            d_key[...] += more_key
            sums = sums + more_value
    d_value[...] = sums.astype(bf16)
    cos, sin = cosine[...], -sine[...]
    scales = scale[0]
    for index, (grad, before, inner_out) in enumerate(
        ((d_query, query_p, inner_q), (d_key, key_p, inner_k))
    ):
        back = turn(grad[...] * HEAD_DIM ** (-0.5), cos, sin)
        grad[...] = back
        moved = back * before[...]
        inner_out[0] = jnp.sum(moved * scales[index : index + 1], axis=1, keepdims=True)
        gains[0, index : index + 1] = jnp.sum(moved * stats[:, index : index + 1], axis=0, keepdims=True)


def attend_back(projected, query, keyv, d_attended, log_total, stats, scales, cosine, sine, places, heads):
    rows = projected.shape[0]
    head = lambda offset: pl.BlockSpec((rows, HEAD_DIM), lambda h: (0, offset + h))
    whole = lambda shape: pl.BlockSpec(shape, lambda h: (0,) * len(shape))
    column = pl.BlockSpec((1, rows, 1), lambda h: (h, 0, 0))
    pair = pl.BlockSpec((1, 2, HEAD_DIM), lambda h: (h, 0, 0))
    full = (rows, heads * HEAD_DIM)
    return pl.pallas_call(
        lambda *refs: attend_back_kernel(min(256, rows), *refs),
        grid=(heads,),
        in_specs=[
            head(0), head(heads), head(2 * heads), head(0), head(0), head(0),
            column, whole((rows, 2)), pair,
            whole((rows, HEAD_DIM)), whole((rows, HEAD_DIM)),
            whole((rows, 1)), whole((1, rows)),
        ],
        out_specs=[head(0), head(0), head(0), column, column, pair],
        out_shape=[
            jax.ShapeDtypeStruct(full, f32),
            jax.ShapeDtypeStruct(full, f32),
            jax.ShapeDtypeStruct(full, bf16),
            jax.ShapeDtypeStruct((heads, rows, 1), f32),
            jax.ShapeDtypeStruct((heads, rows, 1), f32),
            jax.ShapeDtypeStruct((heads, 2, HEAD_DIM), f32),
        ],
        compiler_params=params(1),
        cost_estimate=cost(0, 8 * rows * HEAD_DIM),
        name="attend_back",
    )(
        projected, projected, projected, query, keyv, d_attended, log_total, stats, scales,
        cosine, sine, places[:, None], places[None, :],
    )


def block_of(place):
    array, block, rows = place
    return pl.BlockSpec((rows, array.shape[1]), lambda i: (block, 0))


def pull_down_kernel(places, own, pull, *refs):
    down_w, (out, down) = refs[:-2], refs[-2:]

    @pl.when(pl.program_id(0) == 0)
    def _():
        for (k, unit, offset), part in zip(places, down_w):
            start = pl.multiple_of((own[0] ^ k) * unit + offset, 16)
            down[pl.ds(start, part.shape[0]), :] = part[...]

    out[...] = dot(pull[...], down[...], ((1,), (1,)))


def pull_down(own, pull, down_k):
    rows, width = pull.shape
    sizes = [part[0][2] for part in down_k]
    unit = sum(sizes)
    hidden = unit * len(down_k[0])
    places = [
        (k, unit, sum(sizes[:j])) for j in range(len(down_k)) for k in range(len(down_k[0]))
    ]
    flat = [place for part in down_k for place in part]
    block = min(512, rows)
    here = lambda n: pl.BlockSpec((block, n), lambda i: (i, 0))
    return pl.pallas_call(
        lambda *refs: pull_down_kernel(places, *refs),
        grid=(rows // block,),
        in_specs=[pl.BlockSpec(memory_space=pltpu.SMEM), here(width)] + [block_of(w) for w in flat],
        out_specs=[here(hidden), pl.BlockSpec((hidden, width), lambda i: (0, 0))],
        out_shape=[
            jax.ShapeDtypeStruct((rows, hidden), f32),
            jax.ShapeDtypeStruct((hidden, width), bf16),
        ],
        compiler_params=params(1),
        cost_estimate=cost(2 * rows * width * hidden, 2 * rows * width + 4 * width * hidden + 4 * rows * hidden),
        name="pull_down",
    )(own, pull, *[w[0] for w in flat])


def experts_kernel(e, n_ctx, mixed, back, gates, *refs):
    gate_w, up_w = refs[:n_ctx], refs[n_ctx : 2 * n_ctx]
    hidden_g, d_acts, d_gates = refs[2 * n_ctx :]
    depth, width = gate_w[0].shape
    gate = gates[:, e : e + 1]
    gate_act = up_act = 0.0
    for k in range(n_ctx):
        rows = mixed[:, k * depth : (k + 1) * depth]
        gate_act += dot(rows, gate_w[k][...], ((1,), (0,)))
        up_act += dot(rows, up_w[k][...], ((1,), (0,)))
    sig = jax.nn.sigmoid(gate_act)
    silu = gate_act * sig
    hidden = (silu * up_act).astype(bf16).astype(f32)
    d_gates[...] = jnp.sum(hidden * back[...], axis=1, keepdims=True)
    hidden_g[...] = (gate * hidden).astype(bf16)
    d_hidden = gate * back[...]
    d_acts[:, :width] = (d_hidden * up_act * sig * (1.0 + gate_act * (1.0 - sig))).astype(bf16)
    d_acts[:, width:] = (d_hidden * silu).astype(bf16)


def run_experts(mixed, back, gates, gate_k, up_k, e):
    rows, wide = mixed.shape
    hidden = back.shape[1]
    width = gate_k[0][2] * len(gate_k)
    block = min(256, rows)
    here = lambda n: pl.BlockSpec((block, n), lambda i: (i, 0))
    return pl.pallas_call(
        lambda *refs: experts_kernel(e, len(gate_k), *refs),
        grid=(rows // block,),
        in_specs=[here(wide), here(hidden), here(gates.shape[1])] + [block_of(w) for w in (*gate_k, *up_k)],
        out_specs=[here(hidden), here(2 * hidden), here(1)],
        out_shape=[
            jax.ShapeDtypeStruct((rows, hidden), bf16),
            jax.ShapeDtypeStruct((rows, 2 * hidden), bf16),
            jax.ShapeDtypeStruct((rows, 1), f32),
        ],
        compiler_params=params(1),
        cost_estimate=cost(
            4 * rows * width * hidden, 2 * (rows * width + 2 * width * hidden + 5 * rows * hidden), rows * hidden
        ),
        name="expert",
    )(mixed, back, gates, *[w[0] for w in (*gate_k, *up_k)])


def combine_kernel(count, *refs):
    total = dot(refs[0][...], refs[count][...], ((1,), (0,)))
    for e in range(1, count):
        total += dot(refs[e][...], refs[count + e][...], ((1,), (0,)))
    refs[-1][...] = total.astype(bf16)


def combine(hidden_g, down_w):
    count, (rows, hidden), width = len(hidden_g), hidden_g[0].shape, down_w[0].shape[1]
    block = min(512, rows)
    return pl.pallas_call(
        lambda *refs: combine_kernel(count, *refs),
        grid=(rows // block,),
        in_specs=[pl.BlockSpec((block, hidden), lambda i: (i, 0))] * count
        + [pl.BlockSpec((hidden, width), lambda i: (0, 0))] * count,
        out_specs=pl.BlockSpec((block, width), lambda i: (i, 0)),
        out_shape=jax.ShapeDtypeStruct((rows, width), bf16),
        compiler_params=params(1),
        cost_estimate=cost(2 * count * rows * width * hidden, 2 * count * hidden * (rows + width) + 2 * rows * width),
        name="combine",
    )(*hidden_g, *down_w)


def rows_back_kernel(count, n_ctx, *refs):
    d_acts, weights = refs[:count], refs[count : count * (1 + 2 * n_ctx)]
    d_logits, router, out = refs[count * (1 + 2 * n_ctx) :]
    depth, hidden = weights[0].shape
    for k in range(n_ctx):
        here = slice(k * depth, (k + 1) * depth)
        total = dot(d_logits[...], router[here], ((1,), (1,)))
        for e in range(count):
            for half in range(2):
                part = weights[(2 * e + half) * n_ctx + k]
                total += dot(d_acts[e][:, half * hidden : (half + 1) * hidden], part[...], ((1,), (1,)))
        out[:, here] = total.astype(bf16)


def rows_back(d_acts, d_logits, weights, router):
    rows = d_logits.shape[0]
    count, n_ctx = len(d_acts), len(weights[0][0])
    flat = [part for pair in weights for parts in pair for part in parts]
    depth, hidden = flat[0][2], flat[0][0].shape[1]
    block = min(512, rows)
    here = lambda n: pl.BlockSpec((block, n), lambda i: (i, 0))
    return pl.pallas_call(
        lambda *refs: rows_back_kernel(count, n_ctx, *refs),
        grid=(rows // block,),
        in_specs=[here(2 * hidden)] * count
        + [block_of(w) for w in flat]
        + [here(d_logits.shape[1]), pl.BlockSpec(router.shape, lambda i: (0, 0))],
        out_specs=here(n_ctx * depth),
        out_shape=jax.ShapeDtypeStruct((rows, n_ctx * depth), bf16),
        compiler_params=params(1),
        cost_estimate=cost(0, 8 * rows * HEAD_DIM),
        name="rows_back",
    )(*d_acts, *[w[0] for w in flat], d_logits, router)


def inverse_rms(values):
    return lax.rsqrt(jnp.mean(values * values, axis=-1, keepdims=True) + epsilon)


def shards(
    tokens_in,
    positions,
    routes,
    cotangent,
    w_query,
    w_key,
    w_value,
    w_output,
    router,
    attn_gain,
    query_gain,
    key_gain,
    moe_gain,
    expert_gate,
    expert_up,
    expert_down,
):
    n_ctx, n_exp = lax.axis_size("context"), lax.axis_size("expert")
    own_ctx, own_exp = lax.axis_index("context"), lax.axis_index("expert")
    own_rows = tokens_in[0]
    tokens, width = own_rows.shape
    sequence = positions.shape[1]
    experts = EXP_DEV * n_exp
    heads = HEADS // n_ctx
    columns = heads * HEAD_DIM
    part = w_query.shape[0]

    def sum_rows(stats):
        total = stats
        for k in range(1, n_ctx):
            came = jnp.split(swap(stats, "context", n_ctx, k), n_ctx, axis=1)
            total += jnp.concatenate([came[j ^ k] for j in range(n_ctx)], axis=1)
        return total

    small = jnp.concatenate(
        [attn_gain[:, None], moe_gain[:, None], query_gain[:, None], key_gain[:, None], router], axis=1
    )
    small = jnp.pad(small, ((0, 0), (0, EXTRA - small.shape[1])))

    def packed_for(owner):
        cut = [lax.dynamic_slice_in_dim(w, owner * columns, columns, 1) for w in (w_query, w_key, w_value)]
        return jnp.concatenate(cut + [small], axis=1)

    def trade(blocks):
        return [blocks[0]] + [swap(blocks[k], "context", n_ctx, k) for k in range(1, n_ctx)]

    packed = jnp.stack(trade([packed_for(own_ctx ^ k) for k in range(n_ctx)]))
    packed = xor_blocks(packed, own_ctx, n_ctx, 0)
    packed = lax.all_gather(packed, "expert", axis=0, tiled=False)
    small_full = packed[:, :, :, 3 * columns :].transpose(1, 0, 2, 3).reshape(width, EXTRA)
    small_rows = small_full[:, :4].T.astype(f32)
    attn_scale, moe_scale = small_rows[0], small_rows[1]
    query_scale = lax.dynamic_slice_in_dim(small_rows[2], own_ctx * columns, columns)
    key_scale = lax.dynamic_slice_in_dim(small_rows[3], own_ctx * columns, columns)
    router_full = jnp.pad(small_full[:, 4 : 4 + experts], ((0, 0), (0, EXTRA - experts)))

    inputs = jnp.concatenate(gather_direct(own_rows, "context", n_ctx))
    places = xor_blocks(positions[0], own_ctx, n_ctx, 0)
    named = jnp.sum(
        (routes[0][:, :, None] == jnp.arange(experts, dtype=jnp.int32)[None, None, :]).astype(f32), axis=1
    )
    w_out = lax.all_gather(after(w_output, inputs), "expert", axis=0, tiled=True)

    steps = n_ctx.bit_length() - 1
    downs = []
    for e in range(EXP_DEV):
        points = cuts(expert_down.shape[1], steps)
        downs.append(
            gather_start([expert_down[e, points[j] : points[j + 1]] for j in range(steps)])
        )
    down_came = gather_step(downs[0], "context", n_ctx)

    pull = lax.all_gather(after(cotangent[0], down_came), "expert", axis=0, tiled=True)
    down_came = [gather_step(state, "context", n_ctx, down_came) for state in downs[1:]]
    input_r = inverse_rms(inputs.astype(f32))
    projected, normed, squares = project(inputs, input_r, attn_scale[None], packed, columns)
    query_p, key_p = projected[:, :columns], projected[:, columns : 2 * columns]
    squares = sum_rows(after(squares, down_came))
    r_both = lax.rsqrt(squares / width + epsilon)
    down_came = [
        gather_step(downs[0], "context", n_ctx, r_both if step == 0 else ()) for step in range(steps - 1)
    ]
    query_r, key_r = r_both[0][:, None], r_both[1][:, None]
    frequency = jnp.exp(
        jnp.arange(HEAD_DIM // 2, dtype=f32) * (-2.0 * math.log(rope_base) / HEAD_DIM)
    )
    angles = places.astype(f32)[:, None] * frequency[None, :]
    cosine, sine = jnp.cos(angles), jnp.sin(angles)
    cosine, sine = jnp.concatenate([cosine, cosine], 1), jnp.concatenate([-sine, sine], 1)
    stats = r_both.T
    scales = jnp.stack(
        [query_scale.reshape(heads, HEAD_DIM), key_scale.reshape(heads, HEAD_DIM)], axis=1
    )
    attended, query, keyv, log_total = attend(
        projected, stats, scales, cosine, sine, places, heads
    )
    branch = dot(attended, w_out, ((1,), (0,))).astype(bf16)
    branch = after(branch, down_came)
    branch_own = scatter_xor(jnp.split(branch, n_ctx), "context", n_ctx)
    middle = own_rows.astype(f32) + branch_own
    middle_r = inverse_rms(middle)
    mixed_own = (middle * middle_r * moe_scale).astype(bf16)

    own_probs = jax.nn.softmax(dot(mixed_own, router_full, ((1,), (0,)))[:, :experts], axis=-1)
    probs_high = own_probs.astype(bf16)
    probs_low = (own_probs - probs_high.astype(f32)).astype(bf16)
    beside = jnp.concatenate([probs_high, probs_low, named.astype(bf16)], axis=1)
    beside = jnp.pad(beside, ((0, 0), (0, EXTRA - beside.shape[1])))
    mixed_own = jnp.concatenate([xor_blocks(mixed_own, own_ctx, n_ctx, 1), beside], axis=1)
    mixed_wide = lax.all_gather(after(mixed_own, pull), "expert", axis=0, tiled=True)

    own = own_ctx.astype(jnp.int32)[None]
    weights, first_came = [], []
    links_free = [branch_own]
    back, down = pull_down(own, after(pull, mixed_own), gathered(downs[0]))
    for e in range(EXP_DEV):
        if e > 0:
            for _ in range(steps - 1):
                gather_step(downs[e], "context", n_ctx, *links_free)
        pair = gather_start([expert_gate[e], expert_up[e]])
        came = [gather_step(pair, "context", n_ctx, *links_free)]
        came += [gather_step(pair, "context", n_ctx) for _ in range(steps - 1)]
        weights.append(gathered(pair))
        first_came.append(came[0])
        links_free = [branch_own, came, back]
    mixed_wide = after(mixed_wide, back)
    mixed, beside = mixed_wide[:, :width], mixed_wide[:, width:].astype(f32)
    router_x = xor_blocks(router_full, own_ctx, n_ctx, 0)
    router_probs = beside[:, :experts] + beside[:, experts : 2 * experts]
    named_all = beside[:, 2 * experts : 3 * experts]
    local = own_exp * EXP_DEV
    gates = lax.dynamic_slice_in_dim(router_probs * named_all, local, EXP_DEV, 1)
    def weight_grad(left, right):
        return dot(left, right, ((0,), (0,))).astype(bf16)

    def gate_up_grads(e, *first):
        grads = after(d_acts[e], *first)
        return weight_grad(mixed, grads[:, :ff]), weight_grad(mixed, grads[:, ff:])

    def owner_rows(grad):
        rows = ff // n_ctx
        return [lax.dynamic_slice_in_dim(grad, (own_ctx ^ k) * rows, rows, 0) for k in range(n_ctx)]

    def sums_of(state):
        return [found[0] for found in state]

    ff = back.shape[1]
    backs, down_w = [back], [down]
    hidden_g, d_acts, d_gates, g_raw = [], [], [], []
    for e in range(EXP_DEV):
        rows_in = after(mixed_wide, g_raw, backs[e])
        for kept, made in zip(
            (hidden_g, d_acts, d_gates), run_experts(rows_in, backs[e], gates, *weights[e], e)
        ):
            kept.append(made)
        if e + 1 < EXP_DEV:
            g_raw.append(gate_up_grads(e, first_came[e + 1]))
            back, down = pull_down(own, after(pull, d_acts), gathered(downs[e + 1]))
            backs.append(back)
            down_w.append(down)
    pairs = [scatter_state([jnp.split(grad, n_ctx) for grad in raw]) for raw in g_raw]
    pair_came = [scatter_step(pair, "context", n_ctx, 0) for pair in pairs]

    slots = jnp.arange(experts, dtype=jnp.int32)[None, :]
    drp = sum(
        jnp.where(slots == local + e, d_gates[e] * named_all, 0.0) for e in range(EXP_DEV)
    )
    d_logits = (
        router_probs * (drp - jnp.sum(router_probs * drp, axis=-1, keepdims=True))
    ).astype(bf16)
    d_logits = jnp.pad(d_logits, ((0, 0), (0, EXTRA - experts)))

    d_mixed_part = rows_back(d_acts, d_logits, weights, router_x)
    d_mixed_part = after(d_mixed_part, pair_came)
    pair_came = [
        scatter_step(pair, "context", n_ctx, step, pair_came) for pair in pairs for step in range(1, steps)
    ]
    d_mixed = lax.psum_scatter(d_mixed_part, "expert", scatter_dimension=0, tiled=True).astype(f32)
    d_mixed = xor_blocks(d_mixed, own_ctx, n_ctx, 1)

    raw = gate_up_grads(EXP_DEV - 1, d_mixed_part)
    pairs.append(scatter_state([jnp.split(grad, n_ctx) for grad in raw]))
    last_came = scatter_step(pairs[-1], "context", n_ctx, 0, pair_came)
    out_part = combine(after(hidden_g, raw, pair_came), down_w)
    out_part = after(out_part, last_came)
    out_own = lax.psum_scatter(out_part, "expert", scatter_dimension=0, tiled=True).astype(f32)
    d_mixed = after(d_mixed, out_part)
    g_router = xor_blocks(dot(mixed, d_logits, ((0,), (0,)))[:, :experts], own_ctx, n_ctx, 0)

    scaled = d_mixed * moe_scale
    g_moe = jnp.sum(d_mixed * middle * middle_r, axis=0)
    d_middle = (
        cotangent[0].astype(f32)
        + middle_r * scaled
        - middle * (middle_r**3 * jnp.mean(scaled * middle, axis=-1, keepdims=True))
    )
    points = cuts(tokens, steps)
    d_low = d_middle.astype(bf16)
    state = gather_start([d_low[points[j] : points[j + 1]] for j in range(steps)])
    came, down_raw = (), []
    for step in range(max(steps, EXP_DEV)):
        if step < EXP_DEV:
            down_raw.append(weight_grad(after(hidden_g[step], d_middle, *came), pull))
        if step < steps:
            came = gather_step(state, "context", n_ctx)
    d_branch = jnp.concatenate(
        [
            lax.slice_in_dim(array, block * rows, (block + 1) * rows, axis=0)
            for parts in zip(*gathered(state))
            for array, block, rows in parts
        ]
    )
    d_branch = after(d_branch, down_raw)
    last_came = [
        scatter_step(pairs[-1], "context", n_ctx, step, d_branch) for step in range(1, steps)
    ]
    down_sums = scatter_state([owner_rows(grad) for grad in down_raw])
    down_came = scatter_step(down_sums, "context", n_ctx, 0, last_came)

    d_attended = dot(d_branch, w_out, ((1,), (1,))).astype(bf16)
    d_query, d_key, d_value, inner_q, inner_k, g_heads = attend_back(
        projected, query, keyv, d_attended, log_total, stats, scales, cosine, sine, places, heads
    )
    result = (middle + after(out_own, d_query)).astype(bf16)
    inner_q, inner_k = jnp.sum(inner_q[:, :, 0], axis=0), jnp.sum(inner_k[:, :, 0], axis=0)
    g_side = side_grads(normed, after(d_value, last_came), attended, d_branch, n_exp, n_ctx).reshape(width, 2 * columns)
    g_side = lax.psum_scatter(g_side, "expert", scatter_dimension=0, tiled=True)
    inner_both = jnp.stack([inner_q, inner_k])
    inner_both = sum_rows(after(inner_both, down_came)) / width
    g_heads = g_heads.transpose(1, 0, 2).reshape(2, columns)
    d_query_p = query_r * (query_scale * d_query) - query_p * (query_r**3 * inner_both[0][:, None])
    d_key_p = key_r * (key_scale * d_key) - key_p * (key_r**3 * inner_both[1][:, None])
    d_projected = jnp.concatenate(
        [d_query_p.astype(bf16), d_key_p.astype(bf16), d_value], axis=1
    )
    spread = lax.dynamic_update_slice(
        jnp.zeros((2, width), f32), g_heads, (jnp.zeros_like(own_ctx), own_ctx * columns)
    )
    beside = jnp.concatenate([jnp.zeros((width, 1), f32), g_moe[:, None], spread.T, g_router], axis=1)
    beside = jnp.pad(beside, ((0, 0), (0, EXTRA - beside.shape[1])))
    d_normed_part, g_packed = project_back(d_projected, packed, inputs, input_r, normed, beside)
    down_came = [
        scatter_step(down_sums, "context", n_ctx, step, inner_both) for step in range(1, steps)
    ]
    d_normed = scatter_xor(jnp.split(after(d_normed_part, down_came), n_ctx), "context", n_ctx)
    own_in = own_rows.astype(f32)
    own_r = inverse_rms(own_in)
    scaled_in = d_normed * attn_scale
    input_grad = (
        d_middle
        + own_r * scaled_in
        - own_in * (own_r**3 * jnp.mean(scaled_in * own_in, axis=-1, keepdims=True))
    )

    def to_owners(grads):
        grads = xor_blocks(grads.reshape(n_ctx, part, -1), own_ctx, n_ctx, 0)
        grads = jnp.stack(trade([grads[k] for k in range(n_ctx)])).astype(f32)
        return xor_blocks(grads, own_ctx, n_ctx, 0)

    def full_rows(grads):
        return grads.transpose(1, 0, 2).reshape(part, width)

    g_packed = g_packed.reshape(width, 2 * columns + EXTRA)
    g_packed = to_owners(lax.psum_scatter(g_packed, "expert", scatter_dimension=0, tiled=True))
    g_small = jnp.sum(g_packed[:, :, 2 * columns :], axis=0)
    return (
        result[None],
        input_grad[None],
        full_rows(g_packed[:, :, :columns]),
        full_rows(g_packed[:, :, columns : 2 * columns]),
        full_rows(to_owners(g_side[:, :columns])),
        full_rows(g_side[:, columns:].astype(f32).reshape(n_ctx, part, columns)),
        g_small[:, 4 : 4 + experts],
        g_small[:, 0],
        g_small[:, 2],
        g_small[:, 3],
        g_small[:, 1],
        jnp.stack([sums_of(pair)[0] for pair in pairs]),
        jnp.stack([sums_of(pair)[1] for pair in pairs]),
        jnp.stack(sums_of(down_sums)),
    )


def solution(mesh):
    rows = P("expert", "context", None)
    split = P(("context", "expert"), None)
    line = P(("context", "expert"))
    return jax.shard_map(
        shards,
        mesh=mesh,
        in_specs=(rows, P("expert", None), rows, rows) + (split,) * 5 + (line,) * 4 + (rows,) * 3,
        out_specs=(rows, rows) + (split,) * 5 + (line,) * 4 + (rows,) * 3,
        check_vma=False,
    )
```

time: 962 us -> 857 us (0.89)
  Pallas kernels: 170 us -> 247 us
  local copies, waits for them, and re-layouts: 125 us -> 53.1 us
  matrix products: 154 us -> 86.1 us
  blocking collectives: 34 us -> 0 us
  starting transfers between devices: 80.8 us -> 68.3 us
    pallas_call x3 -> x9, Pallas kernels: 125 us -> 201 us  [the longest x2 56.1 us: run_experts(): pl.pallas_call(lambda *refs: experts_kernel(e, len(gate_k), *refs), grid=...]
    dot_general x16 -> x10, matrix products: 154 us -> 86.1 us  [dot(): lax.dot_general(left, right, (dims, ((), ())), preferred_element_type=f32)]
    psum x2 -> x0, blocking collectives: 34 us -> none  [psum_rows(): stats = lax.psum(xor_blocks(stats, own_ctx, n_ctx, 1), 'context')]
    unnamed x218 -> x155, local copies, waits for them, and re-layouts: 53.1 us -> 19.6 us
    add x10 -> x3, other arithmetic: 16.6 us -> 1.03 us  [the longest x2 1.01 us: scatter_step(): found[p ^ bit] = found[p ^ bit].astype(f32) + part.astype(f32)]
    concatenate x9 -> x5, local copies, waits for them, and re-layouts: 18 us -> 3.78 us  [the longest x2 3.38 us: scatter_step(): jnp.concatenate(send)]
    concatenate x2 -> x18, other arithmetic: 6.96 us -> 20.7 us  [the longest x9 14.1 us: gather_step(): send = arrays[0] if len(arrays) == 1 else jnp.concatenate(arrays)]
    ppermute x78 -> x58, starting transfers between devices: 80 us -> 68 us  [swap(): return lax.ppermute(value, axis, [(i, i ^ bit) for i in range(count)])]
  transfers between devices with their start and end apart: 86 -> 66, of which waited for: 34 -> 36; matrix products, arithmetic and copies ran while one was open for 34% -> 25% of each run, Pallas kernels for 9% -> 29%
where the time goes in v3:
time: 857 us; the launch traced here: 844 us
  waiting for transfers between devices  277 us (32%)
  Pallas kernels  247 us (29%)
  other arithmetic  96.4 us (11%)
  matrix products  86.1 us (10%)
  starting transfers between devices  68.3 us (8%)
  local copies, waits for them, and re-layouts  53.1 us (6%)
  between operations  15.8 us (2%)
    ppermute x58, waiting for transfers between devices, swap(): return lax.ppermute(value, axis, [(i, i ^ bit) for i in range(count)])  265 us
    dot_general x10, matrix products, dot(): lax.dot_general(left, right, (dims, ((), ())), preferred_element_type=f32)  86.1 us
    ppermute x58, starting transfers between devices, swap(): return lax.ppermute(value, axis, [(i, i ^ bit) for i in range(count)])  68 us
    pallas_call x2, Pallas kernels, run_experts(): pl.pallas_call(lambda *refs: experts_kernel(e, len(gate_k), *refs), grid=...  56.1 us
    pallas_call x1, Pallas kernels, rows_back(): pl.pallas_call(lambda *refs: rows_back_kernel(count, n_ctx, *refs), grid=...  47.2 us
    pallas_call x1, Pallas kernels, attend_back(): pl.pallas_call(lambda *refs: attend_back_kernel(min(256, rows), *refs), g...  29.3 us
    pallas_call x2, Pallas kernels, pull_down(): pl.pallas_call(lambda *refs: pull_down_kernel(places, *refs), grid=(rows...  28.4 us
    pallas_call x1, Pallas kernels, combine(): pl.pallas_call(lambda *refs: combine_kernel(count, *refs), grid=(rows //...  24 us
  transfers between devices with their start and end apart: 66, of which 36 were waited for; matrix products, arithmetic and copies ran while one was open for 25% of the time, Pallas kernels for 29%

profile of v3, /device:TPU:0, one launch (start us, length us, event | category | flops | bytes accessed | tf_op | source)
XLA Modules:
  0.0 844.0 jit_solution(3410332188711486043)
XLA Ops:
  16.5 5.5 collective-permute-done.5
  31.0 23.5 %collective-permute-done.2 = bf16[256,2048]{1,0:T(8,128)(2,1)S(1)} collective-permute-done((bf16[256,2048]{1,0:T(8,128)(2,1)S(1)}, bf16[256,2048]{1,0:T(8,128)(2,1)S(1)}, u32[]{:S(2)}, u32[]{:S(2)}) %collective-permute-start.2) | collective-permute-done | bytes 1048608 | tf_op jit(solution)/shard_map/ppermute | solution.py:38
  54.5 21.2 %collective-permute-done.1 = bf16[256,2048]{1,0:T(8,128)(2,1)S(1)} collective-permute-done((bf16[256,2048]{1,0:T(8,128)(2,1)S(1)}, bf16[256,2048]{1,0:T(8,128)(2,1)S(1)}, u32[]{:S(2)}, u32[]{:S(2)}) %collective-permute-start.1) | collective-permute-done | bytes 1048608 | tf_op jit(solution)/shard_map/ppermute | solution.py:38
  82.4 11.7 %collective-permute-done.6.refs_3_ = bf16[128,2048]{1,0:T(8,128)(2,1)S(1)} collective-permute-done((bf16[128,2048]{1,0:T(8,128)(2,1)S(1)}, bf16[128,2048]{1,0:T(8,128)(2,1)S(1)}, u32[]{:S(2)}, u32[]{:S(2)}) %collective-permute-start.6) | collective-permute-done | bytes 524320 | tf_op jit(solution)/shard_map/ppermute | solution.py:38
  107.0 16.1 %project.1 = (f32[1024,1536]{1,0:T(8,128)}, bf16[1024,2048]{1,0:T(8,128)(2,1)}, f32[2,1024]{1,0:T(2,128)}) custom-call(bf16[1024,2048]{1,0:T(8,128)(2,1)} %get-tuple-element.248.refs_0_.refs_2_, f32[1024,1]{1,0:T(8,128)} %copy.215.refs_1_.refs_3_, f32[1,2048]{1,0:T(1,128)} %get-tuple-element.340.refs_2_, bf16[8,4,64,1664]{3,2,1,0:T(8,128)(2,1)} %bitcast.174), custom_call_target="tpu_custom_call" | custom-call | flops 6442450944 | bytes 21495808 | tf_op jit(solution)/shard_map/project/pallas_call | solution.py:163
  136.9 16.9 %attend.1 = (bf16[1024,512]{1,0:T(8,128)(2,1)}, bf16[1024,512]{1,0:T(8,128)(2,1)}, bf16[1024,512]{1,0:T(8,128)(2,1)}, f32[4,1024,1]{2,1,0:T(8,128)}) custom-call(f32[1024,1536]{1,0:T(8,128)} %get-tuple-element.87.refs_0_.refs_1_.refs_2_, f32[1024,1536]{1,0:T(8,128)} %get-tuple-element.87.refs_0_.refs_1_.refs_2_, ...), custom_call_target="tpu_custom_call" | custom-call | flops 2147483648 | bytes 6291456 | tf_op jit(solution)/shard_map/attend/pallas_call | solution.py:285
  161.3 19.3 %collective-permute-done.16 = bf16[256,2048]{1,0:T(8,128)(2,1)S(1)} collective-permute-done((bf16[256,2048]{1,0:T(8,128)(2,1)S(1)}, bf16[256,2048]{1,0:T(8,128)(2,1)S(1)}, u32[]{:S(2)}, u32[]{:S(2)}) %collective-permute-start.16) | collective-permute-done | bytes 1048608 | tf_op jit(solution)/shard_map/ppermute | solution.py:38
  185.4 6.8 collective-permute-done.17
  199.1 10.3 %all-gather.8.cloned.1.call-done.refs_1_ = bf16[2048,2048]{1,0:T(8,128)(2,1)} async-done(((bf16[256,2048]{1,0:T(8,128)(2,1)}), bf16[2048,2048]{1,0:T(8,128)(2,1)}) %all-gather.8.cloned.1.call-update) | async-done | bytes 8388624 | tf_op jit(solution)/shard_map/all_gather | solution.py:596
  214.7 22.1 %collective-permute-done.19.refs_4_.refs_3_ = bf16[512,1024]{1,0:T(8,128)(2,1)S(1)} collective-permute-done((bf16[512,1024]{1,0:T(8,128)(2,1)S(1)}, bf16[512,1024]{1,0:T(8,128)(2,1)S(1)}, u32[]{:S(2)}, u32[]{:S(2)}) %collective-permute-start.19) | collective-permute-done | bytes 1048608 | tf_op jit(solution)/shard_map/ppermute | solution.py:38
  243.1 14.2 %pull_down.2 = (f32[2048,1024]{1,0:T(8,128)}, bf16[1024,2048]{1,0:T(8,128)(2,1)}) custom-call(s32[1]{0:T(128)} %bitcast.32.refs_0_, bf16[2048,2048]{1,0:T(8,128)(2,1)} %all-gather.8.cloned.1.call-done.refs_1_, bf16[128,2048]{1,0:T(8,128)(2,1)} %copy-done.27, bf16[128,2048]{1,0:T(8,128)(2,1)} %copy-done.43, ...), custom_call_target="tpu_custom_call" | custom-call | flops 8589934592 | bytes 25165824 | tf_op jit(solution)/shard_map/pull_down/pallas_call | solution.py:402
  257.3 28.5 %collective-permute-done.20.refs_5_.refs_6_.refs_4_ = bf16[1024,1024]{1,0:T(8,128)(2,1)S(1)} collective-permute-done((bf16[1024,1024]{1,0:T(8,128)(2,1)}, bf16[1024,1024]{1,0:T(8,128)(2,1)S(1)}, u32[]{:S(2)}, u32[]{:S(2)}) %collective-permute-start.20) | collective-permute-done | bytes 2097184 | tf_op jit(solution)/shard_map/ppermute | solution.py:38
  297.7 17.1 %collective-permute-done.23.refs_4_.refs_11_ = bf16[512,1024]{1,0:T(8,128)(2,1)} collective-permute-done((bf16[512,1024]{1,0:T(8,128)(2,1)S(1)}, bf16[512,1024]{1,0:T(8,128)(2,1)}, u32[]{:S(2)}, u32[]{:S(2)}) %collective-permute-start.23) | collective-permute-done | bytes 1048608 | tf_op jit(solution)/shard_map/ppermute | solution.py:38
  325.7 28.0 %expert.2 = (bf16[2048,1024]{1,0:T(8,128)(2,1)}, bf16[2048,2048]{1,0:T(8,128)(2,1)}, f32[2048,1]{1,0:T(8,128)}) custom-call(bf16[2048,2176]{1,0:T(8,128)(2,1)} %all-gather.10.cloned.1.call-done.refs_0_, f32[2048,1024]{1,0:T(8,128)} %get-tuple-element.102.refs_1_, f32[2048,2]{1,0:T(8,128)} %dynamic-slice_multiply_fusion.refs_2_, bf16[512,1024]{1,0:T(8,128)(2,1)} %copy-done.5, ...), custom_call_target="tpu_custom_call" | custom-call | flops 17179869184 | bytes 37748736 | tf_op jit(solution)/shard_map/expert/pallas_call | solution.py:443
  353.7 12.7 %fusion.14 = bf16[2048,1024]{1,0:T(8,128)(2,1)S(1)} fusion(bf16[2048,2048]{1,0:T(8,128)(2,1)} %get-tuple-element.111.refs_0_, bf16[2048,2176]{1,0:T(8,128)(2,1)} %all-gather.10.cloned.1.call-done.refs_0_), kind=kOutput, calls=%fused_computation.19 | convolution fusion | flops 8592031744 | bytes 16777216 | tf_op jit(solution)/shard_map/dot_general | solution.py:24
  370.1 14.3 %pull_down.3 = (f32[2048,1024]{1,0:T(8,128)}, bf16[1024,2048]{1,0:T(8,128)(2,1)}) custom-call(s32[1]{0:T(128)} %bitcast.32.refs_0_, bf16[2048,2048]{1,0:T(8,128)(2,1)} %all-gather.8.cloned.1.call-done.refs_1_, bf16[128,2048]{1,0:T(8,128)(2,1)} %get-tuple-element.89.refs_2_, bf16[128,2048]{1,0:T(8,128)(2,1)} %collective-permute-done.8.refs_3_, ...), custom_call_target="tpu_custom_call" | custom-call | flops 8589934592 | bytes 25165824 | tf_op jit(solution)/shard_map/pull_down/pallas_call | solution.py:402
  384.4 12.7 %fusion.19 = bf16[2048,1024]{1,0:T(8,128)(2,1)S(1)} fusion(bf16[2048,2048]{1,0:T(8,128)(2,1)} %get-tuple-element.111.refs_0_, bf16[2048,2176]{1,0:T(8,128)(2,1)} %all-gather.10.cloned.1.call-done.refs_0_), kind=kOutput, calls=%fused_computation.20 | convolution fusion | flops 8592031744 | bytes 16777216 | tf_op jit(solution)/shard_map/dot_general | solution.py:24
  401.1 28.1 %expert.3 = (bf16[2048,1024]{1,0:T(8,128)(2,1)}, bf16[2048,2048]{1,0:T(8,128)(2,1)}, f32[2048,1]{1,0:T(8,128)}) custom-call(bf16[2048,2176]{1,0:T(8,128)(2,1)} %all-gather.10.cloned.1.call-done.refs_0_, f32[2048,1024]{1,0:T(8,128)} %get-tuple-element.115.refs_1_, f32[2048,2]{1,0:T(8,128)} %dynamic-slice_multiply_fusion.refs_2_, bf16[512,1024]{1,0:T(8,128)(2,1)} %copy-done.4, ...), custom_call_target="tpu_custom_call" | custom-call | flops 17179869184 | bytes 37748736 | tf_op jit(solution)/shard_map/expert/pallas_call | solution.py:443
  434.5 47.2 %rows_back.1 = bf16[2048,2048]{1,0:T(8,128)(2,1)} custom-call(bf16[2048,2048]{1,0:T(8,128)(2,1)} %get-tuple-element.111.refs_0_, bf16[2048,2048]{1,0:T(8,128)(2,1)} %get-tuple-element.122.refs_1_, bf16[512,1024]{1,0:T(8,128)(2,1)} %copy-done.5, bf16[512,1024]{1,0:T(8,128)(2,1)} %copy-done.18, bf16[1024,1024]{1,0:T(8,128)(2,1)} %copy-done.8, ...), custom_call_target="tpu_custom_call" | custom-call | bytes 2097152 | tf_op jit(solution)/shard_map/rows_back/pallas_call | solution.py:505
  488.9 12.8 %fusion.24 = bf16[2048,1024]{1,0:T(8,128)(2,1)S(1)} fusion(bf16[2048,2048]{1,0:T(8,128)(2,1)} %get-tuple-element.122.refs_1_, bf16[2048,2176]{1,0:T(8,128)(2,1)} %all-gather.10.cloned.1.call-done.refs_0_), kind=kOutput, calls=%fused_computation.21 | convolution fusion | flops 8592031744 | bytes 16777216 | tf_op jit(solution)/shard_map/dot_general | solution.py:24
  501.8 12.9 %fusion.29 = bf16[2048,1024]{1,0:T(8,128)(2,1)S(1)} fusion(bf16[2048,2048]{1,0:T(8,128)(2,1)S(1)} %bitcast.139, bf16[2048,2176]{1,0:T(8,128)(2,1)} %all-gather.10.cloned.1.call-done.refs_0_), kind=kOutput, calls=%fused_computation.22 | convolution fusion | flops 8592031744 | bytes 16777216 | tf_op jit(solution)/shard_map/dot_general | solution.py:24
  521.8 24.0 %combine.1 = bf16[2048,2048]{1,0:T(8,128)(2,1)} custom-call(bf16[2048,1024]{1,0:T(8,128)(2,1)} %get-tuple-element.135.refs_0_, bf16[2048,1024]{1,0:T(8,128)(2,1)} %get-tuple-element.136.refs_1_, bf16[1024,2048]{1,0:T(8,128)(2,1)} %get-tuple-element.127.refs_2_, bf16[1024,2048]{1,0:T(8,128)(2,1)} %get-tuple-element.128.refs_3_), custom_call_target="tpu_custom_call" | custom-call | flops 17179869184 | bytes 25165824 | tf_op jit(solution)/shard_map/combine/pallas_call | solution.py:471
  545.8 15.7 %collective-permute-done.33 = bf16[1024,1024]{1,0:T(8,128)(2,1)} collective-permute-done((bf16[1024,1024]{1,0:T(8,128)(2,1)}, bf16[1024,1024]{1,0:T(8,128)(2,1)}, u32[]{:S(2)}, u32[]{:S(2)}) %collective-permute-start.33) | collective-permute-done | bytes 2097184 | tf_op jit(solution)/shard_map/ppermute | solution.py:38
  579.8 11.0 %convolution_convert_fusion.1 = bf16[1024,2048]{1,0:T(8,128)(2,1)} fusion(bf16[2048,1024]{1,0:T(8,128)(2,1)S(1)} %copy-done.65, bf16[2048,2048]{1,0:T(8,128)(2,1)S(1)} %bitcast.194), kind=kOutput, calls=%fused_computation.24 | convolution fusion | flops 8592031744 | bytes 16777216 | tf_op jit(solution)/shard_map/dot_general | solution.py:24
  593.1 11.0 %convolution_convert_fusion = bf16[1024,2048]{1,0:T(8,128)(2,1)} fusion(bf16[2048,1024]{1,0:T(8,128)(2,1)S(1)} %copy-done.66, bf16[2048,2048]{1,0:T(8,128)(2,1)S(1)} %bitcast.194), kind=kOutput, calls=%fused_computation.23 | convolution fusion | flops 8592031744 | bytes 16777216 | tf_op jit(solution)/shard_map/dot_general | solution.py:24
  604.1 9.0 %collective-permute-done.37 = bf16[256,2048]{1,0:T(8,128)(2,1)S(1)} collective-permute-done((bf16[256,2048]{1,0:T(8,128)(2,1)S(1)}, bf16[256,2048]{1,0:T(8,128)(2,1)S(1)}, u32[]{:S(2)}, u32[]{:S(2)}) %collective-permute-start.37) | collective-permute-done | bytes 1048608 | tf_op jit(solution)/shard_map/ppermute | solution.py:38
  620.0 29.3 %attend_back.1 = (f32[1024,512]{1,0:T(8,128)}, f32[1024,512]{1,0:T(8,128)}, bf16[1024,512]{1,0:T(8,128)(2,1)}, f32[4,1024,1]{2,1,0:T(8,128)}, f32[4,1024,1]{2,1,0:T(8,128)}, /*index=5*/f32[4,2,128]{2,1,0:T(2,128)}) custom-call(f32[1024,1536]{1,0:T(8,128)} %get-tuple-element.87.refs_0_.refs_1_.refs_2_, ...), custom_call_target="tpu_custom_call" | custom-call | bytes 1048576 | tf_op jit(solution)/shard_map/attend_back/pallas_call | solution.py:347
  649.4 10.0 %side_grads.1 = bf16[8,4,64,1024]{3,2,1,0:T(8,128)(2,1)} custom-call(bf16[1024,2048]{1,0:T(8,128)(2,1)} %get-tuple-element.150.refs_4_.refs_0_, bf16[1024,512]{1,0:T(8,128)(2,1)} %get-tuple-element.159.refs_1_, bf16[1024,512]{1,0:T(8,128)(2,1)} %get-tuple-element.92.refs_2_, bf16[1024,2048]{1,0:T(8,128)(2,1)} %copy-done.46), custom_call_target="tpu_custom_call" | custom-call | flops 4294967296 | bytes 12582912 | tf_op jit(solution)/shard_map/side_grads/pallas_call | solution.py:202
  676.9 32.7 %collective-permute-done.41 = bf16[512,2048]{1,0:T(8,128)(2,1)} collective-permute-done((bf16[512,2048]{1,0:T(8,128)(2,1)}, bf16[512,2048]{1,0:T(8,128)(2,1)}, u32[]{:S(2)}, u32[]{:S(2)}) %collective-permute-start.41) | collective-permute-done | bytes 2097184 | tf_op jit(solution)/shard_map/ppermute | solution.py:38
  725.2 19.2 %project_back.1 = (bf16[1024,2048]{1,0:T(8,128)(2,1)}, bf16[8,4,64,1152]{3,2,1,0:T(8,128)(2,1)}) custom-call(bf16[1024,1536]{1,0:T(8,128)(2,1)} %pad_maximum_fusion.4.refs_0_, bf16[8,4,64,1664]{3,2,1,0:T(8,128)(2,1)} %bitcast.175, bf16[1024,2048]{1,0:T(8,128)(2,1)} %get-tuple-element.248.refs_0_.refs_2_, f32[1024,1]{1,0:T(8,128)} %copy.215.refs_1_.refs_3_, ...), custom_call_target="tpu_custom_call" | custom-call | flops 10737418240 | bytes 30408704 | tf_op jit(solution)/shard_map/project_back/pallas_call | solution.py:232
  768.2 8.2 collective-permute-done.46
  785.2 16.1 %collective-permute-done.49 = bf16[256,2048]{1,0:T(8,128)(2,1)S(1)} collective-permute-done((bf16[256,2048]{1,0:T(8,128)(2,1)S(1)}, bf16[256,2048]{1,0:T(8,128)(2,1)S(1)}, u32[]{:S(2)}, u32[]{:S(2)}) %collective-permute-start.49) | collective-permute-done | bytes 1048608 | tf_op jit(solution)/shard_map/ppermute | solution.py:38
  (435 shorter events, 260.3 us)
Async XLA Ops:
  7.2 97.6 %all-gather.12.cloned.1.call-start = ((), (), s32[]{:S(2)}) async-start(), calls=%async_computation.11 | async-start | bytes 7667712 | tf_op jit(solution)/shard_map/all_gather | solution.py:572
  27.2 126.6 %all-gather.6.cloned.1.call-start = ((), (), s32[]{:S(2)}) async-start(), calls=%async_computation.4 | async-start | bytes 2359296 | tf_op jit(solution)/shard_map/all_gather | solution.py:585
  27.5 27.0 %collective-permute-start.2 = (bf16[256,2048]{1,0:T(8,128)(2,1)S(1)}, bf16[256,2048]{1,0:T(8,128)(2,1)S(1)}, u32[]{:S(2)}, u32[]{:S(2)}) collective-permute-start(bf16[256,2048]{1,0:T(8,128)(2,1)S(1)} %bitcast.134), channel_id=1, source_target_pairs={{0,24},{8,16},{16,8},{24,0},{1,25},{9,17},{17,9},{25,1},{2,26},{10... | collective-permute-start | bytes 3145736 | tf_op jit(solution)/shard_map/ppermute | solution.py:38
  29.0 46.6 %collective-permute-start.1 = (bf16[256,2048]{1,0:T(8,128)(2,1)S(1)}, bf16[256,2048]{1,0:T(8,128)(2,1)S(1)}, u32[]{:S(2)}, u32[]{:S(2)}) collective-permute-start(bf16[256,2048]{1,0:T(8,128)(2,1)S(1)} %bitcast.135), channel_id=1, source_target_pairs={{0,16},{8,24},{16,0},{24,8},{1,17},{9,25},{17,1},{25,9},{2,18},{10... | collective-permute-start | bytes 3145736 | tf_op jit(solution)/shard_map/ppermute | solution.py:38
  30.4 45.5 %collective-permute-start = (bf16[256,2048]{1,0:T(8,128)(2,1)S(1)}, bf16[256,2048]{1,0:T(8,128)(2,1)S(1)}, u32[]{:S(2)}, u32[]{:S(2)}) collective-permute-start(bf16[256,2048]{1,0:T(8,128)(2,1)S(1)} %bitcast.136), channel_id=1, source_target_pairs={{0,8},{8,0},{16,24},{24,16},{1,9},{9,1},{17,25},{25,17},{2,10},{10... | collective-permute-start | bytes 3145736 | tf_op jit(solution)/shard_map/ppermute | solution.py:38
  78.4 131.1 %all-gather.8.cloned.1.call-start = ((), (), s32[]{:S(2)}) async-start(), calls=%async_computation.5 | async-start | bytes 9437184 | tf_op jit(solution)/shard_map/all_gather | solution.py:596
  96.4 225.9 %all-gather.10.cloned.1.call-start = ((), (), s32[]{:S(2)}) async-start(), calls=%async_computation.6 | async-start | bytes 10027008 | tf_op jit(solution)/shard_map/all_gather | solution.py:633
  132.8 25.3 %collective-permute-start.13 = (bf16[256,2048]{1,0:T(8,128)(2,1)}, bf16[256,2048]{1,0:T(8,128)(2,1)}, u32[]{:S(2)}, u32[]{:S(2)}) collective-permute-start(bf16[256,2048]{1,0:T(8,128)(2,1)} %pad_maximum_fusion.16), channel_id=1, source_target_pairs={{0,16},{8,24},{16,0},{24,8},{1,17},{9,25},{17,1},{25,9},{2,18},{10... | collective-permute-start | bytes 3145736 | tf_op jit(solution)/shard_map/ppermute | solution.py:38
  209.5 360.6 %reduce-scatter.7.cloned.1.call-start = ((), (), s32[]{:S(2)}) async-start(), calls=%async_computation.8 | async-start | bytes 9437184 | tf_op jit(solution)/shard_map/reduce_scatter | solution.py:701
  211.4 25.4 %collective-permute-start.19 = (bf16[512,1024]{1,0:T(8,128)(2,1)S(1)}, bf16[512,1024]{1,0:T(8,128)(2,1)S(1)}, u32[]{:S(2)}, u32[]{:S(2)}) collective-permute-start(bf16[512,1024]{1,0:T(8,128)(2,1)S(1)} %get-tuple-element.105.refs_3_.refs_2_), channel_id=1, source_target_pairs={{0,8},{8,0},{16,24},{24,16},{1,9},{9,1},{17,25},{25,17},{2,10},{10... | collective-permute-start | bytes 3145736 | tf_op jit(solution)/shard_map/ppermute | solution.py:38
  213.2 26.8 %collective-permute-start.21 = (bf16[512,1024]{1,0:T(8,128)(2,1)S(1)}, bf16[512,1024]{1,0:T(8,128)(2,1)S(1)}, u32[]{:S(2)}, u32[]{:S(2)}) collective-permute-start(bf16[512,1024]{1,0:T(8,128)(2,1)S(1)} %get-tuple-element.106.refs_7_.refs_6_), channel_id=1, source_target_pairs={{0,16},{8,24},{16,0},{24,8},{1,17},{9,25},{17,1},{25,9},{2,18},{10... | collective-permute-start | bytes 3145736 | tf_op jit(solution)/shard_map/ppermute | solution.py:38
  238.5 47.3 %collective-permute-start.20 = (bf16[1024,1024]{1,0:T(8,128)(2,1)}, bf16[1024,1024]{1,0:T(8,128)(2,1)S(1)}, u32[]{:S(2)}, u32[]{:S(2)}) collective-permute-start(bf16[1024,1024]{1,0:T(8,128)(2,1)} %pad_maximum_fusion.6), channel_id=1, source_target_pairs={{0,16},{8,24},{16,0},{24,8},{1,17},{9,25},{17,1},{25,9},{2,18},{10... | collective-permute-start | bytes 6291464 | tf_op jit(solution)/shard_map/ppermute | solution.py:38
  241.7 47.0 %collective-permute-start.22 = (bf16[1024,1024]{1,0:T(8,128)(2,1)}, bf16[1024,1024]{1,0:T(8,128)(2,1)S(1)}, u32[]{:S(2)}, u32[]{:S(2)}) collective-permute-start(bf16[1024,1024]{1,0:T(8,128)(2,1)} %pad_maximum_fusion.7), channel_id=1, source_target_pairs={{0,8},{8,0},{16,24},{24,16},{1,9},{9,1},{17,25},{25,17},{2,10},{10... | collective-permute-start | bytes 6291464 | tf_op jit(solution)/shard_map/ppermute | solution.py:38
  288.6 26.2 %collective-permute-start.23 = (bf16[512,1024]{1,0:T(8,128)(2,1)S(1)}, bf16[512,1024]{1,0:T(8,128)(2,1)}, u32[]{:S(2)}, u32[]{:S(2)}) collective-permute-start(bf16[512,1024]{1,0:T(8,128)(2,1)S(1)} %get-tuple-element.109.refs_3_.refs_10_), channel_id=1, source_target_pairs={{0,8},{8,0},{16,24},{24,16},{1,9},{9,1},{17,25},{25,17},{2,10},{10... | collective-permute-start | bytes 3145736 | tf_op jit(solution)/shard_map/ppermute | solution.py:38
  290.1 28.0 %collective-permute-start.24 = (bf16[512,1024]{1,0:T(8,128)(2,1)S(1)}, bf16[512,1024]{1,0:T(8,128)(2,1)}, u32[]{:S(2)}, u32[]{:S(2)}) collective-permute-start(bf16[512,1024]{1,0:T(8,128)(2,1)S(1)} %get-tuple-element.110.refs_7_.refs_14_), channel_id=1, source_target_pairs={{0,16},{8,24},{16,0},{24,8},{1,17},{9,25},{17,1},{25,9},{2,18},{10... | collective-permute-start | bytes 3145736 | tf_op jit(solution)/shard_map/ppermute | solution.py:38
  294.9 74.2 %collective-permute-start.25 = (bf16[256,2048]{1,0:T(8,128)(2,1)}, bf16[256,2048]{1,0:T(8,128)(2,1)S(1)}, u32[]{:S(2)}, u32[]{:S(2)}) collective-permute-start(bf16[256,2048]{1,0:T(8,128)(2,1)} %get-tuple-element.113), channel_id=1, source_target_pairs={{0,16},{8,24},{16,0},{24,8},{1,17},{9,25},{17,1},{25,9},{2,18},{10... | collective-permute-start | bytes 3145736 | tf_op jit(solution)/shard_map/ppermute | solution.py:38
  296.4 72.7 %collective-permute-start.26 = (bf16[256,2048]{1,0:T(8,128)(2,1)}, bf16[256,2048]{1,0:T(8,128)(2,1)}, u32[]{:S(2)}, u32[]{:S(2)}) collective-permute-start(bf16[256,2048]{1,0:T(8,128)(2,1)} %get-tuple-element.114), channel_id=1, source_target_pairs={{0,8},{8,0},{16,24},{24,16},{1,9},{9,1},{17,25},{25,17},{2,10},{10... | collective-permute-start | bytes 3145736 | tf_op jit(solution)/shard_map/ppermute | solution.py:38
  317.6 83.5 %collective-permute-start.27 = (bf16[1024,1024]{1,0:T(8,128)(2,1)}, bf16[1024,1024]{1,0:T(8,128)(2,1)}, u32[]{:S(2)}, u32[]{:S(2)}) collective-permute-start(bf16[1024,1024]{1,0:T(8,128)(2,1)} %pad_maximum_fusion.8), channel_id=1, source_target_pairs={{0,16},{8,24},{16,0},{24,8},{1,17},{9,25},{17,1},{25,9},{2,18},{10... | collective-permute-start | bytes 6291464 | tf_op jit(solution)/shard_map/ppermute | solution.py:38
  320.8 80.2 %collective-permute-start.28 = (bf16[1024,1024]{1,0:T(8,128)(2,1)}, bf16[1024,1024]{1,0:T(8,128)(2,1)}, u32[]{:S(2)}, u32[]{:S(2)}) collective-permute-start(bf16[1024,1024]{1,0:T(8,128)(2,1)} %pad_maximum_fusion.9), channel_id=1, source_target_pairs={{0,8},{8,0},{16,24},{24,16},{1,9},{9,1},{17,25},{25,17},{2,10},{10... | collective-permute-start | bytes 6291464 | tf_op jit(solution)/shard_map/ppermute | solution.py:38
  397.1 84.7 %collective-permute-start.29 = (bf16[1024,1024]{1,0:T(8,128)(2,1)}, bf16[1024,1024]{1,0:T(8,128)(2,1)}, u32[]{:S(2)}, u32[]{:S(2)}) collective-permute-start(bf16[1024,1024]{1,0:T(8,128)(2,1)} %concatenate.211), channel_id=1, source_target_pairs={{0,16},{8,24},{16,0},{24,8},{1,17},{9,25},{17,1},{25,9},{2,18},{10... | collective-permute-start | bytes 6291464 | tf_op jit(solution)/shard_map/ppermute | solution.py:38
  400.5 81.2 %collective-permute-start.30 = (bf16[1024,1024]{1,0:T(8,128)(2,1)}, bf16[1024,1024]{1,0:T(8,128)(2,1)}, u32[]{:S(2)}, u32[]{:S(2)}) collective-permute-start(bf16[1024,1024]{1,0:T(8,128)(2,1)} %pad_maximum_fusion.10), channel_id=1, source_target_pairs={{0,8},{8,0},{16,24},{24,16},{1,9},{9,1},{17,25},{25,17},{2,10},{10... | collective-permute-start | bytes 6291464 | tf_op jit(solution)/shard_map/ppermute | solution.py:38
  481.8 285.0 %reduce-scatter.5.cloned.1.call-start = ((), (), s32[]{:S(2)}) async-start(), calls=%async_computation.7 | async-start | bytes 9437184 | tf_op jit(solution)/shard_map/reduce_scatter | solution.py:709
  485.9 33.3 %collective-permute-start.31 = (bf16[512,1024]{1,0:T(8,128)(2,1)S(1)}, bf16[512,1024]{1,0:T(8,128)(2,1)S(1)}, u32[]{:S(2)}, u32[]{:S(2)}) collective-permute-start(bf16[512,1024]{1,0:T(8,128)(2,1)S(1)} %add_convert_fusion.6), channel_id=1, source_target_pairs={{0,8},{8,0},{16,24},{24,16},{1,9},{9,1},{17,25},{25,17},{2,10},{10... | collective-permute-start | bytes 3145736 | tf_op jit(solution)/shard_map/ppermute | solution.py:38
  487.5 31.7 %collective-permute-start.32 = (bf16[512,1024]{1,0:T(8,128)(2,1)S(1)}, bf16[512,1024]{1,0:T(8,128)(2,1)S(1)}, u32[]{:S(2)}, u32[]{:S(2)}) collective-permute-start(bf16[512,1024]{1,0:T(8,128)(2,1)S(1)} %add_convert_fusion.5), channel_id=1, source_target_pairs={{0,16},{8,24},{16,0},{24,8},{1,17},{9,25},{17,1},{25,9},{2,18},{10... | collective-permute-start | bytes 3145736 | tf_op jit(solution)/shard_map/ppermute | solution.py:38
  520.1 41.3 %collective-permute-start.33 = (bf16[1024,1024]{1,0:T(8,128)(2,1)}, bf16[1024,1024]{1,0:T(8,128)(2,1)}, u32[]{:S(2)}, u32[]{:S(2)}) collective-permute-start(bf16[1024,1024]{1,0:T(8,128)(2,1)} %concatenate.212), channel_id=1, source_target_pairs={{0,16},{8,24},{16,0},{24,8},{1,17},{9,25},{17,1},{25,9},{2,18},{10... | collective-permute-start | bytes 6291464 | tf_op jit(solution)/shard_map/ppermute | solution.py:38
  521.1 41.2 %collective-permute-start.34 = (bf16[1024,1024]{1,0:T(8,128)(2,1)}, bf16[1024,1024]{1,0:T(8,128)(2,1)S(1)}, u32[]{:S(2)}, u32[]{:S(2)}) collective-permute-start(bf16[1024,1024]{1,0:T(8,128)(2,1)} %pad_maximum_fusion.11), channel_id=1, source_target_pairs={{0,8},{8,0},{16,24},{24,16},{1,9},{9,1},{17,25},{25,17},{2,10},{10... | collective-permute-start | bytes 6291464 | tf_op jit(solution)/shard_map/ppermute | solution.py:38
  562.4 252.5 %reduce-scatter.11.cloned.1.call-start = ((), (), s32[]{:S(2)}) async-start(), calls=%async_computation.10 | async-start | bytes 4718592 | tf_op jit(solution)/shard_map/reduce_scatter | solution.py:750
  614.6 34.8 %collective-permute-start.39 = (bf16[512,1024]{1,0:T(8,128)(2,1)S(1)}, bf16[512,1024]{1,0:T(8,128)(2,1)S(1)}, u32[]{:S(2)}, u32[]{:S(2)}) collective-permute-start(bf16[512,1024]{1,0:T(8,128)(2,1)S(1)} %copy-done.40), channel_id=1, source_target_pairs={{0,8},{8,0},{16,24},{24,16},{1,9},{9,1},{17,25},{25,17},{2,10},{10... | collective-permute-start | bytes 3145736 | tf_op jit(solution)/shard_map/ppermute | solution.py:38
  615.4 34.0 %collective-permute-start.40 = (bf16[512,1024]{1,0:T(8,128)(2,1)S(1)}, bf16[512,1024]{1,0:T(8,128)(2,1)S(1)}, u32[]{:S(2)}, u32[]{:S(2)}) collective-permute-start(bf16[512,1024]{1,0:T(8,128)(2,1)S(1)} %copy-done.39), channel_id=1, source_target_pairs={{0,16},{8,24},{16,0},{24,8},{1,17},{9,25},{17,1},{25,9},{2,18},{10... | collective-permute-start | bytes 3145736 | tf_op jit(solution)/shard_map/ppermute | solution.py:38
  659.4 164.8 %reduce-scatter.9.cloned.1.call-start = ((), (), s32[]{:S(2)}) async-start(), calls=%async_computation.9 | async-start | bytes 5308416 | tf_op jit(solution)/shard_map/reduce_scatter | solution.py:787
  666.1 43.6 %collective-permute-start.41 = (bf16[512,2048]{1,0:T(8,128)(2,1)}, bf16[512,2048]{1,0:T(8,128)(2,1)}, u32[]{:S(2)}, u32[]{:S(2)}) collective-permute-start(bf16[512,2048]{1,0:T(8,128)(2,1)} %pad_maximum_fusion.13), channel_id=1, source_target_pairs={{0,16},{8,24},{16,0},{24,8},{1,17},{9,25},{17,1},{25,9},{2,18},{10... | collective-permute-start | bytes 6291464 | tf_op jit(solution)/shard_map/ppermute | solution.py:38
  666.8 43.3 %collective-permute-start.42 = (bf16[512,2048]{1,0:T(8,128)(2,1)}, bf16[512,2048]{1,0:T(8,128)(2,1)}, u32[]{:S(2)}, u32[]{:S(2)}) collective-permute-start(bf16[512,2048]{1,0:T(8,128)(2,1)} %pad_maximum_fusion.14), channel_id=1, source_target_pairs={{0,8},{8,0},{16,24},{24,16},{1,9},{9,1},{17,25},{25,17},{2,10},{10... | collective-permute-start | bytes 6291464 | tf_op jit(solution)/shard_map/ppermute | solution.py:38
  (105 other events, 1278.8 us)
Sparse Core Ops, SparseCore 0:
  27.3 69.5 all-gather.11
  98.5 27.6 all-gather.5
  127.9 81.5 all-gather.7
  210.9 84.9 all-gather.9
  481.9 88.1 reduce-scatter.6
  572.2 87.9 reduce-scatter.4
  662.5 48.3 reduce-scatter.10
  744.6 58.7 reduce-scatter.8

commit v4 on v3

--- a/solution.py
+++ b/solution.py
@@ -86,8 +86,17 @@
         rows = found[0].shape[0]
         for block, p in enumerate(away):
             part = lax.slice_in_dim(new, block * rows, (block + 1) * rows, axis=0)
-            found[p ^ bit] = found[p ^ bit].astype(f32) + part.astype(f32)
+            if step == steps - 1:
+                found[p ^ bit] = (found[p ^ bit], part)
+            else:
+                found[p ^ bit] = found[p ^ bit].astype(f32) + part.astype(f32)
     return came
+
+
+def scatter_sums(state, *first):
+    last = [found[0] for found in state]
+    last = after(last, *first) if first else last
+    return [one.astype(f32) + other.astype(f32) for one, other in last]
 
 
 def scatter_state(pieces):
@@ -105,7 +114,7 @@
     came = ()
     for step in range(parts):
         came = scatter_step(state, axis, count, step, *came)
-    return jnp.concatenate([found[0] for found in state])
+    return jnp.concatenate(scatter_sums(state))
 
 
 def xor_blocks(value, own, count, dim):
@@ -249,14 +258,19 @@
             jax.ShapeDtypeStruct((n_exp, n_ctx, part, 2 * columns + EXTRA), bf16),
         ],
         compiler_params=params(1),
-        cost_estimate=cost(10 * rows * width * columns, 8 * rows * width + 4 * packed.size),
+        cost_estimate=cost(0, 8 * rows * columns),
         name="project_back",
     )(d_projected, packed, tokens, scale, normed, beside)
 
 
+def causal_scores(queries, keys, start):
+    scores = dot(queries, keys, ((1,), (1,))) * HEAD_DIM ** (-0.5)
+    row = lax.broadcasted_iota(jnp.int32, scores.shape, 0) + start
+    return jnp.where(lax.broadcasted_iota(jnp.int32, scores.shape, 1) <= row, scores, masked_value)
+
+
 def attend_kernel(
-    chunk, query_p, key_p, value, stats, scale, cosine, sine, place_col, place_row,
-    attended, query_out, key_out, log_total,
+    chunk, query_p, key_p, value, stats, scale, cosine, sine, attended, query_out, key_out, log_total
 ):
     cos, sin = cosine[...], sine[...]
     scales = scale[0]
@@ -266,18 +280,17 @@
     key_out[...] = keyv
     values = value[...].astype(bf16)
     for start in range(0, query_p.shape[0], chunk):
-        rows = slice(start, start + chunk)
-        scores = dot(query[rows], keyv, ((1,), (1,))) * HEAD_DIM ** (-0.5)
-        scores = jnp.where(place_row[...] <= place_col[rows], scores, masked_value)
+        end = start + chunk
+        scores = causal_scores(query[start:end], keyv[:end], start)
         peak = jnp.max(scores, axis=1, keepdims=True)
         exponent = jnp.exp(scores - peak)
         total = jnp.sum(exponent, axis=1, keepdims=True)
         weights = (exponent * (1.0 / total)).astype(bf16)
-        attended[rows] = dot(weights, values, ((1,), (0,))).astype(bf16)
-        log_total[0, rows] = peak + jnp.log(total)
-
-
-def attend(projected, stats, scales, cosine, sine, places, heads):
+        attended[start:end] = dot(weights, values[:end], ((1,), (0,))).astype(bf16)
+        log_total[0, start:end] = peak + jnp.log(total)
+
+
+def attend(projected, stats, scales, cosine, sine, heads):
     rows = projected.shape[0]
     head = lambda offset: pl.BlockSpec((rows, HEAD_DIM), lambda h: (0, offset + h))
     whole = lambda shape: pl.BlockSpec(shape, lambda h: (0,) * len(shape))
@@ -290,41 +303,39 @@
             whole((rows, 2)),
             pl.BlockSpec((1, 2, HEAD_DIM), lambda h: (h, 0, 0)),
             whole((rows, HEAD_DIM)), whole((rows, HEAD_DIM)),
-            whole((rows, 1)), whole((1, rows)),
         ],
         out_specs=[head(0), head(0), head(0), pl.BlockSpec((1, rows, 1), lambda h: (h, 0, 0))],
         out_shape=[low, low, low, jax.ShapeDtypeStruct((heads, rows, 1), f32)],
         compiler_params=params(1),
         cost_estimate=cost(4 * heads * rows * rows * HEAD_DIM, 24 * low.size // 2, heads * rows * rows),
         name="attend",
-    )(projected, projected, projected, stats, scales, cosine, sine, places[:, None], places[None, :])
+    )(projected, projected, projected, stats, scales, cosine, sine)
 
 
 def attend_back_kernel(
     chunk, query_p, key_p, value, query, keyv, d_attended, log_total, stats, scale, cosine, sine,
-    place_col, place_row, d_query, d_key, d_value, inner_q, inner_k, gains,
+    d_query, d_key, d_value, inner_q, inner_k, gains, value_sum,
 ):
     values = value[...].astype(bf16)
     keys = keyv[...]
-    for start in range(0, query_p.shape[0], chunk):
-        rows = slice(start, start + chunk)
-        queries, pull = query[rows], d_attended[rows]
-        scores = dot(queries, keys, ((1,), (1,))) * HEAD_DIM ** (-0.5)
-        scores = jnp.where(place_row[...] <= place_col[rows], scores, masked_value)
-        probs = jnp.exp(scores - log_total[0, rows])
-        d_probs = dot(pull, values, ((1,), (1,)))
+    length = query_p.shape[0]
+    for start in reversed(range(0, length, chunk)):
+        end = start + chunk
+        queries, pull = query[start:end], d_attended[start:end]
+        probs = jnp.exp(causal_scores(queries, keys[:end], start) - log_total[0, start:end])
+        d_probs = dot(pull, values[:end], ((1,), (1,)))
         inner = jnp.sum(probs * d_probs, axis=1, keepdims=True)
         d_scores = (probs * (d_probs - inner)).astype(bf16)
-        d_query[rows] = dot(d_scores, keys, ((1,), (0,)))
+        d_query[start:end] = dot(d_scores, keys[:end], ((1,), (0,)))
         more_key = dot(d_scores, queries, ((0,), (0,)))
         more_value = dot(probs.astype(bf16), pull, ((0,), (0,)))
-        if start == 0:
+        if end == length:
             d_key[...] = more_key
-            sums = more_value
+            value_sum[...] = more_value
         else:
-            d_key[...] += more_key
-            sums = sums + more_value
-    d_value[...] = sums.astype(bf16)
+            d_key[:end] += more_key
+            value_sum[:end] += more_value
+    d_value[...] = value_sum[...].astype(bf16)
     cos, sin = cosine[...], -sine[...]
     scales = scale[0]
     for index, (grad, before, inner_out) in enumerate(
@@ -337,7 +348,7 @@
         gains[0, index : index + 1] = jnp.sum(moved * stats[:, index : index + 1], axis=0, keepdims=True)
 
 
-def attend_back(projected, query, keyv, d_attended, log_total, stats, scales, cosine, sine, places, heads):
+def attend_back(projected, query, keyv, d_attended, log_total, stats, scales, cosine, sine, heads):
     rows = projected.shape[0]
     head = lambda offset: pl.BlockSpec((rows, HEAD_DIM), lambda h: (0, offset + h))
     whole = lambda shape: pl.BlockSpec(shape, lambda h: (0,) * len(shape))
@@ -351,7 +362,6 @@
             head(0), head(heads), head(2 * heads), head(0), head(0), head(0),
             column, whole((rows, 2)), pair,
             whole((rows, HEAD_DIM)), whole((rows, HEAD_DIM)),
-            whole((rows, 1)), whole((1, rows)),
         ],
         out_specs=[head(0), head(0), head(0), column, column, pair],
         out_shape=[
@@ -362,12 +372,12 @@
             jax.ShapeDtypeStruct((heads, rows, 1), f32),
             jax.ShapeDtypeStruct((heads, 2, HEAD_DIM), f32),
         ],
+        scratch_shapes=[pltpu.VMEM((rows, HEAD_DIM), f32)],
         compiler_params=params(1),
         cost_estimate=cost(0, 8 * rows * HEAD_DIM),
         name="attend_back",
     )(
-        projected, projected, projected, query, keyv, d_attended, log_total, stats, scales,
-        cosine, sine, places[:, None], places[None, :],
+        projected, projected, projected, query, keyv, d_attended, log_total, stats, scales, cosine, sine
     )
 
 
@@ -549,11 +559,29 @@
     part = w_query.shape[0]
 
     def sum_rows(stats):
-        total = stats
-        for k in range(1, n_ctx):
-            came = jnp.split(swap(stats, "context", n_ctx, k), n_ctx, axis=1)
-            total += jnp.concatenate([came[j ^ k] for j in range(n_ctx)], axis=1)
-        return total
+        flat = stats.reshape(-1, 128)
+        return (flat + sum(swap(flat, "context", n_ctx, k) for k in range(1, n_ctx))).reshape(stats.shape)
+
+    run = tokens // 2
+    runs = positions[0].reshape(n_ctx, 2, run)[:, :, 0] // run
+    runs = [
+        [lax.dynamic_index_in_dim(runs[:, j], own_ctx ^ k, keepdims=False) for j in range(2)]
+        for k in range(n_ctx)
+    ]
+
+    def in_sequence(pieces):
+        whole = jnp.zeros((2 * n_ctx, run, width), pieces[0].dtype)
+        for piece, (first, second) in zip(pieces, runs):
+            whole = lax.dynamic_update_index_in_dim(whole, piece[:run], first, 0)
+            whole = lax.dynamic_update_index_in_dim(whole, piece[run:], second, 0)
+        return whole.reshape(sequence, width)
+
+    def per_device(rows):
+        view = rows.reshape(2 * n_ctx, run, width)
+        return [
+            jnp.concatenate([lax.dynamic_index_in_dim(view, at, keepdims=False) for at in pair])
+            for pair in runs
+        ]
 
     small = jnp.concatenate(
         [attn_gain[:, None], moe_gain[:, None], query_gain[:, None], key_gain[:, None], router], axis=1
@@ -577,7 +605,7 @@
     key_scale = lax.dynamic_slice_in_dim(small_rows[3], own_ctx * columns, columns)
     router_full = jnp.pad(small_full[:, 4 : 4 + experts], ((0, 0), (0, EXTRA - experts)))
 
-    inputs = jnp.concatenate(gather_direct(own_rows, "context", n_ctx))
+    inputs = in_sequence(gather_direct(own_rows, "context", n_ctx))
     places = xor_blocks(positions[0], own_ctx, n_ctx, 0)
     named = jnp.sum(
         (routes[0][:, :, None] == jnp.arange(experts, dtype=jnp.int32)[None, None, :]).astype(f32), axis=1
@@ -600,14 +628,12 @@
     query_p, key_p = projected[:, :columns], projected[:, columns : 2 * columns]
     squares = sum_rows(after(squares, down_came))
     r_both = lax.rsqrt(squares / width + epsilon)
-    down_came = [
-        gather_step(downs[0], "context", n_ctx, r_both if step == 0 else ()) for step in range(steps - 1)
-    ]
+    down_came = [gather_step(downs[0], "context", n_ctx, r_both) for _ in range(steps - 1)]
     query_r, key_r = r_both[0][:, None], r_both[1][:, None]
     frequency = jnp.exp(
         jnp.arange(HEAD_DIM // 2, dtype=f32) * (-2.0 * math.log(rope_base) / HEAD_DIM)
     )
-    angles = places.astype(f32)[:, None] * frequency[None, :]
+    angles = jnp.arange(sequence, dtype=f32)[:, None] * frequency[None, :]
     cosine, sine = jnp.cos(angles), jnp.sin(angles)
     cosine, sine = jnp.concatenate([cosine, cosine], 1), jnp.concatenate([-sine, sine], 1)
     stats = r_both.T
@@ -615,11 +641,11 @@
         [query_scale.reshape(heads, HEAD_DIM), key_scale.reshape(heads, HEAD_DIM)], axis=1
     )
     attended, query, keyv, log_total = attend(
-        projected, stats, scales, cosine, sine, places, heads
+        projected, stats, scales, cosine, sine, heads
     )
     branch = dot(attended, w_out, ((1,), (0,))).astype(bf16)
     branch = after(branch, down_came)
-    branch_own = scatter_xor(jnp.split(branch, n_ctx), "context", n_ctx)
+    branch_own = scatter_xor(per_device(branch), "context", n_ctx)
     middle = own_rows.astype(f32) + branch_own
     middle_r = inverse_rms(middle)
     mixed_own = (middle * middle_r * moe_scale).astype(bf16)
@@ -630,7 +656,7 @@
     beside = jnp.concatenate([probs_high, probs_low, named.astype(bf16)], axis=1)
     beside = jnp.pad(beside, ((0, 0), (0, EXTRA - beside.shape[1])))
     mixed_own = jnp.concatenate([xor_blocks(mixed_own, own_ctx, n_ctx, 1), beside], axis=1)
-    mixed_wide = lax.all_gather(after(mixed_own, pull), "expert", axis=0, tiled=True)
+    mixed_wide = lax.all_gather(mixed_own, "expert", axis=0, tiled=True)
 
     own = own_ctx.astype(jnp.int32)[None]
     weights, first_came = [], []
@@ -665,7 +691,7 @@
         return [lax.dynamic_slice_in_dim(grad, (own_ctx ^ k) * rows, rows, 0) for k in range(n_ctx)]
 
     def sums_of(state):
-        return [found[0] for found in state]
+        return scatter_sums(state, last_came)
 
     ff = back.shape[1]
     backs, down_w = [back], [down]
@@ -707,8 +733,8 @@
     out_part = combine(after(hidden_g, raw, pair_came), down_w)
     out_part = after(out_part, last_came)
     out_own = lax.psum_scatter(out_part, "expert", scatter_dimension=0, tiled=True).astype(f32)
-    d_mixed = after(d_mixed, out_part)
-    g_router = xor_blocks(dot(mixed, d_logits, ((0,), (0,)))[:, :experts], own_ctx, n_ctx, 0)
+    g_router = dot(mixed, d_logits, ((0,), (0,)))
+    d_mixed = after(d_mixed, out_part, g_router)
 
     scaled = d_mixed * moe_scale
     g_moe = jnp.sum(d_mixed * middle * middle_r, axis=0)
@@ -726,30 +752,28 @@
             down_raw.append(weight_grad(after(hidden_g[step], d_middle, *came), pull))
         if step < steps:
             came = gather_step(state, "context", n_ctx)
-    d_branch = jnp.concatenate(
+    parts = gathered(state)
+    d_branch = in_sequence(
         [
-            lax.slice_in_dim(array, block * rows, (block + 1) * rows, axis=0)
-            for parts in zip(*gathered(state))
-            for array, block, rows in parts
+            jnp.concatenate([array[block * rows : (block + 1) * rows] for array, block, rows in own])
+            for own in zip(*parts)
         ]
     )
     d_branch = after(d_branch, down_raw)
+    downs = [scatter_state(row_parts(owner_rows(grad), steps)) for grad in down_raw]
     last_came = [
         scatter_step(pairs[-1], "context", n_ctx, step, d_branch) for step in range(1, steps)
     ]
-    down_sums = scatter_state([owner_rows(grad) for grad in down_raw])
-    down_came = scatter_step(down_sums, "context", n_ctx, 0, last_came)
 
     d_attended = dot(d_branch, w_out, ((1,), (1,))).astype(bf16)
     d_query, d_key, d_value, inner_q, inner_k, g_heads = attend_back(
-        projected, query, keyv, d_attended, log_total, stats, scales, cosine, sine, places, heads
+        projected, query, keyv, d_attended, log_total, stats, scales, cosine, sine, heads
     )
     result = (middle + after(out_own, d_query)).astype(bf16)
     inner_q, inner_k = jnp.sum(inner_q[:, :, 0], axis=0), jnp.sum(inner_k[:, :, 0], axis=0)
-    g_side = side_grads(normed, after(d_value, last_came), attended, d_branch, n_exp, n_ctx).reshape(width, 2 * columns)
-    g_side = lax.psum_scatter(g_side, "expert", scatter_dimension=0, tiled=True)
-    inner_both = jnp.stack([inner_q, inner_k])
-    inner_both = sum_rows(after(inner_both, down_came)) / width
+    inner_both = after(jnp.stack([inner_q, inner_k]), last_came)
+    inner_both = sum_rows(inner_both) / width
+    g_side = side_grads(normed, after(d_value, inner_both), attended, d_branch, n_exp, n_ctx)
     g_heads = g_heads.transpose(1, 0, 2).reshape(2, columns)
     d_query_p = query_r * (query_scale * d_query) - query_p * (query_r**3 * inner_both[0][:, None])
     d_key_p = key_r * (key_scale * d_key) - key_p * (key_r**3 * inner_both[1][:, None])
@@ -759,13 +783,23 @@
     spread = lax.dynamic_update_slice(
         jnp.zeros((2, width), f32), g_heads, (jnp.zeros_like(own_ctx), own_ctx * columns)
     )
+    g_router = xor_blocks(g_router[:, :experts], own_ctx, n_ctx, 0)
     beside = jnp.concatenate([jnp.zeros((width, 1), f32), g_moe[:, None], spread.T, g_router], axis=1)
     beside = jnp.pad(beside, ((0, 0), (0, EXTRA - beside.shape[1])))
+    g_side_sum = lax.psum_scatter(g_side.reshape(width, 2 * columns), "expert", scatter_dimension=0, tiled=True)
+    down_came = [scatter_step(downs[0], "context", n_ctx, 0, inner_both)]
+    d_projected = after(d_projected, g_side)
     d_normed_part, g_packed = project_back(d_projected, packed, inputs, input_r, normed, beside)
-    down_came = [
-        scatter_step(down_sums, "context", n_ctx, step, inner_both) for step in range(1, steps)
-    ]
-    d_normed = scatter_xor(jnp.split(after(d_normed_part, down_came), n_ctx), "context", n_ctx)
+    g_packed = after(g_packed, down_came)
+    d_normed = scatter_state(row_parts(per_device(d_normed_part), steps))
+    last_came = scatter_step(d_normed, "context", n_ctx, 0)
+    for down in downs[1:]:
+        scatter_step(down, "context", n_ctx, 0, *down_came)
+    for step in range(1, steps):
+        scatter_step(d_normed, "context", n_ctx, step)
+        for down in downs:
+            scatter_step(down, "context", n_ctx, step)
+    d_normed = jnp.concatenate(scatter_sums(d_normed))
     own_in = own_rows.astype(f32)
     own_r = inverse_rms(own_in)
     scaled_in = d_normed * attn_scale
@@ -784,15 +818,16 @@
         return grads.transpose(1, 0, 2).reshape(part, width)
 
     g_packed = g_packed.reshape(width, 2 * columns + EXTRA)
-    g_packed = to_owners(lax.psum_scatter(g_packed, "expert", scatter_dimension=0, tiled=True))
-    g_small = jnp.sum(g_packed[:, :, 2 * columns :], axis=0)
+    g_packed = lax.psum_scatter(g_packed, "expert", scatter_dimension=0, tiled=True)
+    g_packed = to_owners(jnp.concatenate([g_packed, g_side_sum[:, :columns]], axis=1))
+    g_small = jnp.sum(g_packed[:, :, 2 * columns : 2 * columns + EXTRA], axis=0)
     return (
         result[None],
         input_grad[None],
         full_rows(g_packed[:, :, :columns]),
         full_rows(g_packed[:, :, columns : 2 * columns]),
-        full_rows(to_owners(g_side[:, :columns])),
-        full_rows(g_side[:, columns:].astype(f32).reshape(n_ctx, part, columns)),
+        full_rows(g_packed[:, :, 2 * columns + EXTRA :]),
+        full_rows(g_side_sum[:, columns:].astype(f32).reshape(n_ctx, part, columns)),
         g_small[:, 4 : 4 + experts],
         g_small[:, 0],
         g_small[:, 2],
@@ -800,7 +835,7 @@
         g_small[:, 1],
         jnp.stack([sums_of(pair)[0] for pair in pairs]),
         jnp.stack([sums_of(pair)[1] for pair in pairs]),
-        jnp.stack(sums_of(down_sums)),
+        jnp.stack([jnp.concatenate(sums_of(down)) for down in downs]),
     )
 
 

time: 857 us -> 805 us (0.939); the launches traced: 844 us -> 801 us
  waiting for transfers between devices: 277 us -> 215 us
  between operations: 15.8 us -> 31.3 us
  local copies, waits for them, and re-layouts: 53.1 us -> 66.4 us
  Pallas kernels: 247 us -> 235 us
    ppermute x58 -> x59, waiting for transfers between devices: 265 us -> 215 us  [swap(): return lax.ppermute(value, axis, [(i, i ^ bit) for i in range(count)])]
    add x2 -> x4, other arithmetic: 1.01 us -> 15.3 us  [scatter_step(): found[p ^ bit] = found[p ^ bit].astype(f32) + part.astype(f32)]
    convert_element_type x8 -> x4, other arithmetic: 16.2 us -> 3.67 us  [scatter_step(): send = [found.pop(p).astype(bf16) for p in away]]
    dynamic_update_slice x0 -> x16, local copies, waits for them, and re-layouts: none -> 11.2 us  [the longest x8 5.61 us: in_sequence(): whole = lax.dynamic_update_index_in_dim(whole, piece[:run], first, 0)]
    all_gather x1, waiting for transfers between devices: 10.3 us -> 0.01 us  [shards(): lax.all_gather(after(cotangent[0], down_came), 'expert', axis=0, tiled=True)]
    pallas_call x1, Pallas kernels: 29.3 us -> 19.6 us  [attend_back(): pl.pallas_call(lambda *refs: attend_back_kernel(min(256, rows), *refs), g...]
    ppermute x58 -> x59, starting transfers between devices: 68 us -> 66.4 us  [swap(): return lax.ppermute(value, axis, [(i, i ^ bit) for i in range(count)])]
  transfers between devices with their start and end apart: 66 -> 67, of which waited for: 36 -> 29; matrix products, arithmetic and copies ran while one was open for 25% -> 28% of each run, Pallas kernels for 29% -> 29%
where the time goes in v4:
time: 805 us; the launch traced here: 801 us
  Pallas kernels  235 us (29%)
  waiting for transfers between devices  215 us (27%)
  other arithmetic  98.5 us (12%)
  matrix products  87.8 us (11%)
  starting transfers between devices  67.2 us (8%)
  local copies, waits for them, and re-layouts  66.4 us (8%)
  between operations  31.3 us (4%)
    ppermute x59, waiting for transfers between devices, swap(): return lax.ppermute(value, axis, [(i, i ^ bit) for i in range(count)])  215 us
    dot_general x10, matrix products, dot(): lax.dot_general(left, right, (dims, ((), ())), preferred_element_type=f32)  87.8 us
    ppermute x59, starting transfers between devices, swap(): return lax.ppermute(value, axis, [(i, i ^ bit) for i in range(count)])  66.4 us
    pallas_call x2, Pallas kernels, run_experts(): pl.pallas_call(lambda *refs: experts_kernel(e, len(gate_k), *refs), grid=...  55.9 us
    pallas_call x1, Pallas kernels, rows_back(): pl.pallas_call(lambda *refs: rows_back_kernel(count, n_ctx, *refs), grid=...  47 us
    pallas_call x2, Pallas kernels, pull_down(): pl.pallas_call(lambda *refs: pull_down_kernel(places, *refs), grid=(rows...  28.9 us
    pallas_call x1, Pallas kernels, combine(): pl.pallas_call(lambda *refs: combine_kernel(count, *refs), grid=(rows //...  23.6 us
    unnamed x155, local copies, waits for them, and re-layouts  22.2 us
  transfers between devices with their start and end apart: 67, of which 29 were waited for; matrix products, arithmetic and copies ran while one was open for 28% of the time, Pallas kernels for 29%

profile of v4, /device:TPU:0, one launch (start us, length us, event | category | flops | bytes accessed | tf_op | source)
XLA Modules:
  0.0 800.9 jit_solution(9602720395731873388)
XLA Ops:
  16.4 4.5 collective-permute-done.3
  20.9 5.2 collective-permute-done.4
  55.4 19.8 %collective-permute-done.1 = bf16[256,2048]{1,0:T(8,128)(2,1)} collective-permute-done((bf16[256,2048]{1,0:T(8,128)(2,1)S(1)}, bf16[256,2048]{1,0:T(8,128)(2,1)}, u32[]{:S(2)}, u32[]{:S(2)}) %collective-permute-start.1) | collective-permute-done | bytes 1048608 | tf_op jit(solution)/shard_map/ppermute | solution.py:38
  85.4 8.6 %collective-permute-done.6.refs_3_ = bf16[128,2048]{1,0:T(8,128)(2,1)S(1)} collective-permute-done((bf16[128,2048]{1,0:T(8,128)(2,1)S(1)}, bf16[128,2048]{1,0:T(8,128)(2,1)S(1)}, u32[]{:S(2)}, u32[]{:S(2)}) %collective-permute-start.6) | collective-permute-done | bytes 524320 | tf_op jit(solution)/shard_map/ppermute | solution.py:38
  108.0 16.0 %project.1 = (f32[1024,1536]{1,0:T(8,128)}, bf16[1024,2048]{1,0:T(8,128)(2,1)}, f32[2,1024]{1,0:T(2,128)}) custom-call(bf16[1024,2048]{1,0:T(8,128)(2,1)} %bitcast.17.refs_0_.refs_2_, f32[1024,1]{1,0:T(8,128)} %copy.144.refs_1_.refs_3_, f32[1,2048]{1,0:T(1,128)} %get-tuple-element.360.refs_2_, bf16[8,4,64,1664]{3,2,1,0:T(8,128)(2,1)} %bitcast.251), custom_call_target="tpu_custom_call" | custom-call | flops 6442450944 | bytes 21495808 | tf_op jit(solution)/shard_map/project/pallas_call | solution.py:172
  136.6 15.1 %attend.1 = (bf16[1024,512]{1,0:T(8,128)(2,1)}, bf16[1024,512]{1,0:T(8,128)(2,1)}, bf16[1024,512]{1,0:T(8,128)(2,1)}, f32[4,1024,1]{2,1,0:T(8,128)}) custom-call(f32[1024,1536]{1,0:T(8,128)} %get-tuple-element.101.refs_0_.refs_1_.refs_2_, f32[1024,1536]{1,0:T(8,128)} %get-tuple-element.101.refs_0_.refs_1_.refs_2_, ...), custom_call_target="tpu_custom_call" | custom-call | flops 2147483648 | bytes 6291456 | tf_op jit(solution)/shard_map/attend/pallas_call | solution.py:298
  159.5 17.8 %collective-permute-done.15 = bf16[256,2048]{1,0:T(8,128)(2,1)S(1)} collective-permute-done((bf16[256,2048]{1,0:T(8,128)(2,1)S(1)}, bf16[256,2048]{1,0:T(8,128)(2,1)S(1)}, u32[]{:S(2)}, u32[]{:S(2)}) %collective-permute-start.15) | collective-permute-done | bytes 1048608 | tf_op jit(solution)/shard_map/ppermute | solution.py:38
  181.2 8.8 %collective-permute-done.17 = bf16[128,2048]{1,0:T(8,128)(2,1)S(1)} collective-permute-done((bf16[128,2048]{1,0:T(8,128)(2,1)S(1)}, bf16[128,2048]{1,0:T(8,128)(2,1)S(1)}, u32[]{:S(2)}, u32[]{:S(2)}) %collective-permute-start.17) | collective-permute-done | bytes 524320 | tf_op jit(solution)/shard_map/ppermute | solution.py:38
  201.1 18.4 %collective-permute-done.21.refs_9_.refs_8_ = bf16[512,1024]{1,0:T(8,128)(2,1)S(1)} collective-permute-done((bf16[512,1024]{1,0:T(8,128)(2,1)S(1)}, bf16[512,1024]{1,0:T(8,128)(2,1)S(1)}, u32[]{:S(2)}, u32[]{:S(2)}) %collective-permute-start.21) | collective-permute-done | bytes 1048608 | tf_op jit(solution)/shard_map/ppermute | solution.py:38
  227.8 14.7 %pull_down.2 = (f32[2048,1024]{1,0:T(8,128)}, bf16[1024,2048]{1,0:T(8,128)(2,1)}) custom-call(s32[1]{0:T(128)} %bitcast.51.refs_0_, bf16[2048,2048]{1,0:T(8,128)(2,1)} %all-gather.10.cloned.1.call-done.refs_1_, bf16[128,2048]{1,0:T(8,128)(2,1)} %copy-done.34, bf16[128,2048]{1,0:T(8,128)(2,1)} %copy-done.48, ...), custom_call_target="tpu_custom_call" | custom-call | flops 8589934592 | bytes 25165824 | tf_op jit(solution)/shard_map/pull_down/pallas_call | solution.py:412
  242.5 22.5 %collective-permute-done.22.refs_8_.refs_10_.refs_7_.refs_9_ = bf16[1024,1024]{1,0:T(8,128)(2,1)} collective-permute-done((bf16[1024,1024]{1,0:T(8,128)(2,1)}, bf16[1024,1024]{1,0:T(8,128)(2,1)}, u32[]{:S(2)}, u32[]{:S(2)}) %collective-permute-start.22) | collective-permute-done | bytes 2097184 | tf_op jit(solution)/shard_map/ppermute | solution.py:38
  275.1 17.4 %collective-permute-done.24.refs_9_.refs_16_ = bf16[512,1024]{1,0:T(8,128)(2,1)} collective-permute-done((bf16[512,1024]{1,0:T(8,128)(2,1)S(1)}, bf16[512,1024]{1,0:T(8,128)(2,1)}, u32[]{:S(2)}, u32[]{:S(2)}) %collective-permute-start.24) | collective-permute-done | bytes 1048608 | tf_op jit(solution)/shard_map/ppermute | solution.py:38
  305.8 27.9 %expert.2 = (bf16[2048,1024]{1,0:T(8,128)(2,1)}, bf16[2048,2048]{1,0:T(8,128)(2,1)}, f32[2048,1]{1,0:T(8,128)}) custom-call(bf16[2048,2176]{1,0:T(8,128)(2,1)} %all-gather.8.cloned.1.call-done.refs_0_, f32[2048,1024]{1,0:T(8,128)} %get-tuple-element.115.refs_1_, f32[2048,2]{1,0:T(8,128)} %dynamic-slice_multiply_fusion.refs_2_, bf16[512,1024]{1,0:T(8,128)(2,1)} %copy-done.7, ...), custom_call_target="tpu_custom_call" | custom-call | flops 17179869184 | bytes 37748736 | tf_op jit(solution)/shard_map/expert/pallas_call | solution.py:453
  333.7 12.7 %fusion.14 = bf16[2048,1024]{1,0:T(8,128)(2,1)S(1)} fusion(bf16[2048,2048]{1,0:T(8,128)(2,1)} %get-tuple-element.124.refs_0_, bf16[2048,2176]{1,0:T(8,128)(2,1)} %all-gather.8.cloned.1.call-done.refs_0_), kind=kOutput, calls=%fused_computation.18 | convolution fusion | flops 8592031744 | bytes 16777216 | tf_op jit(solution)/shard_map/dot_general | solution.py:24
  349.1 14.2 %pull_down.3 = (f32[2048,1024]{1,0:T(8,128)}, bf16[1024,2048]{1,0:T(8,128)(2,1)}) custom-call(s32[1]{0:T(128)} %bitcast.51.refs_0_, bf16[2048,2048]{1,0:T(8,128)(2,1)} %all-gather.10.cloned.1.call-done.refs_1_, bf16[128,2048]{1,0:T(8,128)(2,1)} %get-tuple-element.103.refs_2_, bf16[128,2048]{1,0:T(8,128)(2,1)} %collective-permute-done.8.refs_3_, ...), custom_call_target="tpu_custom_call" | custom-call | flops 8589934592 | bytes 25165824 | tf_op jit(solution)/shard_map/pull_down/pallas_call | solution.py:412
  363.4 12.7 %fusion.19 = bf16[2048,1024]{1,0:T(8,128)(2,1)S(1)} fusion(bf16[2048,2048]{1,0:T(8,128)(2,1)} %get-tuple-element.124.refs_0_, bf16[2048,2176]{1,0:T(8,128)(2,1)} %all-gather.8.cloned.1.call-done.refs_0_), kind=kOutput, calls=%fused_computation.19 | convolution fusion | flops 8592031744 | bytes 16777216 | tf_op jit(solution)/shard_map/dot_general | solution.py:24
  379.6 28.0 %expert.3 = (bf16[2048,1024]{1,0:T(8,128)(2,1)}, bf16[2048,2048]{1,0:T(8,128)(2,1)}, f32[2048,1]{1,0:T(8,128)}) custom-call(bf16[2048,2176]{1,0:T(8,128)(2,1)} %all-gather.8.cloned.1.call-done.refs_0_, f32[2048,1024]{1,0:T(8,128)} %get-tuple-element.128.refs_1_, f32[2048,2]{1,0:T(8,128)} %dynamic-slice_multiply_fusion.refs_2_, bf16[512,1024]{1,0:T(8,128)(2,1)} %copy-done.6, ...), custom_call_target="tpu_custom_call" | custom-call | flops 17179869184 | bytes 37748736 | tf_op jit(solution)/shard_map/expert/pallas_call | solution.py:453
  413.0 47.0 %rows_back.1 = bf16[2048,2048]{1,0:T(8,128)(2,1)} custom-call(bf16[2048,2048]{1,0:T(8,128)(2,1)} %get-tuple-element.124.refs_0_, bf16[2048,2048]{1,0:T(8,128)(2,1)} %get-tuple-element.135.refs_1_, bf16[512,1024]{1,0:T(8,128)(2,1)} %copy-done.7, bf16[512,1024]{1,0:T(8,128)(2,1)} %copy-done.24, ...), custom_call_target="tpu_custom_call" | custom-call | bytes 2097152 | tf_op jit(solution)/shard_map/rows_back/pallas_call | solution.py:515
  460.1 4.6 convert_add_fusion.3
  472.4 13.2 %fusion.29 = bf16[2048,1024]{1,0:T(8,128)(2,1)S(1)} fusion(bf16[2048,2048]{1,0:T(8,128)(2,1)} %get-tuple-element.135.refs_1_, bf16[2048,2176]{1,0:T(8,128)(2,1)} %all-gather.8.cloned.1.call-done.refs_0_), kind=kOutput, calls=%fused_computation.21 | convolution fusion | flops 8592031744 | bytes 16777216 | tf_op jit(solution)/shard_map/dot_general | solution.py:24
  485.7 12.9 %fusion.24 = bf16[2048,1024]{1,0:T(8,128)(2,1)S(1)} fusion(bf16[2048,2048]{1,0:T(8,128)(2,1)S(1)} %bitcast.246, bf16[2048,2176]{1,0:T(8,128)(2,1)} %all-gather.8.cloned.1.call-done.refs_0_), kind=kOutput, calls=%fused_computation.20 | convolution fusion | flops 8592031744 | bytes 16777216 | tf_op jit(solution)/shard_map/dot_general | solution.py:24
  505.2 23.6 %combine.1 = bf16[2048,2048]{1,0:T(8,128)(2,1)} custom-call(bf16[2048,1024]{1,0:T(8,128)(2,1)} %get-tuple-element.148.refs_0_, bf16[2048,1024]{1,0:T(8,128)(2,1)} %get-tuple-element.149.refs_1_, bf16[1024,2048]{1,0:T(8,128)(2,1)} %get-tuple-element.140.refs_2_, bf16[1024,2048]{1,0:T(8,128)(2,1)} %get-tuple-element.141.refs_3_), custom_call_target="tpu_custom_call" | custom-call | flops 17179869184 | bytes 25165824 | tf_op jit(solution)/shard_map/combine/pallas_call | solution.py:481
  528.8 17.7 %collective-permute-done.33 = bf16[1024,1024]{1,0:T(8,128)(2,1)S(1)} collective-permute-done((bf16[1024,1024]{1,0:T(8,128)(2,1)}, bf16[1024,1024]{1,0:T(8,128)(2,1)S(1)}, u32[]{:S(2)}, u32[]{:S(2)}) %collective-permute-start.33) | collective-permute-done | bytes 2097184 | tf_op jit(solution)/shard_map/ppermute | solution.py:38
  548.2 6.0 fusion
  569.8 11.0 %convolution_convert_fusion.1 = bf16[1024,2048]{1,0:T(8,128)(2,1)} fusion(bf16[2048,1024]{1,0:T(8,128)(2,1)S(1)} %copy-done.67, bf16[2048,2048]{1,0:T(8,128)(2,1)S(1)} %bitcast.302), kind=kOutput, calls=%fused_computation.23 | convolution fusion | flops 8592031744 | bytes 16777216 | tf_op jit(solution)/shard_map/dot_general | solution.py:24
  583.8 11.0 %convolution_convert_fusion = bf16[1024,2048]{1,0:T(8,128)(2,1)} fusion(bf16[2048,1024]{1,0:T(8,128)(2,1)S(1)} %copy-done.68, bf16[2048,2048]{1,0:T(8,128)(2,1)S(1)} %bitcast.302), kind=kOutput, calls=%fused_computation.22 | convolution fusion | flops 8592031744 | bytes 16777216 | tf_op jit(solution)/shard_map/dot_general | solution.py:24
  594.9 10.5 %collective-permute-done.37 = bf16[256,2048]{1,0:T(8,128)(2,1)S(1)} collective-permute-done((bf16[256,2048]{1,0:T(8,128)(2,1)S(1)}, bf16[256,2048]{1,0:T(8,128)(2,1)S(1)}, u32[]{:S(2)}, u32[]{:S(2)}) %collective-permute-start.37) | collective-permute-done | bytes 1048608 | tf_op jit(solution)/shard_map/ppermute | solution.py:38
  611.2 19.6 %attend_back.1 = (f32[1024,512]{1,0:T(8,128)}, f32[1024,512]{1,0:T(8,128)}, bf16[1024,512]{1,0:T(8,128)(2,1)}, f32[4,1024,1]{2,1,0:T(8,128)}, f32[4,1024,1]{2,1,0:T(8,128)}, /*index=5*/f32[4,2,128]{2,1,0:T(2,128)}) custom-call(f32[1024,1536]{1,0:T(8,128)} %get-tuple-element.101.refs_0_.refs_1_.refs_2_, ...), custom_call_target="tpu_custom_call" | custom-call | bytes 1048576 | tf_op jit(solution)/shard_map/attend_back/pallas_call | solution.py:358
  641.0 9.2 %side_grads.1 = bf16[8,4,64,1024]{3,2,1,0:T(8,128)(2,1)} custom-call(bf16[1024,2048]{1,0:T(8,128)(2,1)} %get-tuple-element.161.refs_0_.refs_4_, bf16[1024,512]{1,0:T(8,128)(2,1)} %get-tuple-element.162.refs_1_, bf16[1024,512]{1,0:T(8,128)(2,1)} %get-tuple-element.106.refs_2_, bf16[1024,2048]{1,0:T(8,128)(2,1)} %bitcast.262), custom_call_target="tpu_custom_call" | custom-call | flops 4294967296 | bytes 12582912 | tf_op jit(solution)/shard_map/side_grads/pallas_call | solution.py:211
  667.5 19.6 %project_back.1 = (bf16[1024,2048]{1,0:T(8,128)(2,1)}, bf16[8,4,64,1152]{3,2,1,0:T(8,128)(2,1)}) custom-call(bf16[1024,1536]{1,0:T(8,128)(2,1)} %pad_maximum_fusion.3.refs_0_, bf16[8,4,64,1664]{3,2,1,0:T(8,128)(2,1)} %bitcast.252, bf16[1024,2048]{1,0:T(8,128)(2,1)} %bitcast.17.refs_0_.refs_2_, f32[1024,1]{1,0:T(8,128)} %copy.144.refs_1_.refs_3_, ...), custom_call_target="tpu_custom_call" | custom-call | bytes 4194304 | tf_op jit(solution)/shard_map/project_back/pallas_call | solution.py:241
  703.8 14.7 %collective-permute-done.46 = bf16[256,2048]{1,0:T(8,128)(2,1)} collective-permute-done((bf16[256,2048]{1,0:T(8,128)(2,1)}, bf16[256,2048]{1,0:T(8,128)(2,1)}, u32[]{:S(2)}, u32[]{:S(2)}) %collective-permute-start.46) | collective-permute-done | bytes 1048608 | tf_op jit(solution)/shard_map/ppermute | solution.py:38
  731.2 23.0 %collective-permute-done.45 = bf16[128,2048]{1,0:T(8,128)(2,1)S(1)} collective-permute-done((bf16[128,2048]{1,0:T(8,128)(2,1)S(1)}, bf16[128,2048]{1,0:T(8,128)(2,1)S(1)}, u32[]{:S(2)}, u32[]{:S(2)}) %collective-permute-start.45) | collective-permute-done | bytes 524320 | tf_op jit(solution)/shard_map/ppermute | solution.py:38
  (452 shorter events, 261.8 us)
Async XLA Ops:
  7.2 98.7 %all-gather.12.cloned.1.call-start = ((), (), s32[]{:S(2)}) async-start(), calls=%async_computation.11 | async-start | bytes 7667712 | tf_op jit(solution)/shard_map/all_gather | solution.py:600
  27.4 124.3 %all-gather.6.cloned.1.call-start = ((), (), s32[]{:S(2)}) async-start(), calls=%async_computation.4 | async-start | bytes 2359296 | tf_op jit(solution)/shard_map/all_gather | solution.py:613
  28.9 46.3 %collective-permute-start.1 = (bf16[256,2048]{1,0:T(8,128)(2,1)S(1)}, bf16[256,2048]{1,0:T(8,128)(2,1)}, u32[]{:S(2)}, u32[]{:S(2)}) collective-permute-start(bf16[256,2048]{1,0:T(8,128)(2,1)S(1)} %bitcast.243), channel_id=1, source_target_pairs={{0,16},{8,24},{16,0},{24,8},{1,17},{9,25},{17,1},{25,9},{2,18},{10... | collective-permute-start | bytes 3145736 | tf_op jit(solution)/shard_map/ppermute | solution.py:38
  29.7 49.3 %collective-permute-start.2 = (bf16[256,2048]{1,0:T(8,128)(2,1)S(1)}, bf16[256,2048]{1,0:T(8,128)(2,1)}, u32[]{:S(2)}, u32[]{:S(2)}) collective-permute-start(bf16[256,2048]{1,0:T(8,128)(2,1)S(1)} %bitcast.244), channel_id=1, source_target_pairs={{0,24},{8,16},{16,8},{24,0},{1,25},{9,17},{17,9},{25,1},{2,26},{10... | collective-permute-start | bytes 3145736 | tf_op jit(solution)/shard_map/ppermute | solution.py:38
  82.8 145.0 %all-gather.10.cloned.1.call-start = ((), (), s32[]{:S(2)}) async-start(), calls=%async_computation.6 | async-start | bytes 9437184 | tf_op jit(solution)/shard_map/all_gather | solution.py:624
  95.7 206.8 %all-gather.8.cloned.1.call-start = ((), (), s32[]{:S(2)}) async-start(), calls=%async_computation.5 | async-start | bytes 10027008 | tf_op jit(solution)/shard_map/all_gather | solution.py:659
  196.9 364.1 %reduce-scatter.7.cloned.1.call-start = ((), (), s32[]{:S(2)}) async-start(), calls=%async_computation.8 | async-start | bytes 9437184 | tf_op jit(solution)/shard_map/reduce_scatter | solution.py:727
  221.2 43.8 %collective-permute-start.22 = (bf16[1024,1024]{1,0:T(8,128)(2,1)}, bf16[1024,1024]{1,0:T(8,128)(2,1)}, u32[]{:S(2)}, u32[]{:S(2)}) collective-permute-start(bf16[1024,1024]{1,0:T(8,128)(2,1)} %pad_maximum_fusion.6), channel_id=1, source_target_pairs={{0,8},{8,0},{16,24},{24,16},{1,9},{9,1},{17,25},{25,17},{2,10},{10... | collective-permute-start | bytes 6291464 | tf_op jit(solution)/shard_map/ppermute | solution.py:38
  225.2 40.0 %collective-permute-start.20 = (bf16[1024,1024]{1,0:T(8,128)(2,1)}, bf16[1024,1024]{1,0:T(8,128)(2,1)}, u32[]{:S(2)}, u32[]{:S(2)}) collective-permute-start(bf16[1024,1024]{1,0:T(8,128)(2,1)} %pad_maximum_fusion.5), channel_id=1, source_target_pairs={{0,16},{8,24},{16,0},{24,8},{1,17},{9,25},{17,1},{25,9},{2,18},{10... | collective-permute-start | bytes 6291464 | tf_op jit(solution)/shard_map/ppermute | solution.py:38
  268.3 29.4 %collective-permute-start.23 = (bf16[512,1024]{1,0:T(8,128)(2,1)S(1)}, bf16[512,1024]{1,0:T(8,128)(2,1)}, u32[]{:S(2)}, u32[]{:S(2)}) collective-permute-start(bf16[512,1024]{1,0:T(8,128)(2,1)S(1)} %get-tuple-element.122.refs_3_.refs_10_), channel_id=1, source_target_pairs={{0,8},{8,0},{16,24},{24,16},{1,9},{9,1},{17,25},{25,17},{2,10},{10... | collective-permute-start | bytes 3145736 | tf_op jit(solution)/shard_map/ppermute | solution.py:38
  275.1 74.1 %collective-permute-start.26 = (bf16[256,2048]{1,0:T(8,128)(2,1)}, bf16[256,2048]{1,0:T(8,128)(2,1)}, u32[]{:S(2)}, u32[]{:S(2)}) collective-permute-start(bf16[256,2048]{1,0:T(8,128)(2,1)} %get-tuple-element.127), channel_id=1, source_target_pairs={{0,8},{8,0},{16,24},{24,16},{1,9},{9,1},{17,25},{25,17},{2,10},{10... | collective-permute-start | bytes 3145736 | tf_op jit(solution)/shard_map/ppermute | solution.py:38
  275.1 74.1 %collective-permute-start.25 = (bf16[256,2048]{1,0:T(8,128)(2,1)}, bf16[256,2048]{1,0:T(8,128)(2,1)}, u32[]{:S(2)}, u32[]{:S(2)}) collective-permute-start(bf16[256,2048]{1,0:T(8,128)(2,1)} %get-tuple-element.126), channel_id=1, source_target_pairs={{0,16},{8,24},{16,0},{24,8},{1,17},{9,25},{17,1},{25,9},{2,18},{10... | collective-permute-start | bytes 3145736 | tf_op jit(solution)/shard_map/ppermute | solution.py:38
  295.2 84.3 %collective-permute-start.28 = (bf16[1024,1024]{1,0:T(8,128)(2,1)}, bf16[1024,1024]{1,0:T(8,128)(2,1)}, u32[]{:S(2)}, u32[]{:S(2)}) collective-permute-start(bf16[1024,1024]{1,0:T(8,128)(2,1)} %pad_maximum_fusion.8), channel_id=1, source_target_pairs={{0,8},{8,0},{16,24},{24,16},{1,9},{9,1},{17,25},{25,17},{2,10},{10... | collective-permute-start | bytes 6291464 | tf_op jit(solution)/shard_map/ppermute | solution.py:38
  300.4 79.1 %collective-permute-start.27 = (bf16[1024,1024]{1,0:T(8,128)(2,1)}, bf16[1024,1024]{1,0:T(8,128)(2,1)}, u32[]{:S(2)}, u32[]{:S(2)}) collective-permute-start(bf16[1024,1024]{1,0:T(8,128)(2,1)} %pad_maximum_fusion.7), channel_id=1, source_target_pairs={{0,16},{8,24},{16,0},{24,8},{1,17},{9,25},{17,1},{25,9},{2,18},{10... | collective-permute-start | bytes 6291464 | tf_op jit(solution)/shard_map/ppermute | solution.py:38
  379.5 80.4 %collective-permute-start.30 = (bf16[1024,1024]{1,0:T(8,128)(2,1)}, bf16[1024,1024]{1,0:T(8,128)(2,1)}, u32[]{:S(2)}, u32[]{:S(2)}) collective-permute-start(bf16[1024,1024]{1,0:T(8,128)(2,1)} %pad_maximum_fusion.9), channel_id=1, source_target_pairs={{0,8},{8,0},{16,24},{24,16},{1,9},{9,1},{17,25},{25,17},{2,10},{10... | collective-permute-start | bytes 6291464 | tf_op jit(solution)/shard_map/ppermute | solution.py:38
  379.5 80.4 %collective-permute-start.29 = (bf16[1024,1024]{1,0:T(8,128)(2,1)}, bf16[1024,1024]{1,0:T(8,128)(2,1)}, u32[]{:S(2)}, u32[]{:S(2)}) collective-permute-start(bf16[1024,1024]{1,0:T(8,128)(2,1)} %concatenate.172), channel_id=1, source_target_pairs={{0,16},{8,24},{16,0},{24,8},{1,17},{9,25},{17,1},{25,9},{2,18},{10... | collective-permute-start | bytes 6291464 | tf_op jit(solution)/shard_map/ppermute | solution.py:38
  460.0 234.9 %reduce-scatter.5.cloned.1.call-start = ((), (), s32[]{:S(2)}) async-start(), calls=%async_computation.7 | async-start | bytes 9437184 | tf_op jit(solution)/shard_map/reduce_scatter | solution.py:735
  468.5 34.5 %collective-permute-start.31 = (bf16[512,1024]{1,0:T(8,128)(2,1)S(1)}, bf16[512,1024]{1,0:T(8,128)(2,1)S(1)}, u32[]{:S(2)}, u32[]{:S(2)}) collective-permute-start(bf16[512,1024]{1,0:T(8,128)(2,1)S(1)} %get-tuple-element.136), channel_id=1, source_target_pairs={{0,8},{8,0},{16,24},{24,16},{1,9},{9,1},{17,25},{25,17},{2,10},{10... | collective-permute-start | bytes 3145736 | tf_op jit(solution)/shard_map/ppermute | solution.py:38
  470.4 33.5 %collective-permute-start.32 = (bf16[512,1024]{1,0:T(8,128)(2,1)S(1)}, bf16[512,1024]{1,0:T(8,128)(2,1)S(1)}, u32[]{:S(2)}, u32[]{:S(2)}) collective-permute-start(bf16[512,1024]{1,0:T(8,128)(2,1)S(1)} %get-tuple-element.137), channel_id=1, source_target_pairs={{0,16},{8,24},{16,0},{24,8},{1,17},{9,25},{17,1},{25,9},{2,18},{10... | collective-permute-start | bytes 3145736 | tf_op jit(solution)/shard_map/ppermute | solution.py:38
  504.9 41.6 %collective-permute-start.33 = (bf16[1024,1024]{1,0:T(8,128)(2,1)}, bf16[1024,1024]{1,0:T(8,128)(2,1)S(1)}, u32[]{:S(2)}, u32[]{:S(2)}) collective-permute-start(bf16[1024,1024]{1,0:T(8,128)(2,1)} %concatenate.173), channel_id=1, source_target_pairs={{0,16},{8,24},{16,0},{24,8},{1,17},{9,25},{17,1},{25,9},{2,18},{10... | collective-permute-start | bytes 6291464 | tf_op jit(solution)/shard_map/ppermute | solution.py:38
  504.9 43.0 %collective-permute-start.34 = (bf16[1024,1024]{1,0:T(8,128)(2,1)}, bf16[1024,1024]{1,0:T(8,128)(2,1)}, u32[]{:S(2)}, u32[]{:S(2)}) collective-permute-start(bf16[1024,1024]{1,0:T(8,128)(2,1)} %pad_maximum_fusion.10), channel_id=1, source_target_pairs={{0,8},{8,0},{16,24},{24,16},{1,9},{9,1},{17,25},{25,17},{2,10},{10... | collective-permute-start | bytes 6291464 | tf_op jit(solution)/shard_map/ppermute | solution.py:38
  547.9 228.9 %reduce-scatter.11.cloned.1.call-start = ((), (), s32[]{:S(2)}) async-start(), calls=%async_computation.10 | async-start | bytes 4718592 | tf_op jit(solution)/shard_map/reduce_scatter | solution.py:789
  605.6 28.9 %collective-permute-start.39 = (bf16[512,1024]{1,0:T(8,128)(2,1)}, bf16[512,1024]{1,0:T(8,128)(2,1)S(1)}, u32[]{:S(2)}, u32[]{:S(2)}) collective-permute-start(bf16[512,1024]{1,0:T(8,128)(2,1)} %get-tuple-element.156), channel_id=1, source_target_pairs={{0,8},{8,0},{16,24},{24,16},{1,9},{9,1},{17,25},{25,17},{2,10},{10... | collective-permute-start | bytes 3145736 | tf_op jit(solution)/shard_map/ppermute | solution.py:38
  605.7 28.8 %collective-permute-start.40 = (bf16[512,1024]{1,0:T(8,128)(2,1)}, bf16[512,1024]{1,0:T(8,128)(2,1)}, u32[]{:S(2)}, u32[]{:S(2)}) collective-permute-start(bf16[512,1024]{1,0:T(8,128)(2,1)} %get-tuple-element.157), channel_id=1, source_target_pairs={{0,16},{8,24},{16,0},{24,8},{1,17},{9,25},{17,1},{25,9},{2,18},{10... | collective-permute-start | bytes 3145736 | tf_op jit(solution)/shard_map/ppermute | solution.py:38
  650.3 127.6 %reduce-scatter.9.cloned.1.call-start = ((), (), s32[]{:S(2)}) async-start(), calls=%async_computation.9 | async-start | bytes 5308416 | tf_op jit(solution)/shard_map/reduce_scatter | solution.py:821
  659.9 29.9 %collective-permute-start.48 = (bf16[256,2048]{1,0:T(8,128)(2,1)}, bf16[256,2048]{1,0:T(8,128)(2,1)}, u32[]{:S(2)}, u32[]{:S(2)}) collective-permute-start(bf16[256,2048]{1,0:T(8,128)(2,1)} %pad_maximum_fusion.23), channel_id=1, source_target_pairs={{0,16},{8,24},{16,0},{24,8},{1,17},{9,25},{17,1},{25,9},{2,18},{10... | collective-permute-start | bytes 3145736 | tf_op jit(solution)/shard_map/ppermute | solution.py:38
  660.3 29.5 %collective-permute-start.49 = (bf16[256,2048]{1,0:T(8,128)(2,1)}, bf16[256,2048]{1,0:T(8,128)(2,1)}, u32[]{:S(2)}, u32[]{:S(2)}) collective-permute-start(bf16[256,2048]{1,0:T(8,128)(2,1)} %pad_maximum_fusion.24), channel_id=1, source_target_pairs={{0,8},{8,0},{16,24},{24,16},{1,9},{9,1},{17,25},{25,17},{2,10},{10... | collective-permute-start | bytes 3145736 | tf_op jit(solution)/shard_map/ppermute | solution.py:38
  701.4 29.8 %collective-permute-start.53 = (bf16[128,2048]{1,0:T(8,128)(2,1)S(1)}, bf16[128,2048]{1,0:T(8,128)(2,1)S(1)}, u32[]{:S(2)}, u32[]{:S(2)}) collective-permute-start(bf16[128,2048]{1,0:T(8,128)(2,1)S(1)} %get-tuple-element.275), channel_id=1, source_target_pairs={{0,8},{8,0},{16,24},{24,16},{1,9},{9,1},{17,25},{25,17},{2,10},{10... | collective-permute-start | bytes 1572872 | tf_op jit(solution)/shard_map/ppermute | solution.py:38
  701.8 29.4 %collective-permute-start.54 = (bf16[128,2048]{1,0:T(8,128)(2,1)S(1)}, bf16[128,2048]{1,0:T(8,128)(2,1)S(1)}, u32[]{:S(2)}, u32[]{:S(2)}) collective-permute-start(bf16[128,2048]{1,0:T(8,128)(2,1)S(1)} %get-tuple-element.266), channel_id=1, source_target_pairs={{0,16},{8,24},{16,0},{24,8},{1,17},{9,25},{17,1},{25,9},{2,18},{10... | collective-permute-start | bytes 1572872 | tf_op jit(solution)/shard_map/ppermute | solution.py:38
  703.7 53.9 %collective-permute-start.55 = (bf16[256,2048]{1,0:T(8,128)(2,1)S(1)}, bf16[256,2048]{1,0:T(8,128)(2,1)S(1)}, u32[]{:S(2)}, u32[]{:S(2)}) collective-permute-start(bf16[256,2048]{1,0:T(8,128)(2,1)S(1)} %copy-done.45), channel_id=1, source_target_pairs={{0,16},{8,24},{16,0},{24,8},{1,17},{9,25},{17,1},{25,9},{2,18},{10... | collective-permute-start | bytes 3145736 | tf_op jit(solution)/shard_map/ppermute | solution.py:38
  718.5 39.2 %collective-permute-start.57 = (bf16[256,2048]{1,0:T(8,128)(2,1)S(1)}, bf16[256,2048]{1,0:T(8,128)(2,1)S(1)}, u32[]{:S(2)}, u32[]{:S(2)}) collective-permute-start(bf16[256,2048]{1,0:T(8,128)(2,1)S(1)} %copy-done.44), channel_id=1, source_target_pairs={{0,8},{8,0},{16,24},{24,16},{1,9},{9,1},{17,25},{25,17},{2,10},{10... | collective-permute-start | bytes 3145736 | tf_op jit(solution)/shard_map/ppermute | solution.py:38
  719.8 34.4 %collective-permute-start.45 = (bf16[128,2048]{1,0:T(8,128)(2,1)S(1)}, bf16[128,2048]{1,0:T(8,128)(2,1)S(1)}, u32[]{:S(2)}, u32[]{:S(2)}) collective-permute-start(bf16[128,2048]{1,0:T(8,128)(2,1)S(1)} %fusion.41), channel_id=1, source_target_pairs={{0,8},{8,0},{16,24},{24,16},{1,9},{9,1},{17,25},{25,17},{2,10},{10... | collective-permute-start | bytes 1572872 | tf_op jit(solution)/shard_map/ppermute | solution.py:38
  (109 other events, 1318.7 us)
Sparse Core Ops, SparseCore 0:
  27.6 69.4 all-gather.11
  98.7 27.6 all-gather.5
  128.0 81.5 all-gather.9
  211.1 84.9 all-gather.7
  460.1 90.7 reduce-scatter.6
  553.1 87.9 reduce-scatter.4
  650.4 47.4 reduce-scatter.10
  700.2 53.1 reduce-scatter.8

commit v5 on v4

--- a/solution.py
+++ b/solution.py
@@ -40,10 +40,6 @@
 
 def after(value, *others):
     return lax.optimization_barrier((value, others))[0]
-
-
-def gather_direct(shard, axis, count):
-    return [shard] + [swap(shard, axis, count, k) for k in range(1, count)]
 
 
 def gather_step(state, axis, count, *first):
@@ -115,6 +111,13 @@
     for step in range(parts):
         came = scatter_step(state, axis, count, step, *came)
     return jnp.concatenate(scatter_sums(state))
+
+
+def joined(state):
+    return [
+        jnp.concatenate([array[block * rows : (block + 1) * rows] for array, block, rows in own])
+        for own in zip(*gathered(state))
+    ]
 
 
 def xor_blocks(value, own, count, dim):
@@ -605,14 +608,18 @@
     key_scale = lax.dynamic_slice_in_dim(small_rows[3], own_ctx * columns, columns)
     router_full = jnp.pad(small_full[:, 4 : 4 + experts], ((0, 0), (0, EXTRA - experts)))
 
-    inputs = in_sequence(gather_direct(own_rows, "context", n_ctx))
+    steps = n_ctx.bit_length() - 1
+    points = cuts(tokens, steps)
+    state = gather_start([own_rows[points[j] : points[j + 1]] for j in range(steps)])
+    for _ in range(steps):
+        gather_step(state, "context", n_ctx)
+    inputs = in_sequence(joined(state))
     places = xor_blocks(positions[0], own_ctx, n_ctx, 0)
     named = jnp.sum(
         (routes[0][:, :, None] == jnp.arange(experts, dtype=jnp.int32)[None, None, :]).astype(f32), axis=1
     )
     w_out = lax.all_gather(after(w_output, inputs), "expert", axis=0, tiled=True)
 
-    steps = n_ctx.bit_length() - 1
     downs = []
     for e in range(EXP_DEV):
         points = cuts(expert_down.shape[1], steps)
@@ -623,12 +630,13 @@
 
     pull = lax.all_gather(after(cotangent[0], down_came), "expert", axis=0, tiled=True)
     down_came = [gather_step(state, "context", n_ctx, down_came) for state in downs[1:]]
+    down_came = [gather_step(downs[0], "context", n_ctx, down_came) for _ in range(steps - 1)]
     input_r = inverse_rms(inputs.astype(f32))
     projected, normed, squares = project(inputs, input_r, attn_scale[None], packed, columns)
     query_p, key_p = projected[:, :columns], projected[:, columns : 2 * columns]
     squares = sum_rows(after(squares, down_came))
     r_both = lax.rsqrt(squares / width + epsilon)
-    down_came = [gather_step(downs[0], "context", n_ctx, r_both) for _ in range(steps - 1)]
+    down_came = [gather_step(state, "context", n_ctx, r_both) for _ in range(steps - 1) for state in downs[1:]]
     query_r, key_r = r_both[0][:, None], r_both[1][:, None]
     frequency = jnp.exp(
         jnp.arange(HEAD_DIM // 2, dtype=f32) * (-2.0 * math.log(rope_base) / HEAD_DIM)
@@ -659,20 +667,20 @@
     mixed_wide = lax.all_gather(mixed_own, "expert", axis=0, tiled=True)
 
     own = own_ctx.astype(jnp.int32)[None]
-    weights, first_came = [], []
+    weights, first_came, backs, down_w = [], [], [], []
+    for e in range(EXP_DEV):
+        back, down = pull_down(own, after(pull, mixed_own, *backs), gathered(downs[e]))
+        backs.append(back)
+        down_w.append(down)
     links_free = [branch_own]
-    back, down = pull_down(own, after(pull, mixed_own), gathered(downs[0]))
     for e in range(EXP_DEV):
-        if e > 0:
-            for _ in range(steps - 1):
-                gather_step(downs[e], "context", n_ctx, *links_free)
         pair = gather_start([expert_gate[e], expert_up[e]])
         came = [gather_step(pair, "context", n_ctx, *links_free)]
         came += [gather_step(pair, "context", n_ctx) for _ in range(steps - 1)]
         weights.append(gathered(pair))
         first_came.append(came[0])
-        links_free = [branch_own, came, back]
-    mixed_wide = after(mixed_wide, back)
+        links_free = [branch_own, came]
+    mixed_wide = after(mixed_wide, backs)
     mixed, beside = mixed_wide[:, :width], mixed_wide[:, width:].astype(f32)
     router_x = xor_blocks(router_full, own_ctx, n_ctx, 0)
     router_probs = beside[:, :experts] + beside[:, experts : 2 * experts]
@@ -693,8 +701,7 @@
     def sums_of(state):
         return scatter_sums(state, last_came)
 
-    ff = back.shape[1]
-    backs, down_w = [back], [down]
+    ff = backs[0].shape[1]
     hidden_g, d_acts, d_gates, g_raw = [], [], [], []
     for e in range(EXP_DEV):
         rows_in = after(mixed_wide, g_raw, backs[e])
@@ -704,9 +711,6 @@
             kept.append(made)
         if e + 1 < EXP_DEV:
             g_raw.append(gate_up_grads(e, first_came[e + 1]))
-            back, down = pull_down(own, after(pull, d_acts), gathered(downs[e + 1]))
-            backs.append(back)
-            down_w.append(down)
     pairs = [scatter_state([jnp.split(grad, n_ctx) for grad in raw]) for raw in g_raw]
     pair_came = [scatter_step(pair, "context", n_ctx, 0) for pair in pairs]
 
@@ -730,11 +734,13 @@
     raw = gate_up_grads(EXP_DEV - 1, d_mixed_part)
     pairs.append(scatter_state([jnp.split(grad, n_ctx) for grad in raw]))
     last_came = scatter_step(pairs[-1], "context", n_ctx, 0, pair_came)
-    out_part = combine(after(hidden_g, raw, pair_came), down_w)
+    down_raw = [weight_grad(after(hidden_g[0], raw), pull)]
+    out_part = combine(after(hidden_g, down_raw, pair_came), down_w)
     out_part = after(out_part, last_came)
     out_own = lax.psum_scatter(out_part, "expert", scatter_dimension=0, tiled=True).astype(f32)
-    g_router = dot(mixed, d_logits, ((0,), (0,)))
-    d_mixed = after(d_mixed, out_part, g_router)
+    d_mixed = after(d_mixed, out_part)
+    downs = [scatter_state(row_parts(owner_rows(down_raw[0]), steps))]
+    down_came = scatter_step(downs[0], "context", n_ctx, 0, last_came)
 
     scaled = d_mixed * moe_scale
     g_moe = jnp.sum(d_mixed * middle * middle_r, axis=0)
@@ -744,23 +750,17 @@
         - middle * (middle_r**3 * jnp.mean(scaled * middle, axis=-1, keepdims=True))
     )
     points = cuts(tokens, steps)
-    d_low = d_middle.astype(bf16)
+    d_low = after(d_middle.astype(bf16), down_came)
     state = gather_start([d_low[points[j] : points[j + 1]] for j in range(steps)])
-    came, down_raw = (), []
-    for step in range(max(steps, EXP_DEV)):
-        if step < EXP_DEV:
-            down_raw.append(weight_grad(after(hidden_g[step], d_middle, *came), pull))
+    came = d_low
+    for step in range(max(steps, EXP_DEV - 1)):
         if step < steps:
             came = gather_step(state, "context", n_ctx)
-    parts = gathered(state)
-    d_branch = in_sequence(
-        [
-            jnp.concatenate([array[block * rows : (block + 1) * rows] for array, block, rows in own])
-            for own in zip(*parts)
-        ]
-    )
-    d_branch = after(d_branch, down_raw)
-    downs = [scatter_state(row_parts(owner_rows(grad), steps)) for grad in down_raw]
+        if step + 1 < EXP_DEV:
+            down_raw.append(weight_grad(after(hidden_g[step + 1], came), pull))
+    g_router = dot(mixed, after(d_logits, d_low, down_raw), ((0,), (0,)))
+    d_branch = after(in_sequence(joined(state)), down_raw, g_router)
+    downs += [scatter_state(row_parts(owner_rows(grad), steps)) for grad in down_raw[1:]]
     last_came = [
         scatter_step(pairs[-1], "context", n_ctx, step, d_branch) for step in range(1, steps)
     ]
@@ -787,14 +787,12 @@
     beside = jnp.concatenate([jnp.zeros((width, 1), f32), g_moe[:, None], spread.T, g_router], axis=1)
     beside = jnp.pad(beside, ((0, 0), (0, EXTRA - beside.shape[1])))
     g_side_sum = lax.psum_scatter(g_side.reshape(width, 2 * columns), "expert", scatter_dimension=0, tiled=True)
-    down_came = [scatter_step(downs[0], "context", n_ctx, 0, inner_both)]
     d_projected = after(d_projected, g_side)
     d_normed_part, g_packed = project_back(d_projected, packed, inputs, input_r, normed, beside)
+    down_came = [scatter_step(down, "context", n_ctx, 0, inner_both) for down in downs[1:]]
     g_packed = after(g_packed, down_came)
     d_normed = scatter_state(row_parts(per_device(d_normed_part), steps))
     last_came = scatter_step(d_normed, "context", n_ctx, 0)
-    for down in downs[1:]:
-        scatter_step(down, "context", n_ctx, 0, *down_came)
     for step in range(1, steps):
         scatter_step(d_normed, "context", n_ctx, step)
         for down in downs:

time: 805 us -> 778 us (0.966)
  waiting for transfers between devices: 215 us -> 197 us
    ppermute x59 -> x60, waiting for transfers between devices: 215 us -> 197 us  [swap(): return lax.ppermute(value, axis, [(i, i ^ bit) for i in range(count)])]
    unnamed x155 -> x183, local copies, waits for them, and re-layouts: 22.2 us -> 18 us
    ppermute x59 -> x60, starting transfers between devices: 66.4 us -> 64.7 us  [swap(): return lax.ppermute(value, axis, [(i, i ^ bit) for i in range(count)])]
  transfers between devices with their start and end apart: 67 -> 68, of which waited for: 29 -> 30; matrix products, arithmetic and copies ran while one was open for 28% -> 28% of each run, Pallas kernels for 29% -> 30%
where the time goes in v5:
time: 778 us; the launch traced here: 773 us
  Pallas kernels  234 us (30%)
  waiting for transfers between devices  197 us (25%)
  other arithmetic  99.7 us (13%)
  matrix products  85.9 us (11%)
  starting transfers between devices  65.3 us (8%)
  local copies, waits for them, and re-layouts  60.6 us (8%)
  between operations  31.4 us (4%)
    ppermute x60, waiting for transfers between devices, swap(): return lax.ppermute(value, axis, [(i, i ^ bit) for i in range(count)])  197 us
    dot_general x10, matrix products, dot(): lax.dot_general(left, right, (dims, ((), ())), preferred_element_type=f32)  85.9 us
    ppermute x60, starting transfers between devices, swap(): return lax.ppermute(value, axis, [(i, i ^ bit) for i in range(count)])  64.7 us
    pallas_call x2, Pallas kernels, run_experts(): pl.pallas_call(lambda *refs: experts_kernel(e, len(gate_k), *refs), grid=...  55.9 us
    pallas_call x1, Pallas kernels, rows_back(): pl.pallas_call(lambda *refs: rows_back_kernel(count, n_ctx, *refs), grid=...  46.8 us
    pallas_call x2, Pallas kernels, pull_down(): pl.pallas_call(lambda *refs: pull_down_kernel(places, *refs), grid=(rows...  28.4 us
    pallas_call x1, Pallas kernels, combine(): pl.pallas_call(lambda *refs: combine_kernel(count, *refs), grid=(rows //...  23.6 us
    pallas_call x1, Pallas kernels, attend_back(): pl.pallas_call(lambda *refs: attend_back_kernel(min(256, rows), *refs), g...  19.5 us
  transfers between devices with their start and end apart: 68, of which 30 were waited for; matrix products, arithmetic and copies ran while one was open for 28% of the time, Pallas kernels for 30%

profile of v5, /device:TPU:0, one launch (start us, length us, event | category | flops | bytes accessed | tf_op | source)
XLA Modules:
  0.0 773.3 jit_solution(361892024757498170)
XLA Ops:
  16.4 4.5 collective-permute-done.4
  20.9 5.2 collective-permute-done.5
  35.7 10.5 %collective-permute-done.1 = bf16[128,2048]{1,0:T(8,128)(2,1)S(1)} collective-permute-done((bf16[128,2048]{1,0:T(8,128)(2,1)S(1)}, bf16[128,2048]{1,0:T(8,128)(2,1)S(1)}, u32[]{:S(2)}, u32[]{:S(2)}) %collective-permute-start.1) | collective-permute-done | bytes 524320 | tf_op jit(solution)/shard_map/ppermute | solution.py:38
  62.3 7.1 collective-permute-done.2
  82.6 8.9 %collective-permute-done.7.refs_3_ = bf16[128,2048]{1,0:T(8,128)(2,1)S(1)} collective-permute-done((bf16[128,2048]{1,0:T(8,128)(2,1)S(1)}, bf16[128,2048]{1,0:T(8,128)(2,1)S(1)}, u32[]{:S(2)}, u32[]{:S(2)}) %collective-permute-start.7) | collective-permute-done | bytes 524320 | tf_op jit(solution)/shard_map/ppermute | solution.py:38
  111.7 16.0 %project.1 = (f32[1024,1536]{1,0:T(8,128)}, bf16[1024,2048]{1,0:T(8,128)(2,1)}, f32[2,1024]{1,0:T(2,128)}) custom-call(bf16[1024,2048]{1,0:T(8,128)(2,1)} %bitcast.247, f32[1024,1]{1,0:T(8,128)} %copy.144.refs_1_.refs_3_, f32[1,2048]{1,0:T(1,128)} %get-tuple-element.367.refs_2_, bf16[8,4,64,1664]{3,2,1,0:T(8,128)(2,1)} %bitcast.256), custom_call_target="tpu_custom_call" | custom-call | flops 6442450944 | bytes 21495808 | tf_op jit(solution)/shard_map/project/pallas_call | solution.py:175
  141.4 15.1 %attend.1 = (bf16[1024,512]{1,0:T(8,128)(2,1)}, bf16[1024,512]{1,0:T(8,128)(2,1)}, bf16[1024,512]{1,0:T(8,128)(2,1)}, f32[4,1024,1]{2,1,0:T(8,128)}) custom-call(f32[1024,1536]{1,0:T(8,128)} %get-tuple-element.103.refs_0_.refs_1_.refs_2_, f32[1024,1536]{1,0:T(8,128)} %get-tuple-element.103.refs_0_.refs_1_.refs_2_, ...), custom_call_target="tpu_custom_call" | custom-call | flops 2147483648 | bytes 6291456 | tf_op jit(solution)/shard_map/attend/pallas_call | solution.py:301
  163.5 20.0 %collective-permute-done.18 = bf16[256,2048]{1,0:T(8,128)(2,1)S(1)} collective-permute-done((bf16[256,2048]{1,0:T(8,128)(2,1)S(1)}, bf16[256,2048]{1,0:T(8,128)(2,1)S(1)}, u32[]{:S(2)}, u32[]{:S(2)}) %collective-permute-start.18) | collective-permute-done | bytes 1048608 | tf_op jit(solution)/shard_map/ppermute | solution.py:38
  187.0 7.1 collective-permute-done.20
  206.7 16.4 %collective-permute-done.24.refs_9_.refs_8_ = bf16[512,1024]{1,0:T(8,128)(2,1)S(1)} collective-permute-done((bf16[512,1024]{1,0:T(8,128)(2,1)S(1)}, bf16[512,1024]{1,0:T(8,128)(2,1)S(1)}, u32[]{:S(2)}, u32[]{:S(2)}) %collective-permute-start.24) | collective-permute-done | bytes 1048608 | tf_op jit(solution)/shard_map/ppermute | solution.py:38
  232.7 37.9 %collective-permute-done.25.refs_8_.refs_10_.refs_7_.refs_9_ = bf16[1024,1024]{1,0:T(8,128)(2,1)} collective-permute-done((bf16[1024,1024]{1,0:T(8,128)(2,1)}, bf16[1024,1024]{1,0:T(8,128)(2,1)}, u32[]{:S(2)}, u32[]{:S(2)}) %collective-permute-start.25) | collective-permute-done | bytes 2097184 | tf_op jit(solution)/shard_map/ppermute | solution.py:38
  273.0 14.3 %pull_down.2 = (f32[2048,1024]{1,0:T(8,128)}, bf16[1024,2048]{1,0:T(8,128)(2,1)}) custom-call(s32[1]{0:T(128)} %bitcast.53.refs_0_, bf16[2048,2048]{1,0:T(8,128)(2,1)} %all-gather.10.cloned.1.call-done.refs_1_, bf16[128,2048]{1,0:T(8,128)(2,1)} %copy-done.45, bf16[128,2048]{1,0:T(8,128)(2,1)} %copy-done.58, ...), custom_call_target="tpu_custom_call" | custom-call | flops 8589934592 | bytes 25165824 | tf_op jit(solution)/shard_map/pull_down/pallas_call | solution.py:415
  287.3 14.1 %pull_down.3 = (f32[2048,1024]{1,0:T(8,128)}, bf16[1024,2048]{1,0:T(8,128)(2,1)}) custom-call(s32[1]{0:T(128)} %bitcast.53.refs_0_, bf16[2048,2048]{1,0:T(8,128)(2,1)} %all-gather.10.cloned.1.call-done.refs_1_, bf16[128,2048]{1,0:T(8,128)(2,1)} %get-tuple-element.105.refs_2_, bf16[128,2048]{1,0:T(8,128)(2,1)} %collective-permute-done.9.refs_3_, ...), custom_call_target="tpu_custom_call" | custom-call | flops 8589934592 | bytes 25165824 | tf_op jit(solution)/shard_map/pull_down/pallas_call | solution.py:415
  310.2 27.9 %expert.2 = (bf16[2048,1024]{1,0:T(8,128)(2,1)}, bf16[2048,2048]{1,0:T(8,128)(2,1)}, f32[2048,1]{1,0:T(8,128)}) custom-call(bf16[2048,2176]{1,0:T(8,128)(2,1)} %all-gather.8.cloned.1.call-done.refs_0_, f32[2048,1024]{1,0:T(8,128)} %get-tuple-element.119.refs_1_, f32[2048,2]{1,0:T(8,128)} %dynamic-slice_multiply_fusion.refs_2_, bf16[512,1024]{1,0:T(8,128)(2,1)} %copy-done.15, ...), custom_call_target="tpu_custom_call" | custom-call | flops 17179869184 | bytes 37748736 | tf_op jit(solution)/shard_map/expert/pallas_call | solution.py:456
  338.0 13.0 %fusion.14 = bf16[2048,1024]{1,0:T(8,128)(2,1)S(1)} fusion(bf16[2048,2048]{1,0:T(8,128)(2,1)} %get-tuple-element.130.refs_0_, bf16[2048,2176]{1,0:T(8,128)(2,1)} %all-gather.8.cloned.1.call-done.refs_0_), kind=kOutput, calls=%fused_computation.18 | convolution fusion | flops 8592031744 | bytes 16777216 | tf_op jit(solution)/shard_map/dot_general | solution.py:24
  353.7 11.4 %fusion.19 = bf16[2048,1024]{1,0:T(8,128)(2,1)S(1)} fusion(bf16[2048,2048]{1,0:T(8,128)(2,1)S(1)} %copy-done.16, bf16[2048,2176]{1,0:T(8,128)(2,1)} %all-gather.8.cloned.1.call-done.refs_0_), kind=kOutput, calls=%fused_computation.19 | convolution fusion | flops 8592031744 | bytes 16777216 | tf_op jit(solution)/shard_map/dot_general | solution.py:24
  370.6 28.0 %expert.3 = (bf16[2048,1024]{1,0:T(8,128)(2,1)}, bf16[2048,2048]{1,0:T(8,128)(2,1)}, f32[2048,1]{1,0:T(8,128)}) custom-call(bf16[2048,2176]{1,0:T(8,128)(2,1)} %all-gather.8.cloned.1.call-done.refs_0_, f32[2048,1024]{1,0:T(8,128)} %get-tuple-element.121.refs_1_, f32[2048,2]{1,0:T(8,128)} %dynamic-slice_multiply_fusion.refs_2_, bf16[512,1024]{1,0:T(8,128)(2,1)} %copy-done.14, ...), custom_call_target="tpu_custom_call" | custom-call | flops 17179869184 | bytes 37748736 | tf_op jit(solution)/shard_map/expert/pallas_call | solution.py:456
  404.4 46.8 %rows_back.1 = bf16[2048,2048]{1,0:T(8,128)(2,1)} custom-call(bf16[2048,2048]{1,0:T(8,128)(2,1)} %get-tuple-element.130.refs_0_, bf16[2048,2048]{1,0:T(8,128)(2,1)} %get-tuple-element.137.refs_1_, bf16[512,1024]{1,0:T(8,128)(2,1)} %copy-done.15, bf16[512,1024]{1,0:T(8,128)(2,1)} %copy-done.32, ...), custom_call_target="tpu_custom_call" | custom-call | bytes 2097152 | tf_op jit(solution)/shard_map/rows_back/pallas_call | solution.py:518
  451.3 4.6 convert_add_fusion.3
  461.8 13.0 %fusion.29 = bf16[2048,1024]{1,0:T(8,128)(2,1)S(1)} fusion(bf16[2048,2048]{1,0:T(8,128)(2,1)} %get-tuple-element.137.refs_1_, bf16[2048,2176]{1,0:T(8,128)(2,1)} %all-gather.8.cloned.1.call-done.refs_0_), kind=kOutput, calls=%fused_computation.21 | convolution fusion | flops 8592031744 | bytes 16777216 | tf_op jit(solution)/shard_map/dot_general | solution.py:24
  474.8 12.9 %fusion.24 = bf16[2048,1024]{1,0:T(8,128)(2,1)S(1)} fusion(bf16[2048,2048]{1,0:T(8,128)(2,1)S(1)} %bitcast.251, bf16[2048,2176]{1,0:T(8,128)(2,1)} %all-gather.8.cloned.1.call-done.refs_0_), kind=kOutput, calls=%fused_computation.20 | convolution fusion | flops 8592031744 | bytes 16777216 | tf_op jit(solution)/shard_map/dot_general | solution.py:24
  494.4 13.3 %convolution_convert_fusion.1 = bf16[1024,2048]{1,0:T(8,128)(2,1)} fusion(bf16[2048,1024]{1,0:T(8,128)(2,1)S(1)} %copy-done.79, bf16[2048,2048]{1,0:T(8,128)(2,1)} %all-gather.10.cloned.1.call-done.refs_1_), kind=kOutput, calls=%fused_computation.23 | convolution fusion | flops 8592031744 | bytes 16777216 | tf_op jit(solution)/shard_map/dot_general | solution.py:24
  507.8 23.6 %combine.1 = bf16[2048,2048]{1,0:T(8,128)(2,1)} custom-call(bf16[2048,1024]{1,0:T(8,128)(2,1)} %get-tuple-element.141.refs_0_, bf16[2048,1024]{1,0:T(8,128)(2,1)} %get-tuple-element.154.refs_1_, bf16[1024,2048]{1,0:T(8,128)(2,1)} %get-tuple-element.143.refs_2_, bf16[1024,2048]{1,0:T(8,128)(2,1)} %get-tuple-element.144.refs_3_), custom_call_target="tpu_custom_call" | custom-call | flops 17179869184 | bytes 25165824 | tf_op jit(solution)/shard_map/combine/pallas_call | solution.py:484
  558.8 7.4 collective-permute-done.38
  566.3 11.5 %convolution_convert_fusion = bf16[1024,2048]{1,0:T(8,128)(2,1)} fusion(bf16[2048,1024]{1,0:T(8,128)(2,1)S(1)} %copy-done.78, bf16[2048,2048]{1,0:T(8,128)(2,1)S(1)} %bitcast.309), kind=kOutput, calls=%fused_computation.22 | convolution fusion | flops 8592031744 | bytes 16777216 | tf_op jit(solution)/shard_map/dot_general | solution.py:24
  582.5 18.7 %collective-permute-done.40 = bf16[256,2048]{1,0:T(8,128)(2,1)S(1)} collective-permute-done((bf16[256,2048]{1,0:T(8,128)(2,1)S(1)}, bf16[256,2048]{1,0:T(8,128)(2,1)S(1)}, u32[]{:S(2)}, u32[]{:S(2)}) %collective-permute-start.40) | collective-permute-done | bytes 1048608 | tf_op jit(solution)/shard_map/ppermute | solution.py:38
  607.7 19.5 %attend_back.1 = (f32[1024,512]{1,0:T(8,128)}, f32[1024,512]{1,0:T(8,128)}, bf16[1024,512]{1,0:T(8,128)(2,1)}, f32[4,1024,1]{2,1,0:T(8,128)}, f32[4,1024,1]{2,1,0:T(8,128)}, /*index=5*/f32[4,2,128]{2,1,0:T(2,128)}) custom-call(f32[1024,1536]{1,0:T(8,128)} %get-tuple-element.103.refs_0_.refs_1_.refs_2_, ...), custom_call_target="tpu_custom_call" | custom-call | bytes 1048576 | tf_op jit(solution)/shard_map/attend_back/pallas_call | solution.py:361
  637.7 9.1 %side_grads.1 = bf16[8,4,64,1024]{3,2,1,0:T(8,128)(2,1)} custom-call(bf16[1024,2048]{1,0:T(8,128)(2,1)} %get-tuple-element.167.refs_0_.refs_4_, bf16[1024,512]{1,0:T(8,128)(2,1)} %get-tuple-element.168.refs_1_, bf16[1024,512]{1,0:T(8,128)(2,1)} %get-tuple-element.110.refs_2_, bf16[1024,2048]{1,0:T(8,128)(2,1)} %bitcast.267), custom_call_target="tpu_custom_call" | custom-call | flops 4294967296 | bytes 12582912 | tf_op jit(solution)/shard_map/side_grads/pallas_call | solution.py:214
  661.3 19.1 %project_back.1 = (bf16[1024,2048]{1,0:T(8,128)(2,1)}, bf16[8,4,64,1152]{3,2,1,0:T(8,128)(2,1)}) custom-call(bf16[1024,1536]{1,0:T(8,128)(2,1)} %pad_maximum_fusion.3.refs_0_, bf16[8,4,64,1664]{3,2,1,0:T(8,128)(2,1)} %bitcast.257, bf16[1024,2048]{1,0:T(8,128)(2,1)} %bitcast.248, f32[1024,1]{1,0:T(8,128)} %copy.144.refs_1_.refs_3_, ...), custom_call_target="tpu_custom_call" | custom-call | bytes 4194304 | tf_op jit(solution)/shard_map/project_back/pallas_call | solution.py:244
  694.2 19.5 %collective-permute-done.56 = bf16[128,2048]{1,0:T(8,128)(2,1)} collective-permute-done((bf16[128,2048]{1,0:T(8,128)(2,1)}, bf16[128,2048]{1,0:T(8,128)(2,1)}, u32[]{:S(2)}, u32[]{:S(2)}) %collective-permute-start.56) | collective-permute-done | bytes 524320 | tf_op jit(solution)/shard_map/ppermute | solution.py:38
  740.8 5.5 collective-permute-done.50
  755.4 5.0 fusion.37
  (484 shorter events, 254.6 us)
Async XLA Ops:
  7.2 102.3 %all-gather.12.cloned.1.call-start = ((), (), s32[]{:S(2)}) async-start(), calls=%async_computation.11 | async-start | bytes 7667712 | tf_op jit(solution)/shard_map/all_gather | solution.py:603
  27.4 129.1 %all-gather.6.cloned.1.call-start = ((), (), s32[]{:S(2)}) async-start(), calls=%async_computation.4 | async-start | bytes 2359296 | tf_op jit(solution)/shard_map/all_gather | solution.py:621
  78.6 154.1 %all-gather.10.cloned.1.call-start = ((), (), s32[]{:S(2)}) async-start(), calls=%async_computation.6 | async-start | bytes 9437184 | tf_op jit(solution)/shard_map/all_gather | solution.py:631
  93.3 213.5 %all-gather.8.cloned.1.call-start = ((), (), s32[]{:S(2)}) async-start(), calls=%async_computation.5 | async-start | bytes 10027008 | tf_op jit(solution)/shard_map/all_gather | solution.py:667
  136.4 24.4 %collective-permute-start.17 = (bf16[256,2048]{1,0:T(8,128)(2,1)}, bf16[256,2048]{1,0:T(8,128)(2,1)}, u32[]{:S(2)}, u32[]{:S(2)}) collective-permute-start(bf16[256,2048]{1,0:T(8,128)(2,1)} %get-tuple-element.113), channel_id=1, source_target_pairs={{0,8},{8,0},{16,24},{24,16},{1,9},{9,1},{17,25},{25,17},{2,10},{10... | collective-permute-start | bytes 3145736 | tf_op jit(solution)/shard_map/ppermute | solution.py:38
  137.1 23.8 %collective-permute-start.16 = (bf16[256,2048]{1,0:T(8,128)(2,1)}, bf16[256,2048]{1,0:T(8,128)(2,1)}, u32[]{:S(2)}, u32[]{:S(2)}) collective-permute-start(bf16[256,2048]{1,0:T(8,128)(2,1)} %get-tuple-element.112), channel_id=1, source_target_pairs={{0,16},{8,24},{16,0},{24,8},{1,17},{9,25},{17,1},{25,9},{2,18},{10... | collective-permute-start | bytes 3145736 | tf_op jit(solution)/shard_map/ppermute | solution.py:38
  201.5 343.4 %reduce-scatter.7.cloned.1.call-start = ((), (), s32[]{:S(2)}) async-start(), calls=%async_computation.8 | async-start | bytes 9437184 | tf_op jit(solution)/shard_map/reduce_scatter | solution.py:731
  203.9 24.5 %collective-permute-start.22 = (bf16[512,1024]{1,0:T(8,128)(2,1)S(1)}, bf16[512,1024]{1,0:T(8,128)(2,1)S(1)}, u32[]{:S(2)}, u32[]{:S(2)}) collective-permute-start(bf16[512,1024]{1,0:T(8,128)(2,1)S(1)} %get-tuple-element.124.refs_3_.refs_2_), channel_id=1, source_target_pairs={{0,8},{8,0},{16,24},{24,16},{1,9},{9,1},{17,25},{25,17},{2,10},{10... | collective-permute-start | bytes 3145736 | tf_op jit(solution)/shard_map/ppermute | solution.py:38
  224.7 45.8 %collective-permute-start.25 = (bf16[1024,1024]{1,0:T(8,128)(2,1)}, bf16[1024,1024]{1,0:T(8,128)(2,1)}, u32[]{:S(2)}, u32[]{:S(2)}) collective-permute-start(bf16[1024,1024]{1,0:T(8,128)(2,1)} %pad_maximum_fusion.6), channel_id=1, source_target_pairs={{0,8},{8,0},{16,24},{24,16},{1,9},{9,1},{17,25},{25,17},{2,10},{10... | collective-permute-start | bytes 6291464 | tf_op jit(solution)/shard_map/ppermute | solution.py:38
  230.1 40.5 %collective-permute-start.23 = (bf16[1024,1024]{1,0:T(8,128)(2,1)}, bf16[1024,1024]{1,0:T(8,128)(2,1)}, u32[]{:S(2)}, u32[]{:S(2)}) collective-permute-start(bf16[1024,1024]{1,0:T(8,128)(2,1)} %pad_maximum_fusion.5), channel_id=1, source_target_pairs={{0,16},{8,24},{16,0},{24,8},{1,17},{9,25},{17,1},{25,9},{2,18},{10... | collective-permute-start | bytes 6291464 | tf_op jit(solution)/shard_map/ppermute | solution.py:38
  270.6 30.9 %collective-permute-start.27 = (bf16[512,1024]{1,0:T(8,128)(2,1)S(1)}, bf16[512,1024]{1,0:T(8,128)(2,1)S(1)}, u32[]{:S(2)}, u32[]{:S(2)}) collective-permute-start(bf16[512,1024]{1,0:T(8,128)(2,1)S(1)} %get-tuple-element.129.refs_7_.refs_14_), channel_id=1, source_target_pairs={{0,16},{8,24},{16,0},{24,8},{1,17},{9,25},{17,1},{25,9},{2,18},{10... | collective-permute-start | bytes 3145736 | tf_op jit(solution)/shard_map/ppermute | solution.py:38
  271.2 32.2 %collective-permute-start.26 = (bf16[512,1024]{1,0:T(8,128)(2,1)S(1)}, bf16[512,1024]{1,0:T(8,128)(2,1)S(1)}, u32[]{:S(2)}, u32[]{:S(2)}) collective-permute-start(bf16[512,1024]{1,0:T(8,128)(2,1)S(1)} %get-tuple-element.128.refs_3_.refs_10_), channel_id=1, source_target_pairs={{0,8},{8,0},{16,24},{24,16},{1,9},{9,1},{17,25},{25,17},{2,10},{10... | collective-permute-start | bytes 3145736 | tf_op jit(solution)/shard_map/ppermute | solution.py:38
  303.2 67.5 %collective-permute-start.29 = (bf16[1024,1024]{1,0:T(8,128)(2,1)}, bf16[1024,1024]{1,0:T(8,128)(2,1)}, u32[]{:S(2)}, u32[]{:S(2)}) collective-permute-start(bf16[1024,1024]{1,0:T(8,128)(2,1)} %pad_maximum_fusion.8), channel_id=1, source_target_pairs={{0,8},{8,0},{16,24},{24,16},{1,9},{9,1},{17,25},{25,17},{2,10},{10... | collective-permute-start | bytes 6291464 | tf_op jit(solution)/shard_map/ppermute | solution.py:38
  305.0 65.6 %collective-permute-start.28 = (bf16[1024,1024]{1,0:T(8,128)(2,1)}, bf16[1024,1024]{1,0:T(8,128)(2,1)}, u32[]{:S(2)}, u32[]{:S(2)}) collective-permute-start(bf16[1024,1024]{1,0:T(8,128)(2,1)} %pad_maximum_fusion.7), channel_id=1, source_target_pairs={{0,16},{8,24},{16,0},{24,8},{1,17},{9,25},{17,1},{25,9},{2,18},{10... | collective-permute-start | bytes 6291464 | tf_op jit(solution)/shard_map/ppermute | solution.py:38
  368.6 82.6 %collective-permute-start.31 = (bf16[1024,1024]{1,0:T(8,128)(2,1)}, bf16[1024,1024]{1,0:T(8,128)(2,1)}, u32[]{:S(2)}, u32[]{:S(2)}) collective-permute-start(bf16[1024,1024]{1,0:T(8,128)(2,1)} %pad_maximum_fusion.9), channel_id=1, source_target_pairs={{0,8},{8,0},{16,24},{24,16},{1,9},{9,1},{17,25},{25,17},{2,10},{10... | collective-permute-start | bytes 6291464 | tf_op jit(solution)/shard_map/ppermute | solution.py:38
  370.6 80.6 %collective-permute-start.30 = (bf16[1024,1024]{1,0:T(8,128)(2,1)}, bf16[1024,1024]{1,0:T(8,128)(2,1)}, u32[]{:S(2)}, u32[]{:S(2)}) collective-permute-start(bf16[1024,1024]{1,0:T(8,128)(2,1)} %concatenate.180), channel_id=1, source_target_pairs={{0,16},{8,24},{16,0},{24,8},{1,17},{9,25},{17,1},{25,9},{2,18},{10... | collective-permute-start | bytes 6291464 | tf_op jit(solution)/shard_map/ppermute | solution.py:38
  451.2 240.2 %reduce-scatter.5.cloned.1.call-start = ((), (), s32[]{:S(2)}) async-start(), calls=%async_computation.7 | async-start | bytes 9437184 | tf_op jit(solution)/shard_map/reduce_scatter | solution.py:740
  459.7 32.4 %collective-permute-start.32 = (bf16[512,1024]{1,0:T(8,128)(2,1)S(1)}, bf16[512,1024]{1,0:T(8,128)(2,1)S(1)}, u32[]{:S(2)}, u32[]{:S(2)}) collective-permute-start(bf16[512,1024]{1,0:T(8,128)(2,1)S(1)} %get-tuple-element.139), channel_id=1, source_target_pairs={{0,8},{8,0},{16,24},{24,16},{1,9},{9,1},{17,25},{25,17},{2,10},{10... | collective-permute-start | bytes 3145736 | tf_op jit(solution)/shard_map/ppermute | solution.py:38
  459.9 32.2 %collective-permute-start.33 = (bf16[512,1024]{1,0:T(8,128)(2,1)S(1)}, bf16[512,1024]{1,0:T(8,128)(2,1)S(1)}, u32[]{:S(2)}, u32[]{:S(2)}) collective-permute-start(bf16[512,1024]{1,0:T(8,128)(2,1)S(1)} %get-tuple-element.140), channel_id=1, source_target_pairs={{0,16},{8,24},{16,0},{24,8},{1,17},{9,25},{17,1},{25,9},{2,18},{10... | collective-permute-start | bytes 3145736 | tf_op jit(solution)/shard_map/ppermute | solution.py:38
  492.1 39.2 %collective-permute-start.34 = (bf16[1024,1024]{1,0:T(8,128)(2,1)}, bf16[1024,1024]{1,0:T(8,128)(2,1)S(1)}, u32[]{:S(2)}, u32[]{:S(2)}) collective-permute-start(bf16[1024,1024]{1,0:T(8,128)(2,1)} %concatenate.181), channel_id=1, source_target_pairs={{0,16},{8,24},{16,0},{24,8},{1,17},{9,25},{17,1},{25,9},{2,18},{10... | collective-permute-start | bytes 6291464 | tf_op jit(solution)/shard_map/ppermute | solution.py:38
  492.4 40.7 %collective-permute-start.35 = (bf16[1024,1024]{1,0:T(8,128)(2,1)}, bf16[1024,1024]{1,0:T(8,128)(2,1)}, u32[]{:S(2)}, u32[]{:S(2)}) collective-permute-start(bf16[1024,1024]{1,0:T(8,128)(2,1)} %pad_maximum_fusion.10), channel_id=1, source_target_pairs={{0,8},{8,0},{16,24},{24,16},{1,9},{9,1},{17,25},{25,17},{2,10},{10... | collective-permute-start | bytes 6291464 | tf_op jit(solution)/shard_map/ppermute | solution.py:38
  533.1 215.5 %reduce-scatter.11.cloned.1.call-start = ((), (), s32[]{:S(2)}) async-start(), calls=%async_computation.10 | async-start | bytes 4718592 | tf_op jit(solution)/shard_map/reduce_scatter | solution.py:789
  577.9 23.4 %collective-permute-start.41 = (bf16[256,2048]{1,0:T(8,128)(2,1)S(1)}, bf16[256,2048]{1,0:T(8,128)(2,1)S(1)}, u32[]{:S(2)}, u32[]{:S(2)}) collective-permute-start(bf16[256,2048]{1,0:T(8,128)(2,1)S(1)} %pad_maximum_fusion.24), channel_id=1, source_target_pairs={{0,16},{8,24},{16,0},{24,8},{1,17},{9,25},{17,1},{25,9},{2,18},{10... | collective-permute-start | bytes 3145736 | tf_op jit(solution)/shard_map/ppermute | solution.py:38
  601.5 29.4 %collective-permute-start.42 = (bf16[512,1024]{1,0:T(8,128)(2,1)}, bf16[512,1024]{1,0:T(8,128)(2,1)S(1)}, u32[]{:S(2)}, u32[]{:S(2)}) collective-permute-start(bf16[512,1024]{1,0:T(8,128)(2,1)} %get-tuple-element.162), channel_id=1, source_target_pairs={{0,8},{8,0},{16,24},{24,16},{1,9},{9,1},{17,25},{25,17},{2,10},{10... | collective-permute-start | bytes 3145736 | tf_op jit(solution)/shard_map/ppermute | solution.py:38
  603.1 27.8 %collective-permute-start.43 = (bf16[512,1024]{1,0:T(8,128)(2,1)}, bf16[512,1024]{1,0:T(8,128)(2,1)}, u32[]{:S(2)}, u32[]{:S(2)}) collective-permute-start(bf16[512,1024]{1,0:T(8,128)(2,1)} %get-tuple-element.163), channel_id=1, source_target_pairs={{0,16},{8,24},{16,0},{24,8},{1,17},{9,25},{17,1},{25,9},{2,18},{10... | collective-permute-start | bytes 3145736 | tf_op jit(solution)/shard_map/ppermute | solution.py:38
  646.9 103.5 %reduce-scatter.9.cloned.1.call-start = ((), (), s32[]{:S(2)}) async-start(), calls=%async_computation.9 | async-start | bytes 5308416 | tf_op jit(solution)/shard_map/reduce_scatter | solution.py:819
  651.6 28.8 %collective-permute-start.51 = (bf16[256,2048]{1,0:T(8,128)(2,1)}, bf16[256,2048]{1,0:T(8,128)(2,1)}, u32[]{:S(2)}, u32[]{:S(2)}) collective-permute-start(bf16[256,2048]{1,0:T(8,128)(2,1)} %pad_maximum_fusion.27), channel_id=1, source_target_pairs={{0,16},{8,24},{16,0},{24,8},{1,17},{9,25},{17,1},{25,9},{2,18},{10... | collective-permute-start | bytes 3145736 | tf_op jit(solution)/shard_map/ppermute | solution.py:38
  652.5 27.9 %collective-permute-start.52 = (bf16[256,2048]{1,0:T(8,128)(2,1)}, bf16[256,2048]{1,0:T(8,128)(2,1)}, u32[]{:S(2)}, u32[]{:S(2)}) collective-permute-start(bf16[256,2048]{1,0:T(8,128)(2,1)} %pad_maximum_fusion.28), channel_id=1, source_target_pairs={{0,8},{8,0},{16,24},{24,16},{1,9},{9,1},{17,25},{25,17},{2,10},{10... | collective-permute-start | bytes 3145736 | tf_op jit(solution)/shard_map/ppermute | solution.py:38
  683.2 30.6 %collective-permute-start.49 = (bf16[256,2048]{1,0:T(8,128)(2,1)}, bf16[256,2048]{1,0:T(8,128)(2,1)}, u32[]{:S(2)}, u32[]{:S(2)}) collective-permute-start(bf16[256,2048]{1,0:T(8,128)(2,1)} %pad_maximum_fusion.26), channel_id=1, source_target_pairs={{0,8},{8,0},{16,24},{24,16},{1,9},{9,1},{17,25},{25,17},{2,10},{10... | collective-permute-start | bytes 3145736 | tf_op jit(solution)/shard_map/ppermute | solution.py:38
  685.2 28.6 %collective-permute-start.47 = (bf16[256,2048]{1,0:T(8,128)(2,1)}, bf16[256,2048]{1,0:T(8,128)(2,1)}, u32[]{:S(2)}, u32[]{:S(2)}) collective-permute-start(bf16[256,2048]{1,0:T(8,128)(2,1)} %pad_maximum_fusion.25), channel_id=1, source_target_pairs={{0,16},{8,24},{16,0},{24,8},{1,17},{9,25},{17,1},{25,9},{2,18},{10... | collective-permute-start | bytes 3145736 | tf_op jit(solution)/shard_map/ppermute | solution.py:38
  689.5 24.2 %collective-permute-start.56 = (bf16[128,2048]{1,0:T(8,128)(2,1)}, bf16[128,2048]{1,0:T(8,128)(2,1)}, u32[]{:S(2)}, u32[]{:S(2)}) collective-permute-start(bf16[128,2048]{1,0:T(8,128)(2,1)} %get-tuple-element.277), channel_id=1, source_target_pairs={{0,8},{8,0},{16,24},{24,16},{1,9},{9,1},{17,25},{25,17},{2,10},{10... | collective-permute-start | bytes 1572872 | tf_op jit(solution)/shard_map/ppermute | solution.py:38
  690.4 23.3 %collective-permute-start.57 = (bf16[128,2048]{1,0:T(8,128)(2,1)}, bf16[128,2048]{1,0:T(8,128)(2,1)}, u32[]{:S(2)}, u32[]{:S(2)}) collective-permute-start(bf16[128,2048]{1,0:T(8,128)(2,1)} %get-tuple-element.268), channel_id=1, source_target_pairs={{0,16},{8,24},{16,0},{24,8},{1,17},{9,25},{17,1},{25,9},{2,18},{10... | collective-permute-start | bytes 1572872 | tf_op jit(solution)/shard_map/ppermute | solution.py:38
  (124 other events, 1481.0 us)
Sparse Core Ops, SparseCore 0:
  27.5 69.4 all-gather.11
  98.6 27.6 all-gather.5
  127.9 81.5 all-gather.9
  211.0 84.9 all-gather.7
  451.3 90.3 reduce-scatter.6
  543.9 87.9 reduce-scatter.4
  647.0 47.2 reduce-scatter.10
  696.6 53.1 reduce-scatter.8

commit v6 on v5

--- a/solution.py
+++ b/solution.py
@@ -752,13 +752,12 @@
     points = cuts(tokens, steps)
     d_low = after(d_middle.astype(bf16), down_came)
     state = gather_start([d_low[points[j] : points[j + 1]] for j in range(steps)])
-    came = d_low
     for step in range(max(steps, EXP_DEV - 1)):
         if step < steps:
-            came = gather_step(state, "context", n_ctx)
+            gather_step(state, "context", n_ctx)
         if step + 1 < EXP_DEV:
-            down_raw.append(weight_grad(after(hidden_g[step + 1], came), pull))
-    g_router = dot(mixed, after(d_logits, d_low, down_raw), ((0,), (0,)))
+            down_raw.append(weight_grad(after(hidden_g[step + 1], d_middle), pull))
+    g_router = dot(mixed, after(d_logits, d_low), ((0,), (0,)))
     d_branch = after(in_sequence(joined(state)), down_raw, g_router)
     downs += [scatter_state(row_parts(owner_rows(grad), steps)) for grad in down_raw[1:]]
     last_came = [

time: 778 us -> 773 us (level)
  waiting for transfers between devices: 197 us -> 189 us
    ppermute x60, waiting for transfers between devices: 197 us -> 188 us  [swap(): return lax.ppermute(value, axis, [(i, i ^ bit) for i in range(count)])]
    unnamed x183 -> x179, local copies, waits for them, and re-layouts: 18 us -> 19.9 us
  transfers between devices with their start and end apart: 68 -> 68, of which waited for: 30 -> 29; matrix products, arithmetic and copies ran while one was open for 28% -> 28% of each run, Pallas kernels for 30% -> 30%
where the time goes in v6:
time: 773 us; the launch traced here: 767 us
  Pallas kernels  234 us (30%)
  waiting for transfers between devices  189 us (24%)
  other arithmetic  96.8 us (13%)
  matrix products  84 us (11%)
  starting transfers between devices  70.1 us (9%)
  local copies, waits for them, and re-layouts  62.2 us (8%)
  between operations  31.5 us (4%)
    ppermute x60, waiting for transfers between devices, swap(): return lax.ppermute(value, axis, [(i, i ^ bit) for i in range(count)])  188 us
    dot_general x10, matrix products, dot(): lax.dot_general(left, right, (dims, ((), ())), preferred_element_type=f32)  84 us
    ppermute x60, starting transfers between devices, swap(): return lax.ppermute(value, axis, [(i, i ^ bit) for i in range(count)])  69.2 us
    pallas_call x2, Pallas kernels, run_experts(): pl.pallas_call(lambda *refs: experts_kernel(e, len(gate_k), *refs), grid=...  56 us
    pallas_call x1, Pallas kernels, rows_back(): pl.pallas_call(lambda *refs: rows_back_kernel(count, n_ctx, *refs), grid=...  46.8 us
    pallas_call x2, Pallas kernels, pull_down(): pl.pallas_call(lambda *refs: pull_down_kernel(places, *refs), grid=(rows...  28.4 us
    pallas_call x1, Pallas kernels, combine(): pl.pallas_call(lambda *refs: combine_kernel(count, *refs), grid=(rows //...  23.6 us
    unnamed x179, local copies, waits for them, and re-layouts  19.9 us
  transfers between devices with their start and end apart: 68, of which 29 were waited for; matrix products, arithmetic and copies ran while one was open for 28% of the time, Pallas kernels for 30%

profile of v6, /device:TPU:0, one launch (start us, length us, event | category | flops | bytes accessed | tf_op | source)
XLA Modules:
  0.0 766.8 jit_solution(7774999921387296623)
XLA Ops:
  16.5 5.5 collective-permute-done.6
  35.5 11.5 %collective-permute-done.1 = bf16[128,2048]{1,0:T(8,128)(2,1)S(1)} collective-permute-done((bf16[128,2048]{1,0:T(8,128)(2,1)S(1)}, bf16[128,2048]{1,0:T(8,128)(2,1)S(1)}, u32[]{:S(2)}, u32[]{:S(2)}) %collective-permute-start.1) | collective-permute-done | bytes 524320 | tf_op jit(solution)/shard_map/ppermute | solution.py:38
  62.6 8.7 %collective-permute-done.2 = bf16[256,2048]{1,0:T(8,128)(2,1)} collective-permute-done((bf16[256,2048]{1,0:T(8,128)(2,1)S(1)}, bf16[256,2048]{1,0:T(8,128)(2,1)}, u32[]{:S(2)}, u32[]{:S(2)}) %collective-permute-start.2) | collective-permute-done | bytes 1048608 | tf_op jit(solution)/shard_map/ppermute | solution.py:38
  84.8 9.6 %collective-permute-done.7.refs_3_ = bf16[128,2048]{1,0:T(8,128)(2,1)S(1)} collective-permute-done((bf16[128,2048]{1,0:T(8,128)(2,1)S(1)}, bf16[128,2048]{1,0:T(8,128)(2,1)S(1)}, u32[]{:S(2)}, u32[]{:S(2)}) %collective-permute-start.7) | collective-permute-done | bytes 524320 | tf_op jit(solution)/shard_map/ppermute | solution.py:38
  116.3 16.0 %project.1 = (f32[1024,1536]{1,0:T(8,128)}, bf16[1024,2048]{1,0:T(8,128)(2,1)}, f32[2,1024]{1,0:T(2,128)}) custom-call(bf16[1024,2048]{1,0:T(8,128)(2,1)} %bitcast.244, f32[1024,1]{1,0:T(8,128)} %copy.144.refs_1_.refs_3_, f32[1,2048]{1,0:T(1,128)} %get-tuple-element.367.refs_2_, bf16[8,4,64,1664]{3,2,1,0:T(8,128)(2,1)} %bitcast.252), custom_call_target="tpu_custom_call" | custom-call | flops 6442450944 | bytes 21495808 | tf_op jit(solution)/shard_map/project/pallas_call | solution.py:175
  144.7 14.7 %attend.1 = (bf16[1024,512]{1,0:T(8,128)(2,1)}, bf16[1024,512]{1,0:T(8,128)(2,1)}, bf16[1024,512]{1,0:T(8,128)(2,1)}, f32[4,1024,1]{2,1,0:T(8,128)}) custom-call(f32[1024,1536]{1,0:T(8,128)} %get-tuple-element.103.refs_0_.refs_1_.refs_2_, f32[1024,1536]{1,0:T(8,128)} %get-tuple-element.103.refs_0_.refs_1_.refs_2_, ...), custom_call_target="tpu_custom_call" | custom-call | flops 2147483648 | bytes 6291456 | tf_op jit(solution)/shard_map/attend/pallas_call | solution.py:301
  159.4 4.3 convolution_convert_fusion.2
  166.7 19.1 %collective-permute-done.19 = bf16[256,2048]{1,0:T(8,128)(2,1)S(1)} collective-permute-done((bf16[256,2048]{1,0:T(8,128)(2,1)S(1)}, bf16[256,2048]{1,0:T(8,128)(2,1)S(1)}, u32[]{:S(2)}, u32[]{:S(2)}) %collective-permute-start.19) | collective-permute-done | bytes 1048608 | tf_op jit(solution)/shard_map/ppermute | solution.py:38
  190.2 7.8 %collective-permute-done.20 = bf16[128,2048]{1,0:T(8,128)(2,1)S(1)} collective-permute-done((bf16[128,2048]{1,0:T(8,128)(2,1)S(1)}, bf16[128,2048]{1,0:T(8,128)(2,1)S(1)}, u32[]{:S(2)}, u32[]{:S(2)}) %collective-permute-start.20) | collective-permute-done | bytes 524320 | tf_op jit(solution)/shard_map/ppermute | solution.py:38
  209.2 16.3 %collective-permute-done.22.refs_4_.refs_3_ = bf16[512,1024]{1,0:T(8,128)(2,1)S(1)} collective-permute-done((bf16[512,1024]{1,0:T(8,128)(2,1)S(1)}, bf16[512,1024]{1,0:T(8,128)(2,1)S(1)}, u32[]{:S(2)}, u32[]{:S(2)}) %collective-permute-start.22) | collective-permute-done | bytes 1048608 | tf_op jit(solution)/shard_map/ppermute | solution.py:38
  235.0 36.7 %collective-permute-done.23.refs_5_.refs_6_.refs_4_ = bf16[1024,1024]{1,0:T(8,128)(2,1)} collective-permute-done((bf16[1024,1024]{1,0:T(8,128)(2,1)}, bf16[1024,1024]{1,0:T(8,128)(2,1)}, u32[]{:S(2)}, u32[]{:S(2)}) %collective-permute-start.23) | collective-permute-done | bytes 2097184 | tf_op jit(solution)/shard_map/ppermute | solution.py:38
  274.1 14.3 %pull_down.2 = (f32[2048,1024]{1,0:T(8,128)}, bf16[1024,2048]{1,0:T(8,128)(2,1)}) custom-call(s32[1]{0:T(128)} %bitcast.53.refs_0_, bf16[2048,2048]{1,0:T(8,128)(2,1)} %all-gather.10.cloned.1.call-done.refs_1_, bf16[128,2048]{1,0:T(8,128)(2,1)} %copy-done.41, bf16[128,2048]{1,0:T(8,128)(2,1)} %copy-done.53, ...), custom_call_target="tpu_custom_call" | custom-call | flops 8589934592 | bytes 25165824 | tf_op jit(solution)/shard_map/pull_down/pallas_call | solution.py:415
  288.4 14.1 %pull_down.3 = (f32[2048,1024]{1,0:T(8,128)}, bf16[1024,2048]{1,0:T(8,128)(2,1)}) custom-call(s32[1]{0:T(128)} %bitcast.53.refs_0_, bf16[2048,2048]{1,0:T(8,128)(2,1)} %all-gather.10.cloned.1.call-done.refs_1_, bf16[128,2048]{1,0:T(8,128)(2,1)} %get-tuple-element.105.refs_2_, bf16[128,2048]{1,0:T(8,128)(2,1)} %collective-permute-done.9.refs_3_, ...), custom_call_target="tpu_custom_call" | custom-call | flops 8589934592 | bytes 25165824 | tf_op jit(solution)/shard_map/pull_down/pallas_call | solution.py:415
  311.1 28.0 %expert.2 = (bf16[2048,1024]{1,0:T(8,128)(2,1)}, bf16[2048,2048]{1,0:T(8,128)(2,1)}, f32[2048,1]{1,0:T(8,128)}) custom-call(bf16[2048,2176]{1,0:T(8,128)(2,1)} %all-gather.8.cloned.1.call-done.refs_0_, f32[2048,1024]{1,0:T(8,128)} %get-tuple-element.119.refs_1_, f32[2048,2]{1,0:T(8,128)} %dynamic-slice_multiply_fusion.refs_2_, bf16[512,1024]{1,0:T(8,128)(2,1)} %copy-done.7, ...), custom_call_target="tpu_custom_call" | custom-call | flops 17179869184 | bytes 37748736 | tf_op jit(solution)/shard_map/expert/pallas_call | solution.py:456
  339.2 13.3 %fusion.14 = bf16[2048,1024]{1,0:T(8,128)(2,1)S(1)} fusion(bf16[2048,2048]{1,0:T(8,128)(2,1)} %get-tuple-element.130.refs_0_, bf16[2048,2176]{1,0:T(8,128)(2,1)} %all-gather.8.cloned.1.call-done.refs_0_), kind=kOutput, calls=%fused_computation.18 | convolution fusion | flops 8592031744 | bytes 16777216 | tf_op jit(solution)/shard_map/dot_general | solution.py:24
  356.0 9.1 %fusion.19 = bf16[2048,1024]{1,0:T(8,128)(2,1)S(1)} fusion(bf16[2048,2048]{1,0:T(8,128)(2,1)S(1)} %copy-done.10, bf16[2048,2176]{1,0:T(8,128)(2,1)S(1)} %bitcast.290), kind=kOutput, calls=%fused_computation.19 | convolution fusion | flops 8592031744 | bytes 16777216 | tf_op jit(solution)/shard_map/dot_general | solution.py:24
  370.6 27.9 %expert.3 = (bf16[2048,1024]{1,0:T(8,128)(2,1)}, bf16[2048,2048]{1,0:T(8,128)(2,1)}, f32[2048,1]{1,0:T(8,128)}) custom-call(bf16[2048,2176]{1,0:T(8,128)(2,1)} %all-gather.8.cloned.1.call-done.refs_0_, f32[2048,1024]{1,0:T(8,128)} %get-tuple-element.121.refs_1_, f32[2048,2]{1,0:T(8,128)} %dynamic-slice_multiply_fusion.refs_2_, bf16[512,1024]{1,0:T(8,128)(2,1)} %copy-done.6, ...), custom_call_target="tpu_custom_call" | custom-call | flops 17179869184 | bytes 37748736 | tf_op jit(solution)/shard_map/expert/pallas_call | solution.py:456
  404.1 46.8 %rows_back.1 = bf16[2048,2048]{1,0:T(8,128)(2,1)} custom-call(bf16[2048,2048]{1,0:T(8,128)(2,1)} %get-tuple-element.130.refs_0_, bf16[2048,2048]{1,0:T(8,128)(2,1)} %get-tuple-element.137.refs_1_, bf16[512,1024]{1,0:T(8,128)(2,1)} %copy-done.7, bf16[512,1024]{1,0:T(8,128)(2,1)} %copy-done.25, ...), custom_call_target="tpu_custom_call" | custom-call | bytes 2097152 | tf_op jit(solution)/shard_map/rows_back/pallas_call | solution.py:518
  450.9 4.6 convert_add_fusion.4
  461.3 13.4 %fusion.24 = bf16[2048,1024]{1,0:T(8,128)(2,1)S(1)} fusion(bf16[2048,2048]{1,0:T(8,128)(2,1)} %get-tuple-element.137.refs_1_, bf16[2048,2176]{1,0:T(8,128)(2,1)} %all-gather.8.cloned.1.call-done.refs_0_), kind=kOutput, calls=%fused_computation.20 | convolution fusion | flops 8592031744 | bytes 16777216 | tf_op jit(solution)/shard_map/dot_general | solution.py:24
  474.7 12.9 %fusion.29 = bf16[2048,1024]{1,0:T(8,128)(2,1)S(1)} fusion(bf16[2048,2048]{1,0:T(8,128)(2,1)S(1)} %bitcast.247, bf16[2048,2176]{1,0:T(8,128)(2,1)} %all-gather.8.cloned.1.call-done.refs_0_), kind=kOutput, calls=%fused_computation.21 | convolution fusion | flops 8592031744 | bytes 16777216 | tf_op jit(solution)/shard_map/dot_general | solution.py:24
  494.2 13.5 %convolution_convert_fusion.1 = bf16[1024,2048]{1,0:T(8,128)(2,1)} fusion(bf16[2048,1024]{1,0:T(8,128)(2,1)S(1)} %copy-done.74, bf16[2048,2048]{1,0:T(8,128)(2,1)} %all-gather.10.cloned.1.call-done.refs_1_), kind=kOutput, calls=%fused_computation.23 | convolution fusion | flops 8592031744 | bytes 16777216 | tf_op jit(solution)/shard_map/dot_general | solution.py:24
  507.7 23.6 %combine.1 = bf16[2048,2048]{1,0:T(8,128)(2,1)} custom-call(bf16[2048,1024]{1,0:T(8,128)(2,1)} %get-tuple-element.141.refs_0_, bf16[2048,1024]{1,0:T(8,128)(2,1)} %get-tuple-element.154.refs_1_, bf16[1024,2048]{1,0:T(8,128)(2,1)} %get-tuple-element.143.refs_2_, bf16[1024,2048]{1,0:T(8,128)(2,1)} %get-tuple-element.144.refs_3_), custom_call_target="tpu_custom_call" | custom-call | flops 17179869184 | bytes 25165824 | tf_op jit(solution)/shard_map/combine/pallas_call | solution.py:484
  536.1 4.1 convert_add_fusion.2
  554.1 11.2 %convolution_convert_fusion = bf16[1024,2048]{1,0:T(8,128)(2,1)} fusion(bf16[2048,1024]{1,0:T(8,128)(2,1)S(1)} %copy-done.73, bf16[2048,2048]{1,0:T(8,128)(2,1)S(1)} %bitcast.307), kind=kOutput, calls=%fused_computation.22 | convolution fusion | flops 8592031744 | bytes 16777216 | tf_op jit(solution)/shard_map/dot_general | solution.py:24
  570.8 20.2 %collective-permute-done.40 = bf16[256,2048]{1,0:T(8,128)(2,1)S(1)} collective-permute-done((bf16[256,2048]{1,0:T(8,128)(2,1)S(1)}, bf16[256,2048]{1,0:T(8,128)(2,1)S(1)}, u32[]{:S(2)}, u32[]{:S(2)}) %collective-permute-start.40) | collective-permute-done | bytes 1048608 | tf_op jit(solution)/shard_map/ppermute | solution.py:38
  597.0 19.5 %attend_back.1 = (f32[1024,512]{1,0:T(8,128)}, f32[1024,512]{1,0:T(8,128)}, bf16[1024,512]{1,0:T(8,128)(2,1)}, f32[4,1024,1]{2,1,0:T(8,128)}, f32[4,1024,1]{2,1,0:T(8,128)}, /*index=5*/f32[4,2,128]{2,1,0:T(2,128)}) custom-call(f32[1024,1536]{1,0:T(8,128)} %get-tuple-element.103.refs_0_.refs_1_.refs_2_, ...), custom_call_target="tpu_custom_call" | custom-call | bytes 1048576 | tf_op jit(solution)/shard_map/attend_back/pallas_call | solution.py:361
  627.2 9.2 %side_grads.1 = bf16[8,4,64,1024]{3,2,1,0:T(8,128)(2,1)} custom-call(bf16[1024,2048]{1,0:T(8,128)(2,1)} %get-tuple-element.167.refs_0_.refs_4_, bf16[1024,512]{1,0:T(8,128)(2,1)} %get-tuple-element.168.refs_1_, bf16[1024,512]{1,0:T(8,128)(2,1)} %get-tuple-element.110.refs_2_, bf16[1024,2048]{1,0:T(8,128)(2,1)} %bitcast.263), custom_call_target="tpu_custom_call" | custom-call | flops 4294967296 | bytes 12582912 | tf_op jit(solution)/shard_map/side_grads/pallas_call | solution.py:214
  651.0 19.4 %project_back.1 = (bf16[1024,2048]{1,0:T(8,128)(2,1)}, bf16[8,4,64,1152]{3,2,1,0:T(8,128)(2,1)}) custom-call(bf16[1024,1536]{1,0:T(8,128)(2,1)} %pad_maximum_fusion.3.refs_0_, bf16[8,4,64,1664]{3,2,1,0:T(8,128)(2,1)} %bitcast.253, bf16[1024,2048]{1,0:T(8,128)(2,1)} %bitcast.245, f32[1024,1]{1,0:T(8,128)} %copy.144.refs_1_.refs_3_, ...), custom_call_target="tpu_custom_call" | custom-call | bytes 4194304 | tf_op jit(solution)/shard_map/project_back/pallas_call | solution.py:244
  684.5 5.1 collective-permute-done.47
  692.0 18.4 %collective-permute-done.49 = bf16[256,2048]{1,0:T(8,128)(2,1)} collective-permute-done((bf16[256,2048]{1,0:T(8,128)(2,1)}, bf16[256,2048]{1,0:T(8,128)(2,1)}, u32[]{:S(2)}, u32[]{:S(2)}) %collective-permute-start.49) | collective-permute-done | bytes 1048608 | tf_op jit(solution)/shard_map/ppermute | solution.py:38
  735.1 5.6 collective-permute-done.50
  (482 shorter events, 250.7 us)
Async XLA Ops:
  7.2 107.0 %all-gather.12.cloned.1.call-start = ((), (), s32[]{:S(2)}) async-start(), calls=%async_computation.11 | async-start | bytes 7667712 | tf_op jit(solution)/shard_map/all_gather | solution.py:603
  27.2 132.2 %all-gather.6.cloned.1.call-start = ((), (), s32[]{:S(2)}) async-start(), calls=%async_computation.4 | async-start | bytes 2359296 | tf_op jit(solution)/shard_map/all_gather | solution.py:621
  47.0 24.3 %collective-permute-start.2 = (bf16[256,2048]{1,0:T(8,128)(2,1)S(1)}, bf16[256,2048]{1,0:T(8,128)(2,1)}, u32[]{:S(2)}, u32[]{:S(2)}) collective-permute-start(bf16[256,2048]{1,0:T(8,128)(2,1)S(1)} %pad_maximum_fusion.13), channel_id=1, source_target_pairs={{0,8},{8,0},{16,24},{24,16},{1,9},{9,1},{17,25},{25,17},{2,10},{10... | collective-permute-start | bytes 3145736 | tf_op jit(solution)/shard_map/ppermute | solution.py:38
  49.8 24.3 %collective-permute-start.3 = (bf16[256,2048]{1,0:T(8,128)(2,1)}, bf16[256,2048]{1,0:T(8,128)(2,1)}, u32[]{:S(2)}, u32[]{:S(2)}) collective-permute-start(bf16[256,2048]{1,0:T(8,128)(2,1)} %pad_maximum_fusion.14), channel_id=1, source_target_pairs={{0,16},{8,24},{16,0},{24,8},{1,17},{9,25},{17,1},{25,9},{2,18},{10... | collective-permute-start | bytes 3145736 | tf_op jit(solution)/shard_map/ppermute | solution.py:38
  80.6 154.3 %all-gather.10.cloned.1.call-start = ((), (), s32[]{:S(2)}) async-start(), calls=%async_computation.6 | async-start | bytes 9437184 | tf_op jit(solution)/shard_map/all_gather | solution.py:631
  96.3 211.5 %all-gather.8.cloned.1.call-start = ((), (), s32[]{:S(2)}) async-start(), calls=%async_computation.5 | async-start | bytes 10027008 | tf_op jit(solution)/shard_map/all_gather | solution.py:667
  139.9 23.8 %collective-permute-start.16 = (bf16[256,2048]{1,0:T(8,128)(2,1)}, bf16[256,2048]{1,0:T(8,128)(2,1)}, u32[]{:S(2)}, u32[]{:S(2)}) collective-permute-start(bf16[256,2048]{1,0:T(8,128)(2,1)} %get-tuple-element.112), channel_id=1, source_target_pairs={{0,16},{8,24},{16,0},{24,8},{1,17},{9,25},{17,1},{25,9},{2,18},{10... | collective-permute-start | bytes 3145736 | tf_op jit(solution)/shard_map/ppermute | solution.py:38
  204.1 338.6 %reduce-scatter.7.cloned.1.call-start = ((), (), s32[]{:S(2)}) async-start(), calls=%async_computation.8 | async-start | bytes 9437184 | tf_op jit(solution)/shard_map/reduce_scatter | solution.py:731
  227.2 44.5 %collective-permute-start.23 = (bf16[1024,1024]{1,0:T(8,128)(2,1)}, bf16[1024,1024]{1,0:T(8,128)(2,1)}, u32[]{:S(2)}, u32[]{:S(2)}) collective-permute-start(bf16[1024,1024]{1,0:T(8,128)(2,1)} %pad_maximum_fusion.5), channel_id=1, source_target_pairs={{0,16},{8,24},{16,0},{24,8},{1,17},{9,25},{17,1},{25,9},{2,18},{10... | collective-permute-start | bytes 6291464 | tf_op jit(solution)/shard_map/ppermute | solution.py:38
  230.4 41.5 %collective-permute-start.25 = (bf16[1024,1024]{1,0:T(8,128)(2,1)}, bf16[1024,1024]{1,0:T(8,128)(2,1)}, u32[]{:S(2)}, u32[]{:S(2)}) collective-permute-start(bf16[1024,1024]{1,0:T(8,128)(2,1)} %pad_maximum_fusion.6), channel_id=1, source_target_pairs={{0,8},{8,0},{16,24},{24,16},{1,9},{9,1},{17,25},{25,17},{2,10},{10... | collective-permute-start | bytes 6291464 | tf_op jit(solution)/shard_map/ppermute | solution.py:38
  272.0 30.6 %collective-permute-start.26 = (bf16[512,1024]{1,0:T(8,128)(2,1)S(1)}, bf16[512,1024]{1,0:T(8,128)(2,1)S(1)}, u32[]{:S(2)}, u32[]{:S(2)}) collective-permute-start(bf16[512,1024]{1,0:T(8,128)(2,1)S(1)} %get-tuple-element.128.refs_3_.refs_10_), channel_id=1, source_target_pairs={{0,8},{8,0},{16,24},{24,16},{1,9},{9,1},{17,25},{25,17},{2,10},{10... | collective-permute-start | bytes 3145736 | tf_op jit(solution)/shard_map/ppermute | solution.py:38
  273.9 32.2 %collective-permute-start.27 = (bf16[512,1024]{1,0:T(8,128)(2,1)S(1)}, bf16[512,1024]{1,0:T(8,128)(2,1)S(1)}, u32[]{:S(2)}, u32[]{:S(2)}) collective-permute-start(bf16[512,1024]{1,0:T(8,128)(2,1)S(1)} %get-tuple-element.129.refs_7_.refs_14_), channel_id=1, source_target_pairs={{0,16},{8,24},{16,0},{24,8},{1,17},{9,25},{17,1},{25,9},{2,18},{10... | collective-permute-start | bytes 3145736 | tf_op jit(solution)/shard_map/ppermute | solution.py:38
  304.3 66.2 %collective-permute-start.28 = (bf16[1024,1024]{1,0:T(8,128)(2,1)}, bf16[1024,1024]{1,0:T(8,128)(2,1)}, u32[]{:S(2)}, u32[]{:S(2)}) collective-permute-start(bf16[1024,1024]{1,0:T(8,128)(2,1)} %pad_maximum_fusion.7), channel_id=1, source_target_pairs={{0,16},{8,24},{16,0},{24,8},{1,17},{9,25},{17,1},{25,9},{2,18},{10... | collective-permute-start | bytes 6291464 | tf_op jit(solution)/shard_map/ppermute | solution.py:38
  307.7 62.8 %collective-permute-start.29 = (bf16[1024,1024]{1,0:T(8,128)(2,1)}, bf16[1024,1024]{1,0:T(8,128)(2,1)}, u32[]{:S(2)}, u32[]{:S(2)}) collective-permute-start(bf16[1024,1024]{1,0:T(8,128)(2,1)} %pad_maximum_fusion.8), channel_id=1, source_target_pairs={{0,8},{8,0},{16,24},{24,16},{1,9},{9,1},{17,25},{25,17},{2,10},{10... | collective-permute-start | bytes 6291464 | tf_op jit(solution)/shard_map/ppermute | solution.py:38
  365.2 85.7 %collective-permute-start.30 = (bf16[1024,1024]{1,0:T(8,128)(2,1)}, bf16[1024,1024]{1,0:T(8,128)(2,1)}, u32[]{:S(2)}, u32[]{:S(2)}) collective-permute-start(bf16[1024,1024]{1,0:T(8,128)(2,1)} %concatenate.180), channel_id=1, source_target_pairs={{0,16},{8,24},{16,0},{24,8},{1,17},{9,25},{17,1},{25,9},{2,18},{10... | collective-permute-start | bytes 6291464 | tf_op jit(solution)/shard_map/ppermute | solution.py:38
  368.8 82.1 %collective-permute-start.31 = (bf16[1024,1024]{1,0:T(8,128)(2,1)}, bf16[1024,1024]{1,0:T(8,128)(2,1)}, u32[]{:S(2)}, u32[]{:S(2)}) collective-permute-start(bf16[1024,1024]{1,0:T(8,128)(2,1)} %pad_maximum_fusion.9), channel_id=1, source_target_pairs={{0,8},{8,0},{16,24},{24,16},{1,9},{9,1},{17,25},{25,17},{2,10},{10... | collective-permute-start | bytes 6291464 | tf_op jit(solution)/shard_map/ppermute | solution.py:38
  450.9 230.8 %reduce-scatter.5.cloned.1.call-start = ((), (), s32[]{:S(2)}) async-start(), calls=%async_computation.7 | async-start | bytes 9437184 | tf_op jit(solution)/shard_map/reduce_scatter | solution.py:740
  459.5 32.5 %collective-permute-start.32 = (bf16[512,1024]{1,0:T(8,128)(2,1)S(1)}, bf16[512,1024]{1,0:T(8,128)(2,1)S(1)}, u32[]{:S(2)}, u32[]{:S(2)}) collective-permute-start(bf16[512,1024]{1,0:T(8,128)(2,1)S(1)} %get-tuple-element.139), channel_id=1, source_target_pairs={{0,8},{8,0},{16,24},{24,16},{1,9},{9,1},{17,25},{25,17},{2,10},{10... | collective-permute-start | bytes 3145736 | tf_op jit(solution)/shard_map/ppermute | solution.py:38
  459.6 32.4 %collective-permute-start.33 = (bf16[512,1024]{1,0:T(8,128)(2,1)S(1)}, bf16[512,1024]{1,0:T(8,128)(2,1)S(1)}, u32[]{:S(2)}, u32[]{:S(2)}) collective-permute-start(bf16[512,1024]{1,0:T(8,128)(2,1)S(1)} %get-tuple-element.140), channel_id=1, source_target_pairs={{0,16},{8,24},{16,0},{24,8},{1,17},{9,25},{17,1},{25,9},{2,18},{10... | collective-permute-start | bytes 3145736 | tf_op jit(solution)/shard_map/ppermute | solution.py:38
  492.0 39.3 %collective-permute-start.34 = (bf16[1024,1024]{1,0:T(8,128)(2,1)}, bf16[1024,1024]{1,0:T(8,128)(2,1)}, u32[]{:S(2)}, u32[]{:S(2)}) collective-permute-start(bf16[1024,1024]{1,0:T(8,128)(2,1)} %concatenate.181), channel_id=1, source_target_pairs={{0,16},{8,24},{16,0},{24,8},{1,17},{9,25},{17,1},{25,9},{2,18},{10... | collective-permute-start | bytes 6291464 | tf_op jit(solution)/shard_map/ppermute | solution.py:38
  492.3 39.0 %collective-permute-start.35 = (bf16[1024,1024]{1,0:T(8,128)(2,1)}, bf16[1024,1024]{1,0:T(8,128)(2,1)S(1)}, u32[]{:S(2)}, u32[]{:S(2)}) collective-permute-start(bf16[1024,1024]{1,0:T(8,128)(2,1)} %pad_maximum_fusion.10), channel_id=1, source_target_pairs={{0,8},{8,0},{16,24},{24,16},{1,9},{9,1},{17,25},{25,17},{2,10},{10... | collective-permute-start | bytes 6291464 | tf_op jit(solution)/shard_map/ppermute | solution.py:38
  531.3 211.2 %reduce-scatter.11.cloned.1.call-start = ((), (), s32[]{:S(2)}) async-start(), calls=%async_computation.10 | async-start | bytes 4718592 | tf_op jit(solution)/shard_map/reduce_scatter | solution.py:788
  568.3 22.7 %collective-permute-start.40 = (bf16[256,2048]{1,0:T(8,128)(2,1)S(1)}, bf16[256,2048]{1,0:T(8,128)(2,1)S(1)}, u32[]{:S(2)}, u32[]{:S(2)}) collective-permute-start(bf16[256,2048]{1,0:T(8,128)(2,1)S(1)} %pad_maximum_fusion.23), channel_id=1, source_target_pairs={{0,8},{8,0},{16,24},{24,16},{1,9},{9,1},{17,25},{25,17},{2,10},{10... | collective-permute-start | bytes 3145736 | tf_op jit(solution)/shard_map/ppermute | solution.py:38
  591.3 28.9 %collective-permute-start.42 = (bf16[512,1024]{1,0:T(8,128)(2,1)}, bf16[512,1024]{1,0:T(8,128)(2,1)}, u32[]{:S(2)}, u32[]{:S(2)}) collective-permute-start(bf16[512,1024]{1,0:T(8,128)(2,1)} %get-tuple-element.162), channel_id=1, source_target_pairs={{0,8},{8,0},{16,24},{24,16},{1,9},{9,1},{17,25},{25,17},{2,10},{10... | collective-permute-start | bytes 3145736 | tf_op jit(solution)/shard_map/ppermute | solution.py:38
  593.3 26.9 %collective-permute-start.43 = (bf16[512,1024]{1,0:T(8,128)(2,1)}, bf16[512,1024]{1,0:T(8,128)(2,1)S(1)}, u32[]{:S(2)}, u32[]{:S(2)}) collective-permute-start(bf16[512,1024]{1,0:T(8,128)(2,1)} %get-tuple-element.163), channel_id=1, source_target_pairs={{0,16},{8,24},{16,0},{24,8},{1,17},{9,25},{17,1},{25,9},{2,18},{10... | collective-permute-start | bytes 3145736 | tf_op jit(solution)/shard_map/ppermute | solution.py:38
  636.5 107.8 %reduce-scatter.9.cloned.1.call-start = ((), (), s32[]{:S(2)}) async-start(), calls=%async_computation.9 | async-start | bytes 5308416 | tf_op jit(solution)/shard_map/reduce_scatter | solution.py:818
  641.2 29.2 %collective-permute-start.51 = (bf16[256,2048]{1,0:T(8,128)(2,1)}, bf16[256,2048]{1,0:T(8,128)(2,1)}, u32[]{:S(2)}, u32[]{:S(2)}) collective-permute-start(bf16[256,2048]{1,0:T(8,128)(2,1)} %pad_maximum_fusion.27), channel_id=1, source_target_pairs={{0,16},{8,24},{16,0},{24,8},{1,17},{9,25},{17,1},{25,9},{2,18},{10... | collective-permute-start | bytes 3145736 | tf_op jit(solution)/shard_map/ppermute | solution.py:38
  641.5 28.9 %collective-permute-start.52 = (bf16[256,2048]{1,0:T(8,128)(2,1)}, bf16[256,2048]{1,0:T(8,128)(2,1)}, u32[]{:S(2)}, u32[]{:S(2)}) collective-permute-start(bf16[256,2048]{1,0:T(8,128)(2,1)} %pad_maximum_fusion.28), channel_id=1, source_target_pairs={{0,8},{8,0},{16,24},{24,16},{1,9},{9,1},{17,25},{25,17},{2,10},{10... | collective-permute-start | bytes 3145736 | tf_op jit(solution)/shard_map/ppermute | solution.py:38
  677.1 37.9 %collective-permute-start.56 = (bf16[128,2048]{1,0:T(8,128)(2,1)}, bf16[128,2048]{1,0:T(8,128)(2,1)}, u32[]{:S(2)}, u32[]{:S(2)}) collective-permute-start(bf16[128,2048]{1,0:T(8,128)(2,1)} %get-tuple-element.279), channel_id=1, source_target_pairs={{0,8},{8,0},{16,24},{24,16},{1,9},{9,1},{17,25},{25,17},{2,10},{10... | collective-permute-start | bytes 1572872 | tf_op jit(solution)/shard_map/ppermute | solution.py:38
  678.6 36.3 %collective-permute-start.57 = (bf16[128,2048]{1,0:T(8,128)(2,1)}, bf16[128,2048]{1,0:T(8,128)(2,1)}, u32[]{:S(2)}, u32[]{:S(2)}) collective-permute-start(bf16[128,2048]{1,0:T(8,128)(2,1)} %get-tuple-element.270), channel_id=1, source_target_pairs={{0,16},{8,24},{16,0},{24,8},{1,17},{9,25},{17,1},{25,9},{2,18},{10... | collective-permute-start | bytes 1572872 | tf_op jit(solution)/shard_map/ppermute | solution.py:38
  680.1 30.4 %collective-permute-start.49 = (bf16[256,2048]{1,0:T(8,128)(2,1)}, bf16[256,2048]{1,0:T(8,128)(2,1)}, u32[]{:S(2)}, u32[]{:S(2)}) collective-permute-start(bf16[256,2048]{1,0:T(8,128)(2,1)} %pad_maximum_fusion.26), channel_id=1, source_target_pairs={{0,8},{8,0},{16,24},{24,16},{1,9},{9,1},{17,25},{25,17},{2,10},{10... | collective-permute-start | bytes 3145736 | tf_op jit(solution)/shard_map/ppermute | solution.py:38
  690.8 38.9 %collective-permute-start.48 = (bf16[128,2048]{1,0:T(8,128)(2,1)S(1)}, bf16[128,2048]{1,0:T(8,128)(2,1)S(1)}, u32[]{:S(2)}, u32[]{:S(2)}) collective-permute-start(bf16[128,2048]{1,0:T(8,128)(2,1)S(1)} %fusion.41), channel_id=1, source_target_pairs={{0,8},{8,0},{16,24},{24,16},{1,9},{9,1},{17,25},{25,17},{2,10},{10... | collective-permute-start | bytes 1572872 | tf_op jit(solution)/shard_map/ppermute | solution.py:38
  (122 other events, 1463.6 us)
Sparse Core Ops, SparseCore 0:
  27.3 69.5 all-gather.11
  98.5 27.7 all-gather.5
  127.9 81.5 all-gather.9
  210.9 84.9 all-gather.7
  451.0 89.5 reduce-scatter.6
  542.8 87.9 reduce-scatter.4
  636.6 51.0 reduce-scatter.10
  690.0 53.0 reduce-scatter.8
